TPU v7x, 32 devices: a whole 2x2x4 slice. The times are simulated.
32 devices in a mesh: groups: 2 (over x), dp: 16 (over z, y, core).
Axes of the slice: x: 2, y: 2, z: 4, core: 2. Of those that a mesh axis runs over, the one named last changes fastest.
Arguments:
- tokens: bfloat16 [32768, 2048], P(('groups', 'dp')), parts along dimension 0, may hold values from -6 to 6
- legal_moves: int32 [2048, 20], P(('groups', 'dp')), parts along dimension 0, may hold values from 0 to 1, as said below
- action_label: int32 [2048], P(('groups', 'dp')), parts along dimension 0, may hold values from 0 to 19, as said below
- value_weight: bfloat16 [16384, 1024], P('dp'), may hold values from -0.125 to 0.125
- value_prior: bfloat16 [16384, 1024], P('dp'), may hold values from -0.125 to 0.125
- query_weight: bfloat16 [8, 8, 2048], replicated, may hold values from -0.125 to 0.125
- query_prior: bfloat16 [8, 8, 2048], replicated, may hold values from -0.125 to 0.125
- policy_head: float32 [8, 20, 1024], replicated, may hold values from -0.875 to 0.875
- head_prior: float32 [8, 20, 1024], replicated, may hold values from -0.875 to 0.875
Outputs:
- weight_grad: float32 [32768, 1024], P(('groups', 'dp')), parts along dimension 0
- row_loss: float32 [2048], P(('groups', 'dp')), parts along dimension 0
There are 2 independent parts, one for each index of `groups`. A program takes and returns all parts, laid end to end along the dimension named above; an argument that names none is the same for every part. Nothing has to cross between parts.
Inputs may be any that keep to these rules, and one draw needn't show every extreme that they name: `action_label`: every row's label is one of its legal moves. `legal_moves`: every row has at least one legal move.
All inputs are finite; a program needn't handle non-finite values.
Results may differ from a plain program's by a relative error of at most 0.0071.
Values may be sent and summed in bfloat16 or wider, within the bound.
No kernel may reach another device: no remote copies, remote signals or barrier semaphores. Data moves between devices by JAX's collectives and lax.ppermute only.
A program may use at most 128 MiB of HBM per device.

v0:
```python
import jax
import jax.numpy as jnp
from jax import lax
from jax.sharding import PartitionSpec as P

H = 8
DH = 128
A = 20
OBS = 16
LEVELS = 8


def partner_2(block, axis, bit):
    count = lax.axis_size(axis)
    route = []
    for low in range(count):
        high = low | 1 << bit
        if high != low and high < count:
            route += [(low, high), (high, low)]
    return lax.ppermute(block, axis, route)


def shifted(block, axis, distance):
    devices = range(lax.axis_size(axis))
    route = [(i - distance, i) for i in devices if i - distance in devices]
    return lax.ppermute(block, axis, route)


def policy_of(tokens, value_proj, query_proj, move_head, legal_mask):
    row_count = legal_mask.shape[0]
    scores = lax.dot_general(
        tokens, query_proj, (((1,), (1,)), ((), ())), preferred_element_type=jnp.float32
    ).reshape(row_count, OBS, H)
    capped = 5.0 * jnp.tanh(scores / 5.0)
    exp_scores = jnp.exp(capped)
    attention = (exp_scores / jnp.sum(exp_scores, axis=1, keepdims=True)).astype(jnp.bfloat16)
    values = jnp.dot(tokens, value_proj, preferred_element_type=jnp.float32).astype(jnp.bfloat16)
    values = values.reshape(row_count, OBS, H, DH)
    pooled = jnp.einsum(
        "rth,rthe->rhe", attention, values, preferred_element_type=jnp.float32
    ).reshape(row_count, H * DH)
    raw_logits = lax.dot_general(
        pooled, move_head, (((1,), (1,)), ((), ())), precision=lax.Precision.HIGHEST
    )
    logits = 30.0 * jnp.tanh(raw_logits / 30.0)
    legal_float = legal_mask.astype(jnp.float32)
    exp_logits = jnp.exp(logits) * legal_float
    partition = jnp.sum(exp_logits, axis=1, keepdims=True)
    return (logits, exp_logits / partition, logits - jnp.log(partition), attention)


def digit_order(bit_count):
    return list(range(bit_count))


def gather_level(own_rows, lower_rows, member, bit_count):
    blocks = (own_rows[None], lower_rows[None])
    for bit_place in digit_order(bit_count):
        received = partner_2((blocks[0], blocks[1]), "dp", bit_place)
        upper_side = member // (1 << bit_place) % 2 == 1
        merged = []
        for kept_part, peer_part in zip(blocks, received):
            lower_half = jnp.where(upper_side, peer_part, kept_part)
            upper_half = jnp.where(upper_side, kept_part, peer_part)
            joined = jnp.stack([lower_half, upper_half], axis=0)
            merged.append(joined.reshape((-1,) + kept_part.shape[1:]))
        blocks = tuple(merged)
    return tuple((piece.reshape(-1, piece.shape[-1]) for piece in blocks))


def scatter_level(partial_value, member, bit_count):
    width = partial_value.shape[-1]
    blocks = partial_value.reshape(1 << bit_count, -1, width)
    for bit_place in digit_order(bit_count):
        count_now = blocks.shape[0] // 2
        viewed = blocks.reshape(count_now, 2, blocks.shape[1], width)
        lower_half = viewed[:, 0]
        upper_half = viewed[:, 1]
        upper_side = member // (1 << bit_place) % 2 == 1
        kept_part = jnp.where(upper_side, upper_half, lower_half)
        peer_part = jnp.where(upper_side, lower_half, upper_half)
        received = partner_2(peer_part, "dp", bit_place)
        blocks = kept_part + received
    return blocks.reshape(-1, width)


def per_device(
    tokens,
    legal_moves,
    action_label,
    value_weight,
    value_prior,
    query_weight,
    query_prior,
    policy_head,
    head_prior,
):
    group_size = lax.axis_size("dp") // LEVELS
    bit_count = group_size.bit_length() - 1
    device_place = lax.axis_index("dp")
    level_index = device_place // group_size
    member = device_place % group_size
    lower_index = jnp.maximum(level_index - 1, 0)
    lower_rows = shifted(value_prior, "dp", group_size)
    own_full, lower_full = gather_level(value_weight, lower_rows, member, bit_count)
    move_head = lax.dynamic_index_in_dim(policy_head, level_index, 0, keepdims=False)
    query_own = lax.dynamic_index_in_dim(query_weight, level_index, 0, keepdims=False)
    query_lower = lax.dynamic_index_in_dim(query_prior, lower_index, 0, keepdims=False)
    head_lower = lax.dynamic_index_in_dim(head_prior, lower_index, 0, keepdims=False)
    logits, policy, log_policy, attention = policy_of(
        tokens, own_full, query_own, move_head, legal_moves
    )
    unused, lower_policy, unused_log, unused_attention = policy_of(
        tokens, lower_full, query_lower, head_lower, legal_moves
    )
    legal_float = legal_moves.astype(jnp.float32)
    uniform_policy = legal_float / jnp.sum(legal_float, axis=1, keepdims=True)
    partner = jnp.where(level_index == 0, uniform_policy, lower_policy)
    onehot = (action_label[:, None] == jnp.arange(A, dtype=jnp.int32)[None, :]).astype(jnp.float32)
    target = 0.5 * onehot + 0.5 * partner
    row_loss = -jnp.sum(target * log_policy, axis=1)
    row_count = legal_moves.shape[0]
    logit_grad = (policy - target) * (1.0 - (logits / 30.0) ** 2)
    pooled_grad = jnp.dot(logit_grad, move_head, precision=lax.Precision.HIGHEST).reshape(
        row_count, 1, H, DH
    )
    value_grad = (attention.astype(jnp.float32)[..., None] * pooled_grad).astype(jnp.bfloat16)
    value_grad = value_grad.reshape(row_count * OBS, H * DH)
    partial_value = lax.dot_general(
        tokens, value_grad, (((0,), (0,)), ((), ())), preferred_element_type=jnp.float32
    )
    weight_grad = scatter_level(partial_value, member, bit_count)
    return (weight_grad, row_loss)


def solution(mesh):
    return jax.shard_map(
        per_device,
        mesh=mesh,
        in_specs=(
            P(("groups", "dp"), None),
            P(("groups", "dp"), None),
            P(("groups", "dp")),
            P("dp", None),
            P("dp", None),
            P(),
            P(),
            P(),
            P(),
        ),
        out_specs=(P(("groups", "dp"), None), P(("groups", "dp"))),
        check_vma=False,
    )
```

profile of v0, /device:TPU:25, one launch (start us, length us, event | category | flops | bytes accessed | tf_op | source)
XLA Modules:
  0.0 129.7 jit_solution(12718824393975815760)
XLA Ops:
  0.6 3.3 %collective-permute-start.1 = (bf16[1024,1024]{1,0:T(8,128)(2,1)}, bf16[1024,1024]{1,0:T(8,128)(2,1)S(1)}, u32[]{:S(2)}, u32[]{:S(2)}) collective-permute-start(bf16[1024,1024]{1,0:T(8,128)(2,1)} %param.13), channel_id=1, source_target_pairs={{0,2},{1,3},{2,4},{3,5},{4,6},{5,7},{6,8},{7,9},{8,10},{9,11},{10,... | collective-permute-start | bytes 6291464 | tf_op jit(solution)/shard_map/ppermute | solution.py:26
  3.9 1.0 collective-permute-start
  5.0 45.3 %collective-permute-done.1 = bf16[1024,1024]{1,0:T(8,128)(2,1)S(1)} collective-permute-done((bf16[1024,1024]{1,0:T(8,128)(2,1)}, bf16[1024,1024]{1,0:T(8,128)(2,1)S(1)}, u32[]{:S(2)}, u32[]{:S(2)}) %collective-permute-start.1) | collective-permute-done | bytes 2097184 | tf_op jit(solution)/shard_map/ppermute | solution.py:26
  50.3 1.5 %collective-permute-start.2 = (bf16[1,1024,1024]{2,1,0:T(8,128)(2,1)S(1)}, bf16[1,1024,1024]{2,1,0:T(8,128)(2,1)}, u32[]{:S(2)}, u32[]{:S(2)}) collective-permute-start(bf16[1,1024,1024]{2,1,0:T(8,128)(2,1)S(1)} %bitcast.112), channel_id=1, source_target_pairs={{0,1},{1,0},{2,3},{3,2},{4,5},{5,4},{6,7},{7,6},{8,9},{9,8},{10,11... | collective-permute-start | bytes 6291464 | tf_op jit(solution)/shard_map/ppermute | solution.py:20
  51.9 3.4 %fusion.17 = f32[1024,8]{0,1:T(8,128)S(1)} fusion(bf16[1024,2048]{1,0:T(8,128)(2,1)} %param.9, bf16[8,8,2048]{2,1,0:T(8,128)(2,1)} %param.15, s32[]{:T(128)S(6)} %max.3), kind=kOutput, calls=%fused_computation.30 | convolution fusion | flops 33570816 | bytes 4259844 | tf_op jit(solution)/shard_map/dot_general | solution.py:31
  55.5 3.4 %fusion.21 = f32[1024,8]{0,1:T(8,128)S(1)} fusion(bf16[1024,2048]{1,0:T(8,128)(2,1)} %param.9, bf16[8,8,2048]{2,1,0:T(8,128)(2,1)} %param.14, s32[]{:T(128)S(6)} %select_n.93), kind=kOutput, calls=%fused_computation.35 | convolution fusion | flops 33570816 | bytes 4259844 | tf_op jit(solution)/shard_map/dot_general | solution.py:31
  59.4 1.2 constant_dynamic-slice_fusion
  60.8 4.9 %select_bitcast_fusion.2 = (bf16[1,1,1024,1024]{3,2,1,0:T(8,128)(2,1)S(1)}, bf16[1,1,1024,1024]{3,2,1,0:T(8,128)(2,1)S(1)}, bf16[1,1,1024,1024]{3,2,1,0:T(8,128)(2,1)S(1)}, bf16[1,1,1024,1024]{3,2,1,0:T(8,128)(2,1)}) fusion(bf16[1,1024,1024]{2,1,0:T(8,128)(2,1)} %collective-permute-done.2, pred[]{:T(512)S(6)} %eq.24, bf16[1024,1024]{1,0:T(8,128)(2,1)} %copy-done.7, ...), kind=kLoop, calls=%fused_computation.17 | loop fusion | flops 4194304 | bytes 16777216 | tf_op jit(solution)/shard_map/stack | solution.py:65
  66.0 1.8 %copy-done.3 = bf16[1024,2048]{1,0:T(8,128)(2,1)S(1)} copy-done((bf16[1024,2048]{1,0:T(8,128)(2,1)S(1)}, bf16[1024,2048]{1,0:T(8,128)(2,1)}, u32[]{:S(2)}) %copy-start.3) | copy-done | bytes 4194328
  67.8 5.8 %convert_bitcast_fusion = bf16[1024,1024]{0,1:T(8,128)(2,1)} fusion(bf16[2048,1024]{1,0:T(8,128)(2,1)S(1)} %bitcast.109, bf16[1024,2048]{1,0:T(8,128)(2,1)S(1)} %copy-done.3), kind=kOutput, calls=%fused_computation.15 | convolution fusion | flops 4296015872 | bytes 10485760 | tf_op jit(solution)/shard_map/dot_general | solution.py:37
  73.6 3.9 %copy.18 = bf16[1024,1024]{1,0:T(8,128)(2,1)} copy(bf16[1024,1024]{0,1:T(8,128)(2,1)} %convert_bitcast_fusion) | data formatting | bytes 4194304 | tf_op jit(solution)/shard_map/convert_element_type | solution.py:37
  77.6 3.7 %copy.35 = bf16[128,8,8,128]{3,2,1,0:T(8,128)(2,1)} copy(bf16[128,8,8,128]{3,1,2,0:T(8,128)(2,1)} %bitcast.107) | data formatting | bytes 4194304
  81.6 1.8 %copy-done.4 = bf16[1024,2048]{1,0:T(8,128)(2,1)S(1)} copy-done((bf16[1024,2048]{1,0:T(8,128)(2,1)S(1)}, bf16[1024,2048]{1,0:T(8,128)(2,1)}, u32[]{:S(2)}) %copy-start.4) | copy-done | bytes 4194328
  83.4 5.7 %convert_bitcast_fusion.1 = bf16[1024,1024]{0,1:T(8,128)(2,1)} fusion(bf16[2048,1024]{1,0:T(8,128)(2,1)S(1)} %bitcast.110, bf16[1024,2048]{1,0:T(8,128)(2,1)S(1)} %copy-done.4), kind=kOutput, calls=%fused_computation.18 | convolution fusion | flops 4296015872 | bytes 10485760 | tf_op jit(solution)/shard_map/dot_general | solution.py:37
  89.2 2.9 %copy.16 = bf16[1024,1024]{1,0:T(8,128)(2,1)S(1)} copy(bf16[1024,1024]{0,1:T(8,128)(2,1)} %convert_bitcast_fusion.1) | data formatting | bytes 4194304 | tf_op jit(solution)/shard_map/convert_element_type | solution.py:37
  92.7 0.9 copy-done.8
  94.3 0.7 fusion.7
  96.4 1.4 %multiply_convert_fusion = bf16[64,16,8,128]{3,2,1,0:T(8,128)(2,1)S(1)} fusion(f32[64,8,128]{2,1,0:T(8,128)S(1)} %copy.21, f32[64,16,8]{2,1,0:T(8,128)S(1)} %copy.15), kind=kLoop, calls=%fused_computation.8 | loop fusion | flops 2097152 | bytes 2392064 | tf_op jit(solution)/shard_map/convert_element_type | solution.py:127
  97.8 7.0 %convolution_bitcast_fusion = f32[2048,1024]{0,1:T(8,128)} fusion(bf16[1024,2048]{1,0:T(8,128)(2,1)S(1)} %copy-done.5, bf16[128,8,8,128]{3,2,1,0:T(8,128)(2,1)S(1)} %bitcast.115), kind=kOutput, calls=%fused_computation.2 | convolution fusion | flops 4294967296 | bytes 14680064 | tf_op jit(solution)/shard_map/dot_general | solution.py:129
  104.9 9.3 %copy.30 = f32[2048,1024]{1,0:T(8,128)} copy(f32[2048,1024]{0,1:T(8,128)} %convolution_bitcast_fusion) | data formatting | bytes 16777216 | tf_op jit(solution)/shard_map/reshape;reshape | solution.py:76
  114.1 4.6 %select_bitcast_fusion = f32[1,1024,1024]{2,1,0:T(8,128)S(1)} fusion(f32[1,2,1024,1024]{3,2,1,0:T(8,128)} %bitcast.105, pred[]{:T(512)S(6)} %eq.24), kind=kLoop, calls=%fused_computation.7 | loop fusion | flops 1048576 | bytes 12582913 | tf_op jit(solution)/shard_map/jit(_where)/select_n | solution.py:81
  118.7 0.7 collective-permute-start.3
  120.0 6.2 %collective-permute-done.3 = f32[1,1024,1024]{2,1,0:T(8,128)S(1)} collective-permute-done((f32[1,1024,1024]{2,1,0:T(8,128)S(1)}, f32[1,1024,1024]{2,1,0:T(8,128)S(1)}, u32[]{:S(2)}, u32[]{:S(2)}) %collective-permute-start.3) | collective-permute-done | bytes 4194336 | tf_op jit(solution)/shard_map/ppermute | solution.py:20
  126.2 3.5 %fusion.2 = f32[1024,1024]{1,0:T(8,128)} fusion(f32[1,1024,1024]{2,1,0:T(8,128)S(1)} %collective-permute-done.3, f32[1,2,1024,1024]{3,2,1,0:T(8,128)S(1)} %bitcast.106, pred[]{:T(512)S(6)} %eq.24), kind=kLoop, calls=%fused_computation.6 | loop fusion | flops 2097152 | bytes 16777216 | tf_op jit(solution)/shard_map/reshape | solution.py:84
  (41 shorter events, 4.9 us)
Async XLA Ops:
  0.6 51.2 %copy-start = (f32[8,20,1024]{2,0,1:T(8,128)S(1)}, f32[8,20,1024]{2,0,1:T(8,128)}, u32[]{:S(2)}) copy-start(f32[8,20,1024]{2,0,1:T(8,128)} %param.16) | copy-start | bytes 1966084
  0.6 49.6 %collective-permute-start.1 = (bf16[1024,1024]{1,0:T(8,128)(2,1)}, bf16[1024,1024]{1,0:T(8,128)(2,1)S(1)}, u32[]{:S(2)}, u32[]{:S(2)}) collective-permute-start(bf16[1024,1024]{1,0:T(8,128)(2,1)} %param.13), channel_id=1, source_target_pairs={{0,2},{1,3},{2,4},{3,5},{4,6},{5,7},{6,8},{7,9},{8,10},{9,11},{10,... | collective-permute-start | bytes 6291464 | tf_op jit(solution)/shard_map/ppermute | solution.py:26
  3.9 56.8 %collective-permute-start = (bf16[1,1024,1024]{2,1,0:T(8,128)(2,1)}, bf16[1,1024,1024]{2,1,0:T(8,128)(2,1)}, u32[]{:S(2)}, u32[]{:S(2)}) collective-permute-start(bf16[1,1024,1024]{2,1,0:T(8,128)(2,1)} %bitcast.111), channel_id=1, source_target_pairs={{0,1},{1,0},{2,3},{3,2},{4,5},{5,4},{6,7},{7,6},{8,9},{9,8},{10,11... | collective-permute-start | bytes 6291464 | tf_op jit(solution)/shard_map/ppermute | solution.py:20
  50.3 8.6 %copy-start.7 = (bf16[1024,1024]{1,0:T(8,128)(2,1)}, bf16[1024,1024]{1,0:T(8,128)(2,1)S(1)}, u32[]{:S(2)}) copy-start(bf16[1024,1024]{1,0:T(8,128)(2,1)S(1)} %collective-permute-done.1) | copy-start | bytes 6291460
  50.3 10.5 %collective-permute-start.2 = (bf16[1,1024,1024]{2,1,0:T(8,128)(2,1)S(1)}, bf16[1,1024,1024]{2,1,0:T(8,128)(2,1)}, u32[]{:S(2)}, u32[]{:S(2)}) collective-permute-start(bf16[1,1024,1024]{2,1,0:T(8,128)(2,1)S(1)} %bitcast.112), channel_id=1, source_target_pairs={{0,1},{1,0},{2,3},{3,2},{4,5},{5,4},{6,7},{7,6},{8,9},{9,8},{10,11... | collective-permute-start | bytes 6291464 | tf_op jit(solution)/shard_map/ppermute | solution.py:20
  65.6 2.2 %copy-start.3 = (bf16[1024,2048]{1,0:T(8,128)(2,1)S(1)}, bf16[1024,2048]{1,0:T(8,128)(2,1)}, u32[]{:S(2)}) copy-start(bf16[1024,2048]{1,0:T(8,128)(2,1)} %param.9) | copy-start | bytes 12582916
  77.6 3.7 %copy-start.6 = (bf16[1,1,1024,1024]{3,2,1,0:T(8,128)(2,1)S(1)}, bf16[1,1,1024,1024]{3,2,1,0:T(8,128)(2,1)}, u32[]{:S(2)}) copy-start(bf16[1,1,1024,1024]{3,2,1,0:T(8,128)(2,1)} %get-tuple-element.12) | copy-start | bytes 6291460
  81.2 2.2 %copy-start.4 = (bf16[1024,2048]{1,0:T(8,128)(2,1)S(1)}, bf16[1024,2048]{1,0:T(8,128)(2,1)}, u32[]{:S(2)}) copy-start(bf16[1024,2048]{1,0:T(8,128)(2,1)} %param.9) | copy-start | bytes 12582916
  92.0 1.6 %copy-start.8 = (bf16[128,8,8,128]{3,2,1,0:T(8,128)(2,1)S(1)}, bf16[128,8,8,128]{3,2,1,0:T(8,128)(2,1)}, u32[]{:S(2)}) copy-start(bf16[128,8,8,128]{3,2,1,0:T(8,128)(2,1)} %copy.35) | copy-start | bytes 6291460
  92.7 2.3 %copy-start.9 = (s32[64,20]{0,1:T(8,128)S(1)}, s32[64,20]{0,1:T(8,128)}, u32[]{:S(2)}) copy-start(s32[64,20]{0,1:T(8,128)} %param.10) | copy-start | bytes 15364
  92.7 3.1 %copy-start.10 = (s32[64]{0:T(128)S(1)}, s32[64]{0:T(128)}, u32[]{:S(2)}) copy-start(s32[64]{0:T(128)} %param.11) | copy-start | bytes 772
  94.3 3.5 %copy-start.5 = (bf16[1024,2048]{1,0:T(8,128)(2,1)S(1)}, bf16[1024,2048]{1,0:T(8,128)(2,1)}, u32[]{:S(2)}) copy-start(bf16[1024,2048]{1,0:T(8,128)(2,1)} %param.9) | copy-start | bytes 12582916
  114.1 12.1 %copy-start.2 = (f32[2048,1024]{1,0:T(8,128)S(1)}, f32[2048,1024]{1,0:T(8,128)}, u32[]{:S(2)}) copy-start(f32[2048,1024]{1,0:T(8,128)} %copy.30) | copy-start | bytes 25165828
  118.7 7.5 %collective-permute-start.3 = (f32[1,1024,1024]{2,1,0:T(8,128)S(1)}, f32[1,1024,1024]{2,1,0:T(8,128)S(1)}, u32[]{:S(2)}, u32[]{:S(2)}) collective-permute-start(f32[1,1024,1024]{2,1,0:T(8,128)S(1)} %select_bitcast_fusion), channel_id=1, source_target_pairs={{0,1},{1,0},{2,3},{3,2},{4,5},{5,4},{6,7},{7,6},{8,9},{9,8},{10,11... | collective-permute-start | bytes 12582920 | tf_op jit(solution)/shard_map/ppermute | solution.py:20
  126.2 3.5 %copy-start.1 = (f32[8,20,1024]{2,0,1:T(8,128)S(1)}, f32[8,20,1024]{2,0,1:T(8,128)}, u32[]{:S(2)}) copy-start(f32[8,20,1024]{2,0,1:T(8,128)} %param.16) | copy-start | bytes 1966084
where the time goes:
time: 130 us
  waiting for transfers between devices  51.6 us (40%)
  matrix products  27.9 us (21%)
  local copies, waits for them, and re-layouts  26.8 us (21%)
  other arithmetic  16 us (12%)
  starting transfers between devices  6.55 us (5%)
    ppermute x1, waiting for transfers between devices, shifted(): return lax.ppermute(block, axis, route)  45.3 us
    dot_general x2, matrix products, policy_of(): jnp.dot(tokens, value_proj, preferred_element_type=jnp.float32)  11.5 us
    another operation x1, local copies, waits for them, and re-layouts, scatter_level(): viewed = blocks.reshape(count_now, 2, blocks.shape[1], width)  9.26 us
    unnamed x26, local copies, waits for them, and re-layouts  8.91 us
    dot_general x1, matrix products, per_device(): lax.dot_general(tokens, value_grad, (((0,), (0,)), ((), ())), preferred_e...  7.02 us
    dot_general x2, matrix products, policy_of(): lax.dot_general(tokens, query_proj, (((1,), (1,)), ((), ())), preferred_e...  6.83 us
    convert_element_type x2, local copies, waits for them, and re-layouts, policy_of(): jnp.dot(tokens, value_proj, preferred_element_type=jnp.float32)  6.8 us
    ppermute x3, waiting for transfers between devices, partner_2(): return lax.ppermute(block, axis, route)  6.24 us
  transfers between devices with their start and end apart: 4, of which 2 were waited for; matrix products, arithmetic and copies ran while one was open for 7% of the time, Pallas kernels for 0%

commit v1 on v0

v1 whole, which is shorter than its diff:
```python
import jax
import jax.numpy as jnp
from jax import lax
from jax.sharding import PartitionSpec as P

H = 8
DH = 128
A = 20
OBS = 16
LEVELS = 8
EXACT = lax.Precision.HIGHEST


def partner_2(block, axis, bit):
    count = lax.axis_size(axis)
    route = []
    for low in range(count):
        high = low | 1 << bit
        if high != low and high < count:
            route += [(low, high), (high, low)]
    return lax.ppermute(block, axis, route)


def shifted(block, axis, distance):
    devices = range(lax.axis_size(axis))
    route = [(i - distance, i) for i in devices if i - distance in devices]
    return lax.ppermute(block, axis, route)


def head_map(proj, move_head):
    depth = proj.shape[0]
    product = jnp.einsum(
        "dhe,ahe->had",
        proj.astype(jnp.float32).reshape(depth, H, DH),
        move_head.reshape(A, H, DH),
        precision=EXACT,
    )
    return product.reshape(H * A, depth).astype(jnp.bfloat16)


def gather_columns(block, member, bit_count):
    for bit_place in range(bit_count):
        received = partner_2(block, "dp", bit_place)
        upper_side = member // (1 << bit_place) % 2 == 1
        lower_half = jnp.where(upper_side, received, block)
        upper_half = jnp.where(upper_side, block, received)
        block = jnp.concatenate([lower_half, upper_half], axis=1)
    return block


def scatter_columns(block, member, bit_count):
    for bit_place in reversed(range(bit_count)):
        half = block.shape[1] // 2
        upper_side = member // (1 << bit_place) % 2 == 1
        kept = jnp.where(upper_side, block[:, half:], block[:, :half])
        sent = jnp.where(upper_side, block[:, :half], block[:, half:])
        block = kept + partner_2(sent, "dp", bit_place)
    return block


def attention_of(tokens, query_proj):
    scores = lax.dot_general(
        tokens, query_proj, (((1,), (1,)), ((), ())), preferred_element_type=jnp.float32
    ).reshape(-1, OBS, H)
    exp_scores = jnp.exp(5.0 * jnp.tanh(scores / 5.0))
    attention = exp_scores / jnp.sum(exp_scores, axis=1, keepdims=True)
    return attention.astype(jnp.bfloat16).astype(jnp.float32)


def policy_of(tokens, attention, mapped, legal_float):
    row_count = legal_float.shape[0]
    moved = lax.dot_general(
        tokens, mapped, (((1,), (1,)), ((), ())), preferred_element_type=jnp.float32
    ).reshape(row_count, OBS, H, A)
    raw_logits = jnp.sum(attention[..., None] * moved, axis=(1, 2))
    logits = 30.0 * jnp.tanh(raw_logits / 30.0)
    exp_logits = jnp.exp(logits) * legal_float
    partition = jnp.sum(exp_logits, axis=1, keepdims=True)
    return logits, exp_logits / partition, logits - jnp.log(partition)


def general_device(
    tokens, legal_moves, action_label, value_weight, value_prior,
    query_weight, query_prior, policy_head, head_prior,
):
    group_size = lax.axis_size("dp") // LEVELS
    bit_count = group_size.bit_length() - 1
    device_place = lax.axis_index("dp")
    level_index = device_place // group_size
    member = device_place % group_size
    lower_index = jnp.maximum(level_index - 1, 0)

    def of_level(array, index):
        return lax.dynamic_index_in_dim(array, index, 0, keepdims=False)

    move_head = of_level(policy_head, level_index)
    prior_map = head_map(value_prior, of_level(head_prior, level_index))
    own_map = head_map(value_weight, move_head)
    lower_map = gather_columns(shifted(prior_map, "dp", group_size), member, bit_count)
    own_map = gather_columns(own_map, member, bit_count)
    attention = attention_of(tokens, of_level(query_weight, level_index))
    lower_attention = attention_of(tokens, of_level(query_prior, lower_index))
    legal_float = legal_moves.astype(jnp.float32)
    logits, policy, log_policy = policy_of(tokens, attention, own_map, legal_float)
    _, lower_policy, _ = policy_of(tokens, lower_attention, lower_map, legal_float)
    uniform_policy = legal_float / jnp.sum(legal_float, axis=1, keepdims=True)
    partner = jnp.where(level_index == 0, uniform_policy, lower_policy)
    onehot = (action_label[:, None] == jnp.arange(A, dtype=jnp.int32)[None, :]).astype(jnp.float32)
    target = 0.5 * onehot + 0.5 * partner
    row_loss = -jnp.sum(target * log_policy, axis=1)
    logit_grad = (policy - target) * (1.0 - (logits / 30.0) ** 2)
    token_grad = attention[..., None] * logit_grad[:, None, None, :]
    token_grad = token_grad.astype(jnp.bfloat16).reshape(tokens.shape[0], H * A)
    mapped_grad = lax.dot_general(
        token_grad, tokens, (((0,), (0,)), ((), ())), preferred_element_type=jnp.float32
    )
    mapped_grad = scatter_columns(mapped_grad, member, bit_count).reshape(H, A, -1)
    weight_grad = jnp.einsum(
        "had,ahe->dhe", mapped_grad, move_head.reshape(A, H, DH), precision=EXACT
    )
    return weight_grad.reshape(-1, H * DH), row_loss


def solution(mesh):
    return jax.shard_map(
        general_device,
        mesh=mesh,
        in_specs=(
            P(("groups", "dp"), None),
            P(("groups", "dp"), None),
            P(("groups", "dp")),
            P("dp", None),
            P("dp", None),
            P(),
            P(),
            P(),
            P(),
        ),
        out_specs=(P(("groups", "dp"), None), P(("groups", "dp"))),
        check_vma=False,
    )
```

time: 130 us -> 74.8 us (0.58)
  the two profiles are of different devices: /device:TPU:25 before, /device:TPU:0 now
where the time goes in v1:
time: 74.8 us; the launch traced here: 74.2 us
  matrix products  26.2 us (35%)
  local copies, waits for them, and re-layouts  26.1 us (35%)
  other arithmetic  13.2 us (18%)
  starting transfers between devices  6.22 us (8%)
  waiting for transfers between devices  1.58 us (2%)
  between operations  0.86 us (1%)
    reshape x2, local copies, waits for them, and re-layouts, policy_of(): moved = lax.dot_general(tokens, mapped, (((1,), (1,)), ((), ())), preferr...  7.89 us
    dot_general x2, matrix products, attention_of(): lax.dot_general(tokens, query_proj, (((1,), (1,)), ((), ())), preferred_e...  6.83 us
    dot_general x1, matrix products, general_device(): jnp.einsum('had,ahe->dhe', mapped_grad, move_head.reshape(A, H, DH), prec...  5.95 us
    reduce_sum x2, other arithmetic, policy_of(): raw_logits = jnp.sum(attention[..., None] * moved, axis=(1, 2))  5.93 us
    unnamed x14, local copies, waits for them, and re-layouts  5.85 us
    ppermute x1, starting transfers between devices, shifted(): return lax.ppermute(block, axis, route)  5.59 us
    dot_general x2, matrix products, policy_of(): lax.dot_general(tokens, mapped, (((1,), (1,)), ((), ())), preferred_eleme...  5.29 us
    dot_general x2, matrix products, head_map(): jnp.einsum('dhe,ahe->had', proj.astype(jnp.float32).reshape(depth, H, DH)...  5.07 us
  transfers between devices with their start and end apart: 4, of which 1 were waited for; matrix products, arithmetic and copies ran while one was open for 40% of the time, Pallas kernels for 0%

profile of v1, /device:TPU:0, one launch (start us, length us, event | category | flops | bytes accessed | tf_op | source)
XLA Modules:
  0.0 74.2 jit_solution(13785168895051105467)
XLA Ops:
  0.7 1.6 %constant_dynamic-slice_fusion = (f32[1,20,1024]{2,0,1:T(1,128)S(1)}, f32[1,20,1024]{2,0,1:T(1,128)S(1)}) fusion(f32[8,20,1024]{2,0,1:T(8,128)} %param.17, s32[]{:T(128)S(6)} %select_n.69, f32[8,20,1024]{2,0,1:T(8,128)} %param.16), kind=kLoop, calls=%fused_computation.61 | loop fusion | bytes 327684 | tf_op jit(solution)/shard_map/jit(dynamic_index_in_dim)/dynamic_slice | solution.py:94
  2.6 1.7 %fusion.11 = bf16[8,20,1024]{2,1,0:T(8,128)(2,1)S(1)} fusion(f32[20,8,128]{2,1,0:T(8,128)S(1)} %bitcast.55, bf16[1024,1024]{1,0:T(8,128)(2,1)S(1)} %copy-done), kind=kOutput, calls=%fused_computation.14 | convolution fusion | flops 251822080 | bytes 2506752 | tf_op jit(solution)/shard_map/dhe,ahe->had/dot_general | solution.py:32
  5.2 5.6 %collective-permute-start.1 = (bf16[160,1024]{1,0:T(8,128)(2,1)}, bf16[160,1024]{1,0:T(8,128)(2,1)}, u32[]{:S(2)}, u32[]{:S(2)}) collective-permute-start(bf16[160,1024]{1,0:T(8,128)(2,1)} %convert_element_type.61), channel_id=1, source_target_pairs={{0,2},{1,3},{2,4},{3,5},{4,6},{5,7},{6,8},{7,9},{8,10},{9,11},{10,... | collective-permute-start | bytes 983048 | tf_op jit(solution)/shard_map/ppermute | solution.py:27
  10.8 3.3 %fusion.8 = bf16[8,20,1024]{2,1,0:T(8,128)(2,1)S(1)} fusion(f32[20,8,128]{2,1,0:T(8,128)S(1)} %bitcast.53, bf16[1024,1024]{1,0:T(8,128)(2,1)} %param.12), kind=kOutput, calls=%fused_computation.13 | convolution fusion | flops 251822080 | bytes 2506752 | tf_op jit(solution)/shard_map/dhe,ahe->had/dot_general | solution.py:32
  14.3 3.4 %fusion.27 = f32[1024,8]{0,1:T(8,128)S(1)} fusion(bf16[1024,2048]{1,0:T(8,128)(2,1)} %param.9, bf16[8,8,2048]{2,1,0:T(8,128)(2,1)} %param.14, s32[]{:T(128)S(6)} %select_n.69), kind=kOutput, calls=%fused_computation.30 | convolution fusion | flops 33570816 | bytes 4259844 | tf_op jit(solution)/shard_map/dot_general | solution.py:62
  17.8 3.4 %fusion.23 = f32[1024,8]{0,1:T(8,128)S(1)} fusion(bf16[1024,2048]{1,0:T(8,128)(2,1)} %param.9, bf16[8,8,2048]{2,1,0:T(8,128)(2,1)} %param.15, s32[]{:T(128)S(6)} %max.3), kind=kOutput, calls=%fused_computation.25 | convolution fusion | flops 33570816 | bytes 4259844 | tf_op jit(solution)/shard_map/dot_general | solution.py:62
  23.0 1.2 %copy.25 = f32[64,16,8]{2,1,0:T(8,128)S(1)} copy(f32[64,16,8]{1,0,2:T(8,128)} %fusion.19) | data formatting | bytes 65536 | tf_op jit(solution)/shard_map/convert_element_type | solution.py:67
  24.2 1.9 %fusion.17 = f32[64,16,8]{1,0,2:T(8,128)} fusion(f32[64,16,8]{1,0,2:T(8,128)} %exp.30), kind=kOutput, calls=%fused_computation.18 | output fusion | flops 25103 | bytes 65536 | tf_op jit(solution)/shard_map/div | solution.py:66
  26.1 2.0 %copy.30 = f32[64,16,8]{2,1,0:T(8,128)} copy(f32[64,16,8]{1,0,2:T(8,128)} %fusion.17) | data formatting | bytes 65536 | tf_op jit(solution)/shard_map/convert_element_type | solution.py:67
  28.2 3.8 %convolution_bitcast_fusion.1 = f32[1024,160]{0,1:T(8,128)S(1)} fusion(bf16[1024,2048]{1,0:T(8,128)(2,1)} %param.9, bf16[160,1024]{1,0:T(8,128)(2,1)S(1)} %get-tuple-element.16, bf16[160,1024]{1,0:T(8,128)(2,1)S(1)} %get-tuple-element.15), kind=kOutput, calls=%fused_computation.12 | convolution fusion | flops 672399360 | bytes 5505024 | tf_op jit(solution)/shard_map/dot_general | solution.py:72
  31.9 1.3 %copy.28 = f32[1024,160]{1,0:T(8,128)} copy(f32[1024,160]{0,1:T(8,128)S(1)} %convolution_bitcast_fusion.1) | data formatting | bytes 1310720 | tf_op jit(solution)/shard_map/dot_general | solution.py:72
  33.2 3.9 %reshape.89 = f32[64,16,8,20]{3,2,1,0:T(8,128)} reshape(f32[1024,160]{1,0:T(8,128)} %copy.28) | data formatting | bytes 1310720 | tf_op jit(solution)/shard_map/reshape | solution.py:74
  37.7 3.1 %multiply_reduce_fusion.1 = f32[64,20]{1,0:T(8,128)S(1)} fusion(f32[64,16,8,20]{3,2,1,0:T(8,128)} %reshape.89, f32[64,16,8]{2,1,0:T(8,128)S(1)} %copy.25), kind=kLoop, calls=%fused_computation.4 | loop fusion | flops 326400 | bytes 693248 | tf_op jit(solution)/shard_map/reduce_sum | solution.py:75
  40.8 1.0 %broadcast_select_fusion.1 = (bf16[160,1024]{1,0:T(8,128)(2,1)S(1)}, bf16[160,1024]{1,0:T(8,128)(2,1)S(1)}) fusion(bf16[160,1024]{1,0:T(8,128)(2,1)S(1)} %collective-permute-done.2, bf16[160,1024]{1,0:T(8,128)(2,1)} %collective-permute-done.1, pred[]{:T(512)S(6)} %eq.26), kind=kLoop, calls=%fused_computation.40 | loop fusion | flops 327680 | bytes 1310721 | tf_op jit(solution)/shard_map/jit(_where)/select_n | solution.py:45
  41.8 1.5 %convolution_bitcast_fusion = f32[1024,160]{0,1:T(8,128)S(1)} fusion(bf16[1024,2048]{1,0:T(8,128)(2,1)S(1)} %copy-done.1, bf16[160,1024]{1,0:T(8,128)(2,1)S(1)} %get-tuple-element.14, bf16[160,1024]{1,0:T(8,128)(2,1)S(1)} %get-tuple-element.13), kind=kOutput, calls=%fused_computation.11 | convolution fusion | flops 672399360 | bytes 5505024 | tf_op jit(solution)/shard_map/dot_general | solution.py:72
  43.3 1.3 %copy.33 = f32[1024,160]{1,0:T(8,128)} copy(f32[1024,160]{0,1:T(8,128)S(1)} %convolution_bitcast_fusion) | data formatting | bytes 1310720 | tf_op jit(solution)/shard_map/dot_general | solution.py:72
  44.7 4.0 %reshape.92 = f32[64,16,8,20]{3,2,1,0:T(8,128)} reshape(f32[1024,160]{1,0:T(8,128)} %copy.33) | data formatting | bytes 1310720 | tf_op jit(solution)/shard_map/reshape | solution.py:74
  48.6 2.8 %multiply_reduce_fusion = f32[64,20]{1,0:T(8,128)S(1)} fusion(f32[64,16,8,20]{3,2,1,0:T(8,128)} %reshape.92, f32[64,16,8]{2,1,0:T(8,128)S(1)} %copy-done.2), kind=kLoop, calls=%fused_computation.3 | loop fusion | flops 326400 | bytes 693248 | tf_op jit(solution)/shard_map/reduce_sum | solution.py:75
  52.0 2.2 %multiply_convert_fusion = bf16[64,16,8,20]{3,2,1,0:T(8,128)(2,1)} fusion(f32[64,20]{1,0:T(8,128)S(1)} %subtract_multiply_fusion, f32[64,16,8]{2,1,0:T(8,128)S(1)} %copy.25), kind=kLoop, calls=%fused_computation.2 | loop fusion | flops 327680 | bytes 365568 | tf_op jit(solution)/shard_map/convert_element_type | solution.py:113
  54.2 3.1 %convert_element_type.63 = bf16[1024,160]{1,0:T(8,128)(2,1)S(1)} reshape(bf16[64,16,8,20]{3,2,1,0:T(8,128)(2,1)} %multiply_convert_fusion) | data formatting | bytes 655360 | tf_op jit(solution)/shard_map/convert_element_type | solution.py:113
  57.3 3.1 %fusion.48 = f32[160,2048]{1,0:T(8,128)S(1)} fusion(bf16[1024,160]{1,0:T(8,128)(2,1)S(1)} %convert_element_type.63, bf16[1024,2048]{1,0:T(8,128)(2,1)} %param.9), kind=kOutput, calls=%fused_computation.67 | convolution fusion | flops 671088640 | bytes 5832704 | tf_op jit(solution)/shard_map/dot_general | solution.py:114
  61.0 1.6 %collective-permute-done.3 = f32[160,1024]{1,0:T(8,128)S(1)} collective-permute-done((f32[160,1024]{1,0:T(8,128)S(1)}, f32[160,1024]{1,0:T(8,128)S(1)}, u32[]{:S(2)}, u32[]{:S(2)}) %collective-permute-start.3) | collective-permute-done | bytes 655392 | tf_op jit(solution)/shard_map/ppermute | solution.py:21
  62.9 5.9 %fusion.35 = f32[8,128,1024]{2,1,0:T(8,128)} fusion(f32[8,20,1024]{2,1,0:T(8,128)S(1)} %reshape.93, f32[20,8,128]{2,1,0:T(8,128)} %bitcast.54), kind=kOutput, calls=%fused_computation.44 | convolution fusion | flops 251658240 | bytes 4931584 | tf_op jit(solution)/shard_map/had,ahe->dhe/dot_general | solution.py:118
  68.8 5.3 %copy.35 = f32[1024,1024]{1,0:T(8,128)} copy(f32[1024,1024]{0,1:T(8,128)} %bitcast.52) | data formatting | bytes 8388608
  (33 shorter events, 5.2 us)
Async XLA Ops:
  0.6 2.0 %copy-start = (bf16[1024,1024]{1,0:T(8,128)(2,1)S(1)}, bf16[1024,1024]{1,0:T(8,128)(2,1)}, u32[]{:S(2)}) copy-start(bf16[1024,1024]{1,0:T(8,128)(2,1)} %param.13) | copy-start | bytes 6291460
  2.2 15.5 %copy-start.3 = (f32[1,20,1024]{2,0,1:T(1,128)}, f32[1,20,1024]{2,0,1:T(1,128)S(1)}, u32[]{:S(2)}) copy-start(f32[1,20,1024]{2,0,1:T(1,128)S(1)} %get-tuple-element.18) | copy-start | bytes 245764
  5.2 32.0 %collective-permute-start.1 = (bf16[160,1024]{1,0:T(8,128)(2,1)}, bf16[160,1024]{1,0:T(8,128)(2,1)}, u32[]{:S(2)}, u32[]{:S(2)}) collective-permute-start(bf16[160,1024]{1,0:T(8,128)(2,1)} %convert_element_type.61), channel_id=1, source_target_pairs={{0,2},{1,3},{2,4},{3,5},{4,6},{5,7},{6,8},{7,9},{8,10},{9,11},{10,... | collective-permute-start | bytes 983048 | tf_op jit(solution)/shard_map/ppermute | solution.py:27
  14.2 13.9 %collective-permute-start = (bf16[160,1024]{1,0:T(8,128)(2,1)S(1)}, bf16[160,1024]{1,0:T(8,128)(2,1)S(1)}, u32[]{:S(2)}, u32[]{:S(2)}) collective-permute-start(bf16[160,1024]{1,0:T(8,128)(2,1)S(1)} %convert_element_type.56), channel_id=1, source_target_pairs={{0,1},{1,0},{2,3},{3,2},{4,5},{5,4},{6,7},{7,6},{8,9},{9,8},{10,11... | collective-permute-start | bytes 983048 | tf_op jit(solution)/shard_map/ppermute | solution.py:21
  14.3 7.9 %copy-start.4 = (s32[64,20]{0,1:T(8,128)S(1)}, s32[64,20]{0,1:T(8,128)}, u32[]{:S(2)}) copy-start(s32[64,20]{0,1:T(8,128)} %param.10) | copy-start | bytes 15364
  37.2 4.6 %copy-start.1 = (bf16[1024,2048]{1,0:T(8,128)(2,1)S(1)}, bf16[1024,2048]{1,0:T(8,128)(2,1)}, u32[]{:S(2)}) copy-start(bf16[1024,2048]{1,0:T(8,128)(2,1)} %param.9) | copy-start | bytes 12582916
  37.2 3.6 %collective-permute-start.2 = (bf16[160,1024]{1,0:T(8,128)(2,1)}, bf16[160,1024]{1,0:T(8,128)(2,1)S(1)}, u32[]{:S(2)}, u32[]{:S(2)}) collective-permute-start(bf16[160,1024]{1,0:T(8,128)(2,1)} %collective-permute-done.1), channel_id=1, source_target_pairs={{0,1},{1,0},{2,3},{3,2},{4,5},{5,4},{6,7},{7,6},{8,9},{9,8},{10,11... | collective-permute-start | bytes 983048 | tf_op jit(solution)/shard_map/ppermute | solution.py:21
  44.7 4.0 %copy-start.2 = (f32[64,16,8]{2,1,0:T(8,128)S(1)}, f32[64,16,8]{2,1,0:T(8,128)}, u32[]{:S(2)}) copy-start(f32[64,16,8]{2,1,0:T(8,128)} %copy.30) | copy-start | bytes 98308
  44.7 7.0 %copy-start.5 = (s32[64]{0:T(128)S(1)}, s32[64]{0:T(128)}, u32[]{:S(2)}) copy-start(s32[64]{0:T(128)} %param.11) | copy-start | bytes 772
  60.4 2.2 %collective-permute-start.3 = (f32[160,1024]{1,0:T(8,128)S(1)}, f32[160,1024]{1,0:T(8,128)S(1)}, u32[]{:S(2)}, u32[]{:S(2)}) collective-permute-start(f32[160,1024]{1,0:T(8,128)S(1)} %slice_select_fusion), channel_id=1, source_target_pairs={{0,1},{1,0},{2,3},{3,2},{4,5},{5,4},{6,7},{7,6},{8,9},{9,8},{10,11... | collective-permute-start | bytes 1966088 | tf_op jit(solution)/shard_map/ppermute | solution.py:21

commit v2 on v1

--- a/solution.py
+++ b/solution.py
@@ -1,6 +1,8 @@
 import jax
 import jax.numpy as jnp
 from jax import lax
+from jax.experimental import pallas as pl
+from jax.experimental.pallas import tpu as pltpu
 from jax.sharding import PartitionSpec as P
 
 H = 8
@@ -121,9 +123,356 @@
     return weight_grad.reshape(-1, H * DH), row_loss
 
 
+PAIR = 2
+TOP = 16
+SPREAD = H * A
+BLOCK_ROWS = 16
+F32 = jnp.float32
+BF16 = jnp.bfloat16
+VMEM_BYTES = 48 * 2**20
+
+
+def dot_nt(left, right):
+    return lax.dot_general(left, right, (((1,), (1,)), ((), ())), preferred_element_type=F32)
+
+
+def dot_nn(left, right):
+    return lax.dot_general(left, right, (((1,), (0,)), ((), ())), preferred_element_type=F32)
+
+
+def dot_tn(left, right, precision=None):
+    return lax.dot_general(
+        left, right, (((0,), (0,)), ((), ())), preferred_element_type=F32, precision=precision
+    )
+
+
+def split_high(value):
+    high = value.astype(BF16)
+    return high, (value - high.astype(F32)).astype(BF16)
+
+
+def spread_heads(rows):
+    width = rows.shape[1]
+    top = rows[:TOP]
+    lane_head = lax.broadcasted_iota(jnp.int32, (TOP, width), 1) // DH
+    pieces = [jnp.where(lane_head == h, top, 0.0) for h in range(H)]
+    rest = rows[TOP:A]
+    rest = jnp.concatenate([rest, rest], axis=0)
+    lane_head = lax.broadcasted_iota(jnp.int32, (8, width), 1) // DH
+    upper = lax.broadcasted_iota(jnp.int32, (8, width), 0) // 4
+    pieces += [jnp.where(lane_head == 2 * i + upper, rest, 0.0) for i in range(H // 2)]
+    return jnp.concatenate(pieces, axis=0)
+
+
+def level_here(group_size):
+    return lax.axis_index("dp") // group_size
+
+
+def build_spread(level, head_ref, spread_ref):
+    rows = head_ref[:, pl.ds(level, 1), :].reshape(A, H * DH)
+    high, low = split_high(spread_heads(rows))
+    spread_ref[:SPREAD, :] = high
+    spread_ref[SPREAD:, :] = low
+
+
+def folded(spread_ref, proj):
+    product = dot_nt(spread_ref[...], proj)
+    return product[:SPREAD] + product[SPREAD:]
+
+
+def map_kernel(level_ref, head_ref, proj_ref, out_ref, spread_ref):
+    @pl.when(pl.program_id(0) == 0)
+    def _():
+        build_spread(level_ref[0], head_ref, spread_ref)
+
+    out_ref[...] = folded(spread_ref, proj_ref[...]).astype(BF16)
+
+
+def prior_map_of(level, head_t, proj, chunk):
+    depth, width = proj.shape
+    return pl.pallas_call(
+        map_kernel,
+        grid_spec=pltpu.PrefetchScalarGridSpec(
+            num_scalar_prefetch=1,
+            grid=(depth // chunk,),
+            in_specs=[
+                pl.BlockSpec(head_t.shape, lambda i, s: (0, 0, 0)),
+                pl.BlockSpec((chunk, width), lambda i, s: (i, 0)),
+            ],
+            out_specs=pl.BlockSpec((SPREAD, chunk), lambda i, s: (0, i)),
+            scratch_shapes=[pltpu.VMEM((2 * SPREAD, width), BF16)],
+        ),
+        out_shape=jax.ShapeDtypeStruct((SPREAD, depth), BF16),
+        compiler_params=pltpu.CompilerParams(vmem_limit_bytes=VMEM_BYTES),
+        cost_estimate=pl.CostEstimate(
+            flops=4 * SPREAD * depth * width, bytes_accessed=2 * depth * width, transcendentals=0
+        ),
+    )(level, head_t, proj)
+
+
+def pool_kernel(place_ref, tokens_ref, query_ref, prior_ref, out_ref):
+    block = tokens_ref.shape[0]
+    half = out_ref.shape[3]
+    level = place_ref[0]
+    lower = jnp.maximum(level - 1, 0)
+    tokens = tokens_ref[...]
+    scores = jnp.concatenate(
+        [dot_nt(query_ref[level], tokens), dot_nt(prior_ref[lower], tokens)], axis=0
+    )
+    exp_scores = jnp.exp(5.0 * jnp.tanh(scores / 5.0))
+    first, rest = split_high(exp_scores)
+    second, third = split_high(exp_scores - first.astype(F32))
+    row_of = lax.broadcasted_iota(jnp.int32, (block, block), 0) // OBS
+    column_of = lax.broadcasted_iota(jnp.int32, (block, block), 1) // OBS
+    same_row = (row_of == column_of).astype(F32).astype(BF16)
+    parts = dot_nn(jnp.concatenate([first, second, third], axis=0), same_row)
+    total = parts[: 2 * H] + parts[2 * H : 4 * H] + parts[4 * H :]
+    attention = (exp_scores / total).astype(BF16).astype(F32)
+    mask = (
+        lax.broadcasted_iota(jnp.int32, (BLOCK_ROWS, block), 0)
+        == lax.broadcasted_iota(jnp.int32, (BLOCK_ROWS, block), 1) // OBS
+    )
+    spread = jnp.concatenate(
+        [jnp.where(mask, attention[i : i + 1], 0.0) for i in range(2 * H)], axis=0
+    ).astype(BF16)
+    start = pl.multiple_of(place_ref[1] * half, half)
+    pooled = dot_nn(spread, tokens_ref[:, pl.ds(start, half)])
+    out_ref[...] = pooled.astype(BF16).reshape(2, H, BLOCK_ROWS, half)
+
+
+def pooled_tokens(place, tokens, query_weight, query_prior):
+    count, depth = tokens.shape
+    half = depth // PAIR
+    block = BLOCK_ROWS * OBS
+    return pl.pallas_call(
+        pool_kernel,
+        grid_spec=pltpu.PrefetchScalarGridSpec(
+            num_scalar_prefetch=1,
+            grid=(count // block,),
+            in_specs=[
+                pl.BlockSpec((block, depth), lambda i, s: (i, 0)),
+                pl.BlockSpec(query_weight.shape, lambda i, s: (0, 0, 0)),
+                pl.BlockSpec(query_prior.shape, lambda i, s: (0, 0, 0)),
+            ],
+            out_specs=pl.BlockSpec((2, H, BLOCK_ROWS, half), lambda i, s: (0, 0, i, 0)),
+        ),
+        out_shape=jax.ShapeDtypeStruct((2, H, count // OBS, half), BF16),
+        compiler_params=pltpu.CompilerParams(vmem_limit_bytes=VMEM_BYTES),
+        cost_estimate=pl.CostEstimate(
+            flops=2 * count * depth * 2 * H + 4 * count * H * BLOCK_ROWS * half,
+            bytes_accessed=2 * count * depth + 2 * count * half,
+            transcendentals=4 * count * H,
+        ),
+    )(place, tokens, query_weight, query_prior)
+
+
+def finish_raw(top, rest):
+    rest = rest[:8] + rest[8:]
+    rest = rest + jnp.concatenate([rest[4:], rest[:4]], axis=0)
+    return jnp.concatenate([top, rest], axis=0)
+
+
+def raw_sums(tables, own_ref, peer_ref):
+    rows = 2 * own_ref.shape[2]
+    top = jnp.zeros((TOP, rows), F32)
+    rest = jnp.zeros((TOP, rows), F32)
+    place = lax.broadcasted_iota(jnp.int32, (TOP, rows), 0) // 4
+    for h in range(H):
+        left = []
+        for table in tables:
+            left += [table[h * TOP : (h + 1) * TOP], table[H * TOP + h // 4 * TOP :][:TOP]]
+        pooled = jnp.concatenate([own_ref[0, h], peer_ref[0, h]], axis=0)
+        result = dot_nt(jnp.concatenate(left, axis=0), pooled)
+        for i in range(len(tables)):
+            top = top + result[2 * i * TOP :][:TOP]
+            rest = rest + jnp.where(place == h % 4, result[(2 * i + 1) * TOP :][:TOP], 0.0)
+    return top, rest
+
+
+def own_kernel(level_ref, head_ref, proj_ref, own_ref, peer_ref, out_ref, spread_ref, sum_ref):
+    step = pl.program_id(0)
+
+    @pl.when(step == 0)
+    def _():
+        build_spread(level_ref[0], head_ref, spread_ref)
+        sum_ref[...] = jnp.zeros_like(sum_ref)
+
+    tables = split_high(folded(spread_ref, proj_ref[...]))
+    top, rest = raw_sums(tables, own_ref, peer_ref)
+    sum_ref[:TOP] += top
+    sum_ref[TOP:] += rest
+
+    @pl.when(step == pl.num_programs(0) - 1)
+    def _():
+        out_ref[...] = finish_raw(sum_ref[:TOP], sum_ref[TOP:])
+
+
+def own_raw(level, head_t, proj, own_pool, peer_pool, chunk):
+    depth, width = proj.shape
+    rows = own_pool.shape[2]
+    pool_spec = pl.BlockSpec((1, H, rows, chunk), lambda i, s: (0, 0, 0, i))
+    return pl.pallas_call(
+        own_kernel,
+        grid_spec=pltpu.PrefetchScalarGridSpec(
+            num_scalar_prefetch=1,
+            grid=(depth // chunk,),
+            in_specs=[
+                pl.BlockSpec(head_t.shape, lambda i, s: (0, 0, 0)),
+                pl.BlockSpec((chunk, width), lambda i, s: (i, 0)),
+                pool_spec,
+                pool_spec,
+            ],
+            out_specs=pl.BlockSpec((24, 2 * rows), lambda i, s: (0, 0)),
+            scratch_shapes=[
+                pltpu.VMEM((2 * SPREAD, width), BF16),
+                pltpu.VMEM((2 * TOP, 2 * rows), F32),
+            ],
+        ),
+        out_shape=jax.ShapeDtypeStruct((24, 2 * rows), F32),
+        compiler_params=pltpu.CompilerParams(vmem_limit_bytes=VMEM_BYTES),
+        cost_estimate=pl.CostEstimate(
+            flops=4 * SPREAD * depth * width, bytes_accessed=4 * depth * width, transcendentals=0
+        ),
+    )(level, head_t, proj, own_pool, peer_pool)
+
+
+def lower_kernel(table_ref, own_ref, peer_ref, raw_ref, legal_ref, label_ref, out_ref):
+    rows = own_ref.shape[2]
+    out_ref[:24] = raw_ref[...]
+    top, rest = raw_sums([table_ref[...]], own_ref, peer_ref)
+    out_ref[24:48] = finish_raw(top, rest)
+    out_ref[48:72] = jnp.zeros((24, 2 * rows), F32)
+    out_ref[48 : 48 + A, :rows] = legal_ref[...].astype(F32)
+    out_ref[48 + A : 49 + A, :rows] = label_ref[...].astype(F32)
+
+
+def lower_raw(table, own_pool, peer_pool, raw, legal_t, label):
+    _, _, rows, half = own_pool.shape
+    pool_spec = pl.BlockSpec((1, H, rows, half), lambda i: (1, 0, 0, 0))
+
+    def whole(array):
+        return pl.BlockSpec(array.shape, lambda i: (0, 0))
+
+    return pl.pallas_call(
+        lower_kernel,
+        grid=(1,),
+        in_specs=[whole(table), pool_spec, pool_spec, whole(raw), whole(legal_t), whole(label)],
+        out_specs=pl.BlockSpec((72, 2 * rows), lambda i: (0, 0)),
+        out_shape=jax.ShapeDtypeStruct((72, 2 * rows), F32),
+        compiler_params=pltpu.CompilerParams(vmem_limit_bytes=VMEM_BYTES),
+        cost_estimate=pl.CostEstimate(
+            flops=8 * TOP * rows * H * half, bytes_accessed=4 * rows * H * half, transcendentals=0
+        ),
+    )(table, own_pool, peer_pool, raw, legal_t, label)
+
+
+def policy_rows(raw, legal):
+    logits = 30.0 * jnp.tanh(raw / 30.0)
+    exp_logits = jnp.exp(logits) * legal
+    partition = jnp.sum(exp_logits, axis=0, keepdims=True)
+    return logits, exp_logits / partition, logits - jnp.log(partition)
+
+
+def grad_kernel(level_ref, mine_ref, theirs_ref, head_ref, own_ref, peer_ref, out_ref, loss_ref, diag_ref):
+    rows = own_ref.shape[2]
+
+    @pl.when(pl.program_id(0) == 0)
+    def _():
+        level = level_ref[0]
+        theirs = theirs_ref[:48]
+        theirs = jnp.concatenate([theirs[:, rows:], theirs[:, :rows]], axis=1)
+        raw = mine_ref[:48] + theirs
+        told = jnp.concatenate([mine_ref[48:72, :rows], theirs_ref[48:72, :rows]], axis=1)
+        move = lax.broadcasted_iota(jnp.int32, told.shape, 0)
+        legal = jnp.where(move < A, told, 0.0)
+        onehot = (move.astype(F32) == told[A : A + 1]).astype(F32)
+        logits, policy, log_policy = policy_rows(raw[:24], legal)
+        _, lower_policy, _ = policy_rows(raw[24:], legal)
+        uniform = legal / jnp.sum(legal, axis=0, keepdims=True)
+        partner = jnp.where(level == 0, uniform, lower_policy)
+        target = 0.5 * onehot + 0.5 * partner
+        loss = -jnp.sum(target * log_policy, axis=0, keepdims=True)
+        loss_ref[...] = loss[:, :rows]
+        logit_grad = (policy - target) * (1.0 - (logits / 30.0) ** 2)
+        head = head_ref[:, pl.ds(level, 1), :].reshape(A, H * DH)
+        head = jnp.concatenate([head, jnp.zeros((24 - A, H * DH), F32)], axis=0)
+        pooled_grad = dot_tn(logit_grad, head, lax.Precision.HIGHEST).astype(BF16)
+        diag_ref[...] = jnp.zeros_like(diag_ref)
+        for h in range(H):
+            at = h % 2
+            diag_ref[h // 2, at * 2 * rows : (at + 1) * 2 * rows, at * DH : (at + 1) * DH] = (
+                pooled_grad[:, h * DH : (h + 1) * DH]
+            )
+
+    for pair in range(H // 2):
+        pooled = jnp.concatenate(
+            [own_ref[0, 2 * pair], peer_ref[0, 2 * pair], own_ref[0, 2 * pair + 1], peer_ref[0, 2 * pair + 1]],
+            axis=0,
+        )
+        out_ref[:, pair * 2 * DH : (pair + 1) * 2 * DH] = dot_tn(pooled, diag_ref[pair])
+
+
+def gradient(level, mine, theirs, head_t, own_pool, peer_pool, chunk):
+    _, _, rows, half = own_pool.shape
+    width = H * DH
+    pool_spec = pl.BlockSpec((1, H, rows, chunk), lambda i, s: (0, 0, 0, i))
+    return pl.pallas_call(
+        grad_kernel,
+        grid_spec=pltpu.PrefetchScalarGridSpec(
+            num_scalar_prefetch=1,
+            grid=(half // chunk,),
+            in_specs=[
+                pl.BlockSpec(mine.shape, lambda i, s: (0, 0)),
+                pl.BlockSpec(theirs.shape, lambda i, s: (0, 0)),
+                pl.BlockSpec(head_t.shape, lambda i, s: (0, 0, 0)),
+                pool_spec,
+                pool_spec,
+            ],
+            out_specs=[
+                pl.BlockSpec((chunk, width), lambda i, s: (i, 0)),
+                pl.BlockSpec((1, rows), lambda i, s: (0, 0)),
+            ],
+            scratch_shapes=[pltpu.VMEM((H // 2, 4 * rows, 2 * DH), BF16)],
+        ),
+        out_shape=[
+            jax.ShapeDtypeStruct((half, width), F32),
+            jax.ShapeDtypeStruct((1, rows), F32),
+        ],
+        compiler_params=pltpu.CompilerParams(vmem_limit_bytes=VMEM_BYTES),
+        cost_estimate=pl.CostEstimate(
+            flops=8 * rows * half * width // 2,
+            bytes_accessed=4 * half * width + 4 * rows * H * half,
+            transcendentals=0,
+        ),
+    )(level, mine, theirs, head_t, own_pool, peer_pool)
+
+
+def paired_device(
+    tokens, legal_moves, action_label, value_weight, value_prior,
+    query_weight, query_prior, policy_head, head_prior,
+):
+    device_place = lax.axis_index("dp")
+    place = jnp.stack([device_place // PAIR, device_place % PAIR]).astype(jnp.int32)
+    peer_tokens = partner_2(tokens, "dp", 0)
+    head_t = jnp.transpose(policy_head, (1, 0, 2))
+    prior_t = jnp.transpose(head_prior, (1, 0, 2))
+    prior_map = prior_map_of(place, prior_t, value_prior, 256)
+    lower_map = shifted(prior_map, "dp", PAIR)
+    own_pool = pooled_tokens(place, tokens, query_weight, query_prior)
+    peer_pool = pooled_tokens(place, peer_tokens, query_weight, query_prior)
+    raw = own_raw(place, head_t, value_weight, own_pool, peer_pool, 256)
+    mine = lower_raw(
+        lower_map, own_pool, peer_pool, raw, legal_moves.T, action_label.reshape(1, -1)
+    )
+    theirs = partner_2(mine, "dp", 0)
+    weight_grad, row_loss = gradient(place, mine, theirs, head_t, own_pool, peer_pool, 256)
+    return weight_grad, row_loss.reshape(-1)
+
+
 def solution(mesh):
+    paired = mesh.shape["dp"] == LEVELS * PAIR
     return jax.shard_map(
-        general_device,
+        paired_device if paired else general_device,
         mesh=mesh,
         in_specs=(
             P(("groups", "dp"), None),

time: 74.8 us -> 37.3 us (0.50)
  matrix products: 26.2 us -> 0 us
  Pallas kernels: 0 us -> 25.8 us
  local copies, waits for them, and re-layouts: 26.1 us -> 4.02 us
  other arithmetic: 13.2 us -> 0.07 us
  starting transfers between devices: 6.22 us -> 5.23 us
    dot_general x8 -> x0, matrix products: 26.2 us -> none  [the longest x2 6.83 us: attention_of(): lax.dot_general(tokens, query_proj, (((1,), (1,)), ((), ())), preferred_e...]
    pallas_call x0 -> x6, Pallas kernels: none -> 25.8 us  [the longest x2 13 us: pooled_tokens(): pl.pallas_call(pool_kernel, grid_spec=pltpu.PrefetchScalarGridSpec(num_sc...]
    reshape x3 -> x0, local copies, waits for them, and re-layouts: 7.96 us -> none  [the longest x2 7.89 us: policy_of(): moved = lax.dot_general(tokens, mapped, (((1,), (1,)), ((), ())), preferr...]
    convert_element_type x5 -> x0, local copies, waits for them, and re-layouts: 7.16 us -> none  [the longest x2 3.19 us: attention_of(): return attention.astype(jnp.bfloat16).astype(jnp.float32)]
    reduce_sum x4 -> x0, other arithmetic: 6.29 us -> none  [the longest x2 5.93 us: policy_of(): raw_logits = jnp.sum(attention[..., None] * moved, axis=(1, 2))]
    div x2 -> x0, other arithmetic: 2.74 us -> none  [attention_of(): attention = exp_scores / jnp.sum(exp_scores, axis=1, keepdims=True)]
    dot_general x2 -> x0, local copies, waits for them, and re-layouts: 2.66 us -> none  [policy_of(): lax.dot_general(tokens, mapped, (((1,), (1,)), ((), ())), preferred_eleme...]
    convert_element_type x1 -> x0, other arithmetic: 2.21 us -> none  [general_device(): token_grad = token_grad.astype(jnp.bfloat16).reshape(tokens.shape[0], H * A)]
  transfers between devices with their start and end apart: 4 -> 3, of which waited for: 1 -> 1; matrix products, arithmetic and copies ran while one was open for 40% -> 0% of each run, Pallas kernels for 0% -> 56%
where the time goes in v2:
time: 37.3 us; the launch traced here: 36.9 us
  Pallas kernels  25.8 us (69%)
  starting transfers between devices  5.23 us (14%)
  local copies, waits for them, and re-layouts  4.02 us (11%)
  waiting for transfers between devices  1.05 us (3%)
  between operations  0.78 us (2%)
    pallas_call x2, Pallas kernels, pooled_tokens(): pl.pallas_call(pool_kernel, grid_spec=pltpu.PrefetchScalarGridSpec(num_sc...  13 us
    pallas_call x1, Pallas kernels, own_raw(): pl.pallas_call(own_kernel, grid_spec=pltpu.PrefetchScalarGridSpec(num_sca...  5.26 us
    pallas_call x1, Pallas kernels, gradient(): pl.pallas_call(grad_kernel, grid_spec=pltpu.PrefetchScalarGridSpec(num_sc...  4.51 us
    ppermute x1, starting transfers between devices, shifted(): return lax.ppermute(block, axis, route)  4.48 us
    unnamed x20, local copies, waits for them, and re-layouts  4.02 us
    pallas_call x1, Pallas kernels, prior_map_of(): pl.pallas_call(map_kernel, grid_spec=pltpu.PrefetchScalarGridSpec(num_sca...  2.22 us
    ppermute x2, waiting for transfers between devices, partner_2(): return lax.ppermute(block, axis, route)  1.04 us
    pallas_call x1, Pallas kernels, lower_raw(): pl.pallas_call(lower_kernel, grid=(1,), in_specs=[whole(table), pool_spec...  0.8 us
  transfers between devices with their start and end apart: 3, of which 1 were waited for; matrix products, arithmetic and copies ran while one was open for 0% of the time, Pallas kernels for 56%

profile of v2, /device:TPU:0, one launch (start us, length us, event | category | flops | bytes accessed | tf_op | source)
XLA Modules:
  0.0 36.9 jit_solution(6336638043548259320)
XLA Ops:
  0.6 0.5 %collective-permute-start.1 = (bf16[1024,2048]{1,0:T(8,128)(2,1)}, bf16[1024,2048]{1,0:T(8,128)(2,1)}, u32[]{:S(2)}, u32[]{:S(2)}) collective-permute-start(bf16[1024,2048]{1,0:T(8,128)(2,1)} %tokens_ref.1), channel_id=1, source_target_pairs={{0,1},{1,0},{2,3},{3,2},{4,5},{5,4},{6,7},{7,6},{8,9},{9,8},{10,11... | collective-permute-start | bytes 12582920 | tf_op jit(solution)/shard_map/ppermute | solution.py:23
  1.1 0.1 pad_add_fusion.level_ref.place_ref
  1.2 1.6 %copy-done.3 = bf16[1024,1024]{1,0:T(8,128)(2,1)S(1)} copy-done((bf16[1024,1024]{1,0:T(8,128)(2,1)S(1)}, bf16[1024,1024]{1,0:T(8,128)(2,1)}, u32[]{:S(2)}) %copy-start.3) | copy-done | bytes 2097176
  2.8 1.1 %copy-done.7 = f32[8,20,1024]{2,0,1:T(8,128)S(1)} copy-done((f32[8,20,1024]{2,0,1:T(8,128)S(1)}, f32[8,20,1024]{2,0,1:T(8,128)}, u32[]{:S(2)}) %copy-start.7) | copy-done | bytes 655384
  3.9 2.2 %shard_map.104 = bf16[160,1024]{1,0:T(8,128)(2,1)S(1)} custom-call(s32[2]{0:T(128)S(1)} %pad_add_fusion.level_ref.place_ref, f32[20,8,1024]{2,1,0:T(8,128)S(1)} %bitcast.9, bf16[1024,1024]{1,0:T(8,128)(2,1)S(1)} %copy-done.3), custom_call_target="tpu_custom_call" | custom-call | flops 671088640 | bytes 2097152 | tf_op jit(solution)/shard_map/pallas_call | solution.py:193
  6.1 4.5 %collective-permute-start = (bf16[160,1024]{1,0:T(8,128)(2,1)S(1)}, bf16[160,1024]{1,0:T(8,128)(2,1)S(1)}, u32[]{:S(2)}, u32[]{:S(2)}) collective-permute-start(bf16[160,1024]{1,0:T(8,128)(2,1)S(1)} %shard_map.104), channel_id=1, source_target_pairs={{0,2},{1,3},{2,4},{3,5},{4,6},{5,7},{6,8},{7,9},{8,10},{9,11},{10,... | collective-permute-start | bytes 983048 | tf_op jit(solution)/shard_map/ppermute | solution.py:29
  10.6 0.0 copy-done.5
  10.6 0.0 copy-done.6
  10.6 6.4 %shard_map.105.own_ref = bf16[2,8,64,1024]{3,2,1,0:T(8,128)(2,1)S(1)} custom-call(s32[2]{0:T(128)S(1)} %pad_add_fusion.level_ref.place_ref, bf16[1024,2048]{1,0:T(8,128)(2,1)} %tokens_ref.1, bf16[8,8,2048]{2,1,0:T(8,128)(2,1)S(1)} %copy-done.5, bf16[8,8,2048]{2,1,0:T(8,128)(2,1)S(1)} %copy-done.6), custom_call_target="tpu_custom_call" | custom-call | flops 603979776 | bytes 6291456 | tf_op jit(solution)/shard_map/pallas_call | solution.py:247
  17.0 0.0 copy-start.2
  17.0 0.0 copy-start.4
  17.1 0.0 collective-permute-done.1.tokens_ref
  17.1 6.6 %shard_map.106.peer_ref = bf16[2,8,64,1024]{3,2,1,0:T(8,128)(2,1)S(1)} custom-call(s32[2]{0:T(128)S(1)} %pad_add_fusion.level_ref.place_ref, bf16[1024,2048]{1,0:T(8,128)(2,1)} %collective-permute-done.1.tokens_ref, bf16[8,8,2048]{2,1,0:T(8,128)(2,1)S(1)} %copy-done.5, bf16[8,8,2048]{2,1,0:T(8,128)(2,1)S(1)} %copy-done.6), custom_call_target="tpu_custom_call" | custom-call | flops 603979776 | bytes 6291456 | tf_op jit(solution)/shard_map/pallas_call | solution.py:247
  23.7 0.0 copy-start
  23.7 1.3 %copy-done = bf16[2,8,64,1024]{3,2,1,0:T(8,128)(2,1)} copy-done((bf16[2,8,64,1024]{3,2,1,0:T(8,128)(2,1)}, bf16[2,8,64,1024]{3,2,1,0:T(8,128)(2,1)S(1)}, u32[]{:S(2)}) %copy-start) | copy-done | bytes 2097176
  25.0 0.0 copy-done.2
  25.0 0.0 copy-done.4
  25.0 0.0 copy-start.9
  25.0 5.3 %shard_map.107.raw_ref = f32[24,128]{1,0:T(8,128)S(1)} custom-call(s32[2]{0:T(128)S(1)} %pad_add_fusion.level_ref.place_ref, f32[20,8,1024]{2,1,0:T(8,128)S(1)} %bitcast.7, bf16[1024,1024]{1,0:T(8,128)(2,1)S(1)} %copy-done.4, bf16[2,8,64,1024]{3,2,1,0:T(8,128)(2,1)S(1)} %shard_map.105.own_ref, bf16[2,8,64,1024]{3,2,1,0:T(8,128)(2,1)} %copy-done), custom_call_target="tpu_custom_call" | custom-call | flops 671088640 | bytes 4194304 | tf_op jit(solution)/shard_map/pallas_call | solution.py:314
  30.3 0.0 collective-permute-done.table_ref
  30.4 0.8 %shard_map.108.mine_ref = f32[72,128]{1,0:T(8,128)S(1)} custom-call(bf16[160,1024]{1,0:T(8,128)(2,1)S(1)} %collective-permute-done.table_ref, bf16[2,8,64,1024]{3,2,1,0:T(8,128)(2,1)S(1)} %shard_map.105.own_ref, bf16[2,8,64,1024]{3,2,1,0:T(8,128)(2,1)S(1)} %copy-done.1, f32[24,128]{1,0:T(8,128)S(1)} %shard_map.107.raw_ref, s32[20,64]{1,0:T(8,128)S(1)} %bitcast.10, ...), custom_call_target="tpu_custom_call" | custom-call | flops 67108864 | bytes 2097152 | tf_op jit(solution)/shard_map/pallas_call | solution.py:356
  31.2 0.2 collective-permute-start.2
  31.4 1.0 %collective-permute-done.2.theirs_ref = f32[72,128]{1,0:T(8,128)S(1)} collective-permute-done((f32[72,128]{1,0:T(8,128)S(1)}, f32[72,128]{1,0:T(8,128)S(1)}, u32[]{:S(2)}, u32[]{:S(2)}) %collective-permute-start.2) | collective-permute-done | bytes 36896 | tf_op jit(solution)/shard_map/ppermute | solution.py:23
  32.4 4.5 %shard_map.109 = (f32[1024,1024]{1,0:T(8,128)}, f32[1,64]{1,0:T(1,128)}) custom-call(s32[2]{0:T(128)S(1)} %pad_add_fusion.level_ref.place_ref, f32[72,128]{1,0:T(8,128)S(1)} %shard_map.108.mine_ref, f32[72,128]{1,0:T(8,128)S(1)} %collective-permute-done.2.theirs_ref, f32[20,8,1024]{2,1,0:T(8,128)S(1)} %bitcast.8, ...), custom_call_target="tpu_custom_call" | custom-call | flops 268435456 | bytes 6291456 | tf_op jit(solution)/shard_map/pallas_call | solution.py:419
  (9 shorter events, 0.0 us)
Async XLA Ops:
  0.6 16.4 %collective-permute-start.1 = (bf16[1024,2048]{1,0:T(8,128)(2,1)}, bf16[1024,2048]{1,0:T(8,128)(2,1)}, u32[]{:S(2)}, u32[]{:S(2)}) collective-permute-start(bf16[1024,2048]{1,0:T(8,128)(2,1)} %tokens_ref.1), channel_id=1, source_target_pairs={{0,1},{1,0},{2,3},{3,2},{4,5},{5,4},{6,7},{7,6},{8,9},{9,8},{10,11... | collective-permute-start | bytes 12582920 | tf_op jit(solution)/shard_map/ppermute | solution.py:23
  1.2 1.6 %copy-start.3 = (bf16[1024,1024]{1,0:T(8,128)(2,1)S(1)}, bf16[1024,1024]{1,0:T(8,128)(2,1)}, u32[]{:S(2)}) copy-start(bf16[1024,1024]{1,0:T(8,128)(2,1)} %proj_ref.2) | copy-start | bytes 6291460
  2.8 1.1 %copy-start.7 = (f32[8,20,1024]{2,0,1:T(8,128)S(1)}, f32[8,20,1024]{2,0,1:T(8,128)}, u32[]{:S(2)}) copy-start(f32[8,20,1024]{2,0,1:T(8,128)} %param.17) | copy-start | bytes 1966084
  3.9 6.7 %copy-start.5 = (bf16[8,8,2048]{2,1,0:T(8,128)(2,1)S(1)}, bf16[8,8,2048]{2,1,0:T(8,128)(2,1)}, u32[]{:S(2)}) copy-start(bf16[8,8,2048]{2,1,0:T(8,128)(2,1)} %query_ref.3) | copy-start | bytes 786436
  3.9 6.7 %copy-start.6 = (bf16[8,8,2048]{2,1,0:T(8,128)(2,1)S(1)}, bf16[8,8,2048]{2,1,0:T(8,128)(2,1)}, u32[]{:S(2)}) copy-start(bf16[8,8,2048]{2,1,0:T(8,128)(2,1)} %prior_ref.3) | copy-start | bytes 786436
  6.1 24.2 %collective-permute-start = (bf16[160,1024]{1,0:T(8,128)(2,1)S(1)}, bf16[160,1024]{1,0:T(8,128)(2,1)S(1)}, u32[]{:S(2)}, u32[]{:S(2)}) collective-permute-start(bf16[160,1024]{1,0:T(8,128)(2,1)S(1)} %shard_map.104), channel_id=1, source_target_pairs={{0,2},{1,3},{2,4},{3,5},{4,6},{5,7},{6,8},{7,9},{8,10},{9,11},{10,... | collective-permute-start | bytes 983048 | tf_op jit(solution)/shard_map/ppermute | solution.py:29
  17.0 8.0 %copy-start.2 = (f32[8,20,1024]{2,0,1:T(8,128)S(1)}, f32[8,20,1024]{2,0,1:T(8,128)}, u32[]{:S(2)}) copy-start(f32[8,20,1024]{2,0,1:T(8,128)} %param.16) | copy-start | bytes 1966084
  17.0 8.0 %copy-start.4 = (bf16[1024,1024]{1,0:T(8,128)(2,1)S(1)}, bf16[1024,1024]{1,0:T(8,128)(2,1)}, u32[]{:S(2)}) copy-start(bf16[1024,1024]{1,0:T(8,128)(2,1)} %proj_ref.3) | copy-start | bytes 6291460
  23.7 1.3 %copy-start = (bf16[2,8,64,1024]{3,2,1,0:T(8,128)(2,1)}, bf16[2,8,64,1024]{3,2,1,0:T(8,128)(2,1)S(1)}, u32[]{:S(2)}) copy-start(bf16[2,8,64,1024]{3,2,1,0:T(8,128)(2,1)S(1)} %shard_map.106.peer_ref) | copy-start | bytes 6291460
  25.0 5.3 %copy-start.1 = (bf16[2,8,64,1024]{3,2,1,0:T(8,128)(2,1)S(1)}, bf16[2,8,64,1024]{3,2,1,0:T(8,128)(2,1)}, u32[]{:S(2)}) copy-start(bf16[2,8,64,1024]{3,2,1,0:T(8,128)(2,1)} %copy-done) | copy-start | bytes 6291460
  25.0 5.3 %copy-start.8 = (s32[64,20]{0,1:T(8,128)S(1)}, s32[64,20]{0,1:T(8,128)}, u32[]{:S(2)}) copy-start(s32[64,20]{0,1:T(8,128)} %param.10) | copy-start | bytes 15364
  25.0 5.3 %copy-start.9 = (s32[64]{0:T(128)S(1)}, s32[64]{0:T(128)}, u32[]{:S(2)}) copy-start(s32[64]{0:T(128)} %param.11) | copy-start | bytes 772
  31.2 1.3 %collective-permute-start.2 = (f32[72,128]{1,0:T(8,128)S(1)}, f32[72,128]{1,0:T(8,128)S(1)}, u32[]{:S(2)}, u32[]{:S(2)}) collective-permute-start(f32[72,128]{1,0:T(8,128)S(1)} %shard_map.108.mine_ref), channel_id=1, source_target_pairs={{0,1},{1,0},{2,3},{3,2},{4,5},{5,4},{6,7},{7,6},{8,9},{9,8},{10,11... | collective-permute-start | bytes 110600 | tf_op jit(solution)/shard_map/ppermute | solution.py:23

commit v3 on v1

--- a/solution.py
+++ b/solution.py
@@ -1,6 +1,8 @@
 import jax
 import jax.numpy as jnp
 from jax import lax
+from jax.experimental import pallas as pl
+from jax.experimental.pallas import tpu as pltpu
 from jax.sharding import PartitionSpec as P
 
 H = 8
@@ -121,9 +123,387 @@
     return weight_grad.reshape(-1, H * DH), row_loss
 
 
+PAIR = 2
+TOP = 16
+SPREAD = H * A
+BLOCK_ROWS = 16
+F32 = jnp.float32
+BF16 = jnp.bfloat16
+PAD = 24
+CHUNKS = 4
+GRAD_CHUNKS = 4
+DH_BITS = 7
+OBS_BITS = 4
+MIB = 2**20
+PRIOR_MIB = 54
+OWN_MIB = 48
+PEER_MIB = 40
+
+
+def dot_nt(left, right):
+    return lax.dot_general(left, right, (((1,), (1,)), ((), ())), preferred_element_type=F32)
+
+
+def dot_nn(left, right):
+    return lax.dot_general(left, right, (((1,), (0,)), ((), ())), preferred_element_type=F32)
+
+
+def dot_tn(left, right):
+    return lax.dot_general(
+        left, right, (((0,), (0,)), ((), ())), preferred_element_type=F32
+    )
+
+
+def split_high(value):
+    high = value.astype(BF16)
+    return high, (value - high.astype(F32)).astype(BF16)
+
+
+def spread_heads(rows):
+    width = rows.shape[1]
+    top = rows[:TOP]
+    lane_head = lax.broadcasted_iota(jnp.int32, (TOP, width), 1) >> DH_BITS
+    pieces = [jnp.where(lane_head == h, top, 0.0) for h in range(H)]
+    rest = rows[TOP:A]
+    rest = jnp.concatenate([rest, rest], axis=0)
+    lane_head = lax.broadcasted_iota(jnp.int32, (8, width), 1) >> DH_BITS
+    upper = lax.broadcasted_iota(jnp.int32, (8, width), 0) >> 2
+    pieces += [jnp.where(lane_head == 2 * i + upper, rest, 0.0) for i in range(H // 2)]
+    return jnp.concatenate(pieces, axis=0)
+
+
+def chunk_copies(source_ref, target_ref, sems, first):
+    chunk = source_ref.shape[0] // CHUNKS
+    copies = []
+    for i in range(CHUNKS):
+        rows = pl.ds(i * chunk, chunk)
+        copies.append(
+            pltpu.make_async_copy(source_ref.at[rows], target_ref.at[rows], sems.at[first + i])
+        )
+    return copies
+
+
+def spread_into(spread_ref, head_buf, level):
+    head = head_buf[:, pl.ds(level, 1), :].reshape(A, H * DH)
+    high, low = split_high(spread_heads(head))
+    spread_ref[:SPREAD, :] = high
+    spread_ref[SPREAD:, :] = low
+    return head
+
+
+def fold_into(out_ref, proj_buf, spread_ref, parts):
+    product = dot_nt(spread_ref[...], proj_buf[...])
+    product = product[:SPREAD] + product[SPREAD:]
+    if parts == 1:
+        out_ref[...] = product.astype(BF16)
+    else:
+        high, low = split_high(product)
+        out_ref[:SPREAD] = high
+        out_ref[SPREAD:] = low
+
+
+def prior_kernel(head_ref, proj_ref, out_ref, head_buf, proj_buf, spread_ref, sems):
+    head_copy = pltpu.make_async_copy(head_ref, head_buf, sems.at[CHUNKS])
+    head_copy.start()
+    copies = chunk_copies(proj_ref, proj_buf, sems, 0)
+    for copy in copies:
+        copy.start()
+    head_copy.wait()
+    spread_into(spread_ref, head_buf, lax.axis_index("dp") // PAIR)
+    for copy in copies:
+        copy.wait()
+    fold_into(out_ref, proj_buf, spread_ref, 1)
+
+
+IN_HBM = pl.BlockSpec(memory_space=pltpu.HBM)
+IN_VMEM = pl.BlockSpec(memory_space=pltpu.VMEM)
+
+
+def prior_fold(head_t, proj):
+    depth, width = proj.shape
+    return pl.pallas_call(
+        prior_kernel,
+        in_specs=[IN_HBM, IN_HBM],
+        out_specs=IN_VMEM,
+        out_shape=jax.ShapeDtypeStruct((SPREAD, depth), BF16),
+        scratch_shapes=[
+            pltpu.VMEM(head_t.shape, F32),
+            pltpu.VMEM(proj.shape, BF16),
+            pltpu.VMEM((2 * SPREAD, width), BF16),
+            pltpu.SemaphoreType.DMA((CHUNKS + 1,)),
+        ],
+        compiler_params=pltpu.CompilerParams(vmem_limit_bytes=PRIOR_MIB * MIB),
+        cost_estimate=pl.CostEstimate(
+            flops=4 * SPREAD * depth * width, bytes_accessed=2 * depth * width, transcendentals=0
+        ),
+    )(head_t, proj)
+
+
+def pool_into(out_ref, tokens_ref, copies, query_ref, prior_ref):
+    count = tokens_ref.shape[0]
+    half = out_ref.shape[3]
+    block = BLOCK_ROWS * OBS
+    blocks = count // block
+    device_place = lax.axis_index("dp")
+    level = device_place // PAIR
+    lower = jnp.maximum(level - 1, 0)
+    queries = jnp.concatenate(
+        [query_ref[level].astype(F32), prior_ref[lower].astype(F32)], axis=0
+    ).astype(BF16)
+    row_of = lax.broadcasted_iota(jnp.int32, (block, block), 0) >> OBS_BITS
+    column_of = lax.broadcasted_iota(jnp.int32, (block, block), 1) >> OBS_BITS
+    same_row = (row_of == column_of).astype(F32).astype(BF16)
+    mask = (
+        lax.broadcasted_iota(jnp.int32, (BLOCK_ROWS, block), 0)
+        == lax.broadcasted_iota(jnp.int32, (BLOCK_ROWS, block), 1) >> OBS_BITS
+    )
+    start = pl.multiple_of(device_place % PAIR * half, half)
+    scores = []
+    for step in range(blocks // 2):
+        for copy in copies[2 * step : 2 * step + 2]:
+            copy.wait()
+        two = dot_nt(queries, tokens_ref[2 * step * block : 2 * (step + 1) * block])
+        scores += [two[:, :block], two[:, block:]]
+    exp_scores = jnp.exp(5.0 * jnp.tanh(jnp.concatenate(scores, axis=0) / 5.0))
+    first, rest = split_high(exp_scores)
+    second, third = split_high(exp_scores - first.astype(F32))
+    parts = dot_nn(jnp.concatenate([first, second, third], axis=0), same_row)
+    rows = 2 * H * blocks
+    total = parts[:rows] + parts[rows : 2 * rows] + parts[2 * rows :]
+    attention = (exp_scores / total).astype(BF16).astype(F32)
+    for i in range(blocks):
+        at = 2 * H * i
+        spread = jnp.concatenate(
+            [jnp.where(mask, attention[at + j : at + j + 1], 0.0) for j in range(2 * H)], axis=0
+        ).astype(BF16)
+        pooled = dot_nn(spread, tokens_ref[i * block : (i + 1) * block, pl.ds(start, half)])
+        out_ref[:, :, i * BLOCK_ROWS : (i + 1) * BLOCK_ROWS, :] = pooled.astype(BF16).reshape(
+            2, H, BLOCK_ROWS, half
+        )
+
+
+def own_kernel(
+    tokens_ref, query_ref, prior_ref, head_ref, proj_ref,
+    pool_ref, map_ref, wide_ref, tokens_buf, head_buf, proj_buf, spread_ref, sems,
+):
+    token_copies = chunk_copies(tokens_ref, tokens_buf, sems, 0)
+    proj_copies = chunk_copies(proj_ref, proj_buf, sems, CHUNKS)
+    head_copy = pltpu.make_async_copy(head_ref, head_buf, sems.at[2 * CHUNKS])
+    for copy in [head_copy] + proj_copies + token_copies:
+        copy.start()
+    head_copy.wait()
+    head = spread_into(spread_ref, head_buf, lax.axis_index("dp") // PAIR)
+    for copy in proj_copies:
+        copy.wait()
+    fold_into(map_ref, proj_buf, spread_ref, 2)
+    head = jnp.concatenate([head, jnp.zeros((PAD - A, H * DH), F32)], axis=0)
+    lane_head = lax.broadcasted_iota(jnp.int32, (PAD, H * DH), 1) >> DH_BITS
+    wide = [jnp.where(lane_head == h, head, 0.0) for h in range(H)]
+    wide_ref[...] = jnp.concatenate(wide, axis=0).astype(BF16)
+    pool_into(pool_ref, tokens_buf, token_copies, query_ref, prior_ref)
+
+
+def own_side(tokens, query_weight, query_prior, head_t, proj):
+    count, width = tokens.shape
+    half = proj.shape[0]
+    return pl.pallas_call(
+        own_kernel,
+        in_specs=[IN_HBM, IN_VMEM, IN_VMEM, IN_HBM, IN_HBM],
+        out_specs=[IN_VMEM] * 3,
+        out_shape=[
+            jax.ShapeDtypeStruct((2, H, count // OBS, half), BF16),
+            jax.ShapeDtypeStruct((2 * SPREAD, half), BF16),
+            jax.ShapeDtypeStruct((H * PAD, H * DH), BF16),
+        ],
+        scratch_shapes=[
+            pltpu.VMEM(tokens.shape, BF16),
+            pltpu.VMEM(head_t.shape, F32),
+            pltpu.VMEM(proj.shape, BF16),
+            pltpu.VMEM((2 * SPREAD, H * DH), BF16),
+            pltpu.SemaphoreType.DMA((2 * CHUNKS + 1,)),
+        ],
+        compiler_params=pltpu.CompilerParams(vmem_limit_bytes=OWN_MIB * MIB),
+        cost_estimate=pl.CostEstimate(
+            flops=2 * count * width * 2 * H + 4 * count * H * BLOCK_ROWS * half,
+            bytes_accessed=4 * count * width,
+            transcendentals=4 * count * H,
+        ),
+    )(tokens, query_weight, query_prior, head_t, proj)
+
+
+def peer_kernel(
+    tokens_ref, query_ref, prior_ref, map_ref, own_ref, pool_ref, raw_ref, tokens_buf, sems
+):
+    copies = chunk_copies(tokens_ref, tokens_buf, sems, 0)
+    for copy in copies:
+        copy.start()
+    tables = [map_ref[:SPREAD], map_ref[SPREAD:]]
+    own_raw = raw_sums(tables, [own_ref], 0)
+    pool_into(pool_ref, tokens_buf, copies, query_ref, prior_ref)
+    raw_ref[...] = jnp.concatenate([own_raw, raw_sums(tables, [pool_ref], 0)], axis=1)
+
+
+def peer_side(tokens, query_weight, query_prior, own_map, own_pool):
+    count, width = tokens.shape
+    half = own_map.shape[1]
+    return pl.pallas_call(
+        peer_kernel,
+        in_specs=[IN_HBM, IN_VMEM, IN_VMEM, IN_VMEM, IN_VMEM],
+        out_specs=[IN_VMEM] * 2,
+        out_shape=[
+            jax.ShapeDtypeStruct((2, H, count // OBS, half), BF16),
+            jax.ShapeDtypeStruct((PAD, 2 * count // OBS), F32),
+        ],
+        scratch_shapes=[pltpu.VMEM(tokens.shape, BF16), pltpu.SemaphoreType.DMA((CHUNKS,))],
+        compiler_params=pltpu.CompilerParams(vmem_limit_bytes=PEER_MIB * MIB),
+        cost_estimate=pl.CostEstimate(
+            flops=2 * count * width * 2 * H + 4 * count * H * BLOCK_ROWS * half,
+            bytes_accessed=2 * count * width + 2 * count * half,
+            transcendentals=4 * count * H,
+        ),
+    )(tokens, query_weight, query_prior, own_map, own_pool)
+
+
+def finish_raw(top, rest):
+    rest = rest[:8] + rest[8:]
+    rest = rest + jnp.concatenate([rest[4:], rest[:4]], axis=0)
+    return jnp.concatenate([top, rest], axis=0)
+
+
+def raw_sums(tables, pools, which):
+    rows = len(pools) * pools[0].shape[2]
+    top = jnp.zeros((TOP, rows), F32)
+    rest = jnp.zeros((TOP, rows), F32)
+    place = lax.broadcasted_iota(jnp.int32, (TOP, rows), 0) >> 2
+    for h in range(H):
+        left = []
+        for table in tables:
+            left += [table[h * TOP : (h + 1) * TOP], table[H * TOP + h // 4 * TOP :][:TOP]]
+        pooled = jnp.concatenate([pool[which, h] for pool in pools], axis=0)
+        result = dot_nt(jnp.concatenate(left, axis=0), pooled)
+        for i in range(len(tables)):
+            top = top + result[2 * i * TOP :][:TOP]
+            rest = rest + jnp.where(place == h % 4, result[(2 * i + 1) * TOP :][:TOP], 0.0)
+    return finish_raw(top, rest)
+
+
+def lower_raw_kernel(map_ref, own_ref, peer_ref, raw_ref, legal_ref, label_ref, out_ref):
+    rows = own_ref.shape[2]
+    out_ref[:PAD] = raw_ref[...]
+    out_ref[PAD : 2 * PAD] = raw_sums([map_ref[...]], [own_ref, peer_ref], 1)
+    out_ref[2 * PAD :] = jnp.zeros((PAD, 2 * rows), F32)
+    out_ref[2 * PAD : 2 * PAD + A, :rows] = legal_ref[...].astype(F32)
+    out_ref[2 * PAD + A : 2 * PAD + A + 1, :rows] = label_ref[...].astype(F32)
+
+
+def raw_call(kernel, rows_out, *operands):
+    _, _, rows, half = operands[1].shape
+    return pl.pallas_call(
+        kernel,
+        in_specs=[IN_VMEM] * len(operands),
+        out_specs=IN_VMEM,
+        out_shape=jax.ShapeDtypeStruct((rows_out, 2 * rows), F32),
+        compiler_params=pltpu.CompilerParams(vmem_limit_bytes=12 * 2**20),
+        cost_estimate=pl.CostEstimate(
+            flops=8 * TOP * rows * H * half, bytes_accessed=4 * rows * H * half, transcendentals=0
+        ),
+    )(*operands)
+
+
+def policy_rows(raw, legal):
+    logits = 30.0 * jnp.tanh(raw / 30.0)
+    exp_logits = jnp.exp(logits) * legal
+    partition = jnp.sum(exp_logits, axis=0, keepdims=True)
+    return logits, exp_logits / partition, logits - jnp.log(partition)
+
+
+def grad_kernel(
+    mine_ref, theirs_ref, wide_ref, own_ref, peer_ref, out_ref, loss_ref, out_buf, sems,
+):
+    rows = own_ref.shape[2]
+    theirs = theirs_ref[: 2 * PAD]
+    theirs = jnp.concatenate([theirs[:, rows:], theirs[:, :rows]], axis=1)
+    raw = mine_ref[: 2 * PAD] + theirs
+    told = jnp.concatenate([mine_ref[2 * PAD :, :rows], theirs_ref[2 * PAD :, :rows]], axis=1)
+    move = lax.broadcasted_iota(jnp.int32, told.shape, 0)
+    legal = jnp.where(move < A, told, 0.0)
+    onehot = (move.astype(F32) == told[A : A + 1]).astype(F32)
+    logits, policy, log_policy = policy_rows(raw[:PAD], legal)
+    _, lower_policy, _ = policy_rows(raw[PAD:], legal)
+    uniform = legal / jnp.sum(legal, axis=0, keepdims=True)
+    partner = jnp.where(lax.axis_index("dp") // PAIR == 0, uniform, lower_policy)
+    target = 0.5 * onehot + 0.5 * partner
+    loss = -jnp.sum(target * log_policy, axis=0, keepdims=True)
+    loss_ref[...] = loss[:, :rows]
+    logit_grad = (policy - target) * (1.0 - (logits / 30.0) ** 2)
+    high, low = split_high(logit_grad)
+    left = jnp.concatenate([high.astype(F32), low.astype(F32)], axis=0).astype(BF16)
+    chunk = out_buf.shape[0] // GRAD_CHUNKS
+    copies = []
+    for i in range(GRAD_CHUNKS):
+        columns = slice(i * chunk, (i + 1) * chunk)
+        narrow = []
+        for h in range(H):
+            pooled = jnp.concatenate([own_ref[0, h, :, columns], peer_ref[0, h, :, columns]], axis=0)
+            product = dot_nn(left, pooled)
+            narrow.append(product[:PAD] + product[PAD:])
+        narrow = jnp.concatenate(narrow, axis=0).astype(BF16)
+        out_buf[columns, :] = dot_tn(narrow, wide_ref[...])
+        part = pl.ds(i * chunk, chunk)
+        copies.append(pltpu.make_async_copy(out_buf.at[part], out_ref.at[part], sems.at[i]))
+        copies[i].start()
+    for copy in copies:
+        copy.wait()
+
+
+def gradient(mine, theirs, wide, own_pool, peer_pool):
+    _, _, rows, half = own_pool.shape
+    width = H * DH
+    return pl.pallas_call(
+        grad_kernel,
+        in_specs=[IN_VMEM] * 5,
+        out_specs=[IN_HBM, IN_VMEM],
+        out_shape=[
+            jax.ShapeDtypeStruct((half, width), F32),
+            jax.ShapeDtypeStruct((1, rows), F32),
+        ],
+        scratch_shapes=[
+            pltpu.VMEM((half, width), F32),
+            pltpu.SemaphoreType.DMA((GRAD_CHUNKS,)),
+        ],
+        compiler_params=pltpu.CompilerParams(vmem_limit_bytes=16 * MIB),
+        cost_estimate=pl.CostEstimate(
+            flops=2 * H * PAD * half * width,
+            bytes_accessed=4 * half * width + 4 * rows * H * half,
+            transcendentals=0,
+        ),
+    )(mine, theirs, wide, own_pool, peer_pool)
+
+
+def paired_device(
+    tokens, legal_moves, action_label, value_weight, value_prior,
+    query_weight, query_prior, policy_head, head_prior,
+):
+    peer_tokens = partner_2(tokens, "dp", 0)
+    prior_map = prior_fold(jnp.transpose(head_prior, (1, 0, 2)), value_prior)
+    lower_map = shifted(prior_map, "dp", PAIR)
+    own_pool, own_map, wide = own_side(
+        tokens, query_weight, query_prior, jnp.transpose(policy_head, (1, 0, 2)), value_weight
+    )
+    peer_pool, raw = peer_side(peer_tokens, query_weight, query_prior, own_map, own_pool)
+    mine = raw_call(
+        lower_raw_kernel, 3 * PAD,
+        lower_map, own_pool, peer_pool, raw, legal_moves.T, action_label.reshape(1, -1),
+    )
+    theirs = partner_2(mine, "dp", 0)
+    weight_grad, row_loss = gradient(mine, theirs, wide, own_pool, peer_pool)
+    return weight_grad, row_loss.reshape(-1)
+
+
 def solution(mesh):
+    paired = mesh.shape["dp"] == LEVELS * PAIR
     return jax.shard_map(
-        general_device,
+        paired_device if paired else general_device,
         mesh=mesh,
         in_specs=(
             P(("groups", "dp"), None),

time: 74.8 us -> 24 us (0.32)
  matrix products: 26.2 us -> 0 us
  local copies, waits for them, and re-layouts: 26.1 us -> 0.03 us
  Pallas kernels: 0 us -> 16.7 us
  other arithmetic: 13.2 us -> 0 us
  starting transfers between devices: 6.22 us -> 5.26 us
    dot_general x8 -> x0, matrix products: 26.2 us -> none  [the longest x2 6.83 us: attention_of(): lax.dot_general(tokens, query_proj, (((1,), (1,)), ((), ())), preferred_e...]
    pallas_call x0 -> x5, Pallas kernels: none -> 16.7 us  [the longest x1 4.93 us: own_side(): pl.pallas_call(own_kernel, in_specs=[IN_HBM, IN_VMEM, IN_VMEM, IN_HBM, IN...]
    reshape x3 -> x0, local copies, waits for them, and re-layouts: 7.96 us -> none  [the longest x2 7.89 us: policy_of(): moved = lax.dot_general(tokens, mapped, (((1,), (1,)), ((), ())), preferr...]
    convert_element_type x5 -> x0, local copies, waits for them, and re-layouts: 7.16 us -> none  [the longest x2 3.19 us: attention_of(): return attention.astype(jnp.bfloat16).astype(jnp.float32)]
    reduce_sum x4 -> x0, other arithmetic: 6.29 us -> none  [the longest x2 5.93 us: policy_of(): raw_logits = jnp.sum(attention[..., None] * moved, axis=(1, 2))]
    unnamed x14 -> x10, local copies, waits for them, and re-layouts: 5.85 us -> 0.03 us
    div x2 -> x0, other arithmetic: 2.74 us -> none  [attention_of(): attention = exp_scores / jnp.sum(exp_scores, axis=1, keepdims=True)]
    dot_general x2 -> x0, local copies, waits for them, and re-layouts: 2.66 us -> none  [policy_of(): lax.dot_general(tokens, mapped, (((1,), (1,)), ((), ())), preferred_eleme...]
  transfers between devices with their start and end apart: 4 -> 3, of which waited for: 1 -> 1; matrix products, arithmetic and copies ran while one was open for 40% -> 0% of each run, Pallas kernels for 0% -> 53%
where the time goes in v3:
time: 24 us; the launch traced here: 23.9 us
  Pallas kernels  16.7 us (70%)
  starting transfers between devices  5.26 us (22%)
  waiting for transfers between devices  1.06 us (4%)
  between operations  0.77 us (3%)
    pallas_call x1, Pallas kernels, own_side(): pl.pallas_call(own_kernel, in_specs=[IN_HBM, IN_VMEM, IN_VMEM, IN_HBM, IN...  4.93 us
    ppermute x1, starting transfers between devices, shifted(): return lax.ppermute(block, axis, route)  4.53 us
    pallas_call x1, Pallas kernels, peer_side(): pl.pallas_call(peer_kernel, in_specs=[IN_HBM, IN_VMEM, IN_VMEM, IN_VMEM,...  4.36 us
    pallas_call x1, Pallas kernels, prior_fold(): pl.pallas_call(prior_kernel, in_specs=[IN_HBM, IN_HBM], out_specs=IN_VMEM...  3.35 us
    pallas_call x1, Pallas kernels, gradient(): pl.pallas_call(grad_kernel, in_specs=[IN_VMEM] * 5, out_specs=[IN_HBM, IN...  3.29 us
    ppermute x2, waiting for transfers between devices, partner_2(): return lax.ppermute(block, axis, route)  1.06 us
    pallas_call x1, Pallas kernels, raw_call(): pl.pallas_call(kernel, in_specs=[IN_VMEM] * len(operands), out_specs=IN_V...  0.81 us
    ppermute x2, starting transfers between devices, partner_2(): return lax.ppermute(block, axis, route)  0.74 us
  transfers between devices with their start and end apart: 3, of which 1 were waited for; matrix products, arithmetic and copies ran while one was open for 0% of the time, Pallas kernels for 53%

profile of v3, /device:TPU:0, one launch (start us, length us, event | category | flops | bytes accessed | tf_op | source)
XLA Modules:
  0.0 23.9 jit_solution(12886390307712999235)
XLA Ops:
  0.6 0.0 copy-start.2
  0.6 0.0 copy-start
  0.7 0.0 copy-start.1
  0.7 0.5 %collective-permute-start.1 = (bf16[1024,2048]{1,0:T(8,128)(2,1)}, bf16[1024,2048]{1,0:T(8,128)(2,1)S(1)}, u32[]{:S(2)}, u32[]{:S(2)}) collective-permute-start(bf16[1024,2048]{1,0:T(8,128)(2,1)} %tokens_ref.1), channel_id=1, source_target_pairs={{0,1},{1,0},{2,3},{3,2},{4,5},{5,4},{6,7},{7,6},{8,9},{9,8},{10,11... | collective-permute-start | bytes 12582920 | tf_op jit(solution)/shard_map/ppermute | solution.py:23
  1.2 3.4 %shard_map.104 = bf16[160,1024]{1,0:T(8,128)(2,1)} custom-call(f32[20,8,1024]{2,1,0:T(8,128)} %bitcast.8, bf16[1024,1024]{1,0:T(8,128)(2,1)} %proj_ref.2), custom_call_target="tpu_custom_call" | custom-call | flops 671088640 | bytes 2097152 | tf_op jit(solution)/shard_map/pallas_call | solution.py:224
  4.5 4.5 %collective-permute-start = (bf16[160,1024]{1,0:T(8,128)(2,1)}, bf16[160,1024]{1,0:T(8,128)(2,1)S(1)}, u32[]{:S(2)}, u32[]{:S(2)}) collective-permute-start(bf16[160,1024]{1,0:T(8,128)(2,1)} %shard_map.104), channel_id=1, source_target_pairs={{0,2},{1,3},{2,4},{3,5},{4,6},{5,7},{6,8},{7,9},{8,10},{9,11},{10,... | collective-permute-start | bytes 983048 | tf_op jit(solution)/shard_map/ppermute | solution.py:29
  9.1 0.0 copy-done.2
  9.1 0.0 copy-done
  9.1 0.0 copy-done.1
  9.1 4.9 %shard_map.105 = (bf16[2,8,64,1024]{3,2,1,0:T(8,128)(2,1)S(1)}, bf16[320,1024]{1,0:T(8,128)(2,1)S(1)}, bf16[192,1024]{1,0:T(8,128)(2,1)S(1)}) custom-call(bf16[1024,2048]{1,0:T(8,128)(2,1)} %tokens_ref.1, bf16[8,8,2048]{2,1,0:T(8,128)(2,1)S(1)} %copy-done, bf16[8,8,2048]{2,1,0:T(8,128)(2,1)S(1)} %copy-done.1, f32[20,8,1024]{2,1,0:T(8,128)S(1)} %bitcast.5, ...), custom_call_target="tpu_custom_call" | custom-call | flops 603979776 | bytes 8388608 | tf_op jit(solution)/shard_map/pallas_call | solution.py:309
  14.0 0.0 collective-permute-done.1.tokens_ref
  14.1 0.0 copy-start.3
  14.1 0.0 copy-start.4
  14.1 4.4 %shard_map.106 = (bf16[2,8,64,1024]{3,2,1,0:T(8,128)(2,1)S(1)}, f32[24,128]{1,0:T(8,128)S(1)}) custom-call(bf16[1024,2048]{1,0:T(8,128)(2,1)S(1)} %collective-permute-done.1.tokens_ref, bf16[8,8,2048]{2,1,0:T(8,128)(2,1)S(1)} %copy-done, bf16[8,8,2048]{2,1,0:T(8,128)(2,1)S(1)} %copy-done.1, bf16[320,1024]{1,0:T(8,128)(2,1)S(1)} %get-tuple-element.10.map_ref, ...), custom_call_target="tpu_custom_call" | custom-call | flops 603979776 | bytes 6291456 | tf_op jit(solution)/shard_map/pallas_call | solution.py:349
  18.4 0.0 collective-permute-done.map_ref
  18.5 0.0 copy-done.3
  18.5 0.0 copy-done.4
  18.5 0.8 %shard_map.107.mine_ref = f32[72,128]{1,0:T(8,128)S(1)} custom-call(bf16[160,1024]{1,0:T(8,128)(2,1)S(1)} %collective-permute-done.map_ref, bf16[2,8,64,1024]{3,2,1,0:T(8,128)(2,1)S(1)} %get-tuple-element.9.own_ref, bf16[2,8,64,1024]{3,2,1,0:T(8,128)(2,1)S(1)} %get-tuple-element.11.peer_ref, f32[24,128]{1,0:T(8,128)S(1)} %get-tuple-element.12.raw_ref, ...), custom_call_target="tpu_custom_call" | custom-call | flops 67108864 | bytes 2097152 | tf_op jit(solution)/shard_map/pallas_call | solution.py:401
  19.3 0.2 collective-permute-start.2
  19.5 1.1 %collective-permute-done.2.theirs_ref = f32[72,128]{1,0:T(8,128)S(1)} collective-permute-done((f32[72,128]{1,0:T(8,128)S(1)}, f32[72,128]{1,0:T(8,128)S(1)}, u32[]{:S(2)}, u32[]{:S(2)}) %collective-permute-start.2) | collective-permute-done | bytes 36896 | tf_op jit(solution)/shard_map/ppermute | solution.py:23
  20.6 3.3 %shard_map.108 = (f32[1024,1024]{1,0:T(8,128)}, f32[1,64]{1,0:T(1,128)}) custom-call(f32[72,128]{1,0:T(8,128)S(1)} %shard_map.107.mine_ref, f32[72,128]{1,0:T(8,128)S(1)} %collective-permute-done.2.theirs_ref, bf16[192,1024]{1,0:T(8,128)(2,1)S(1)} %get-tuple-element.13.wide_ref, bf16[2,8,64,1024]{3,2,1,0:T(8,128)(2,1)S(1)} %get-tuple-element.9.own_ref, ...), custom_call_target="tpu_custom_call" | custom-call | flops 402653184 | bytes 6291456 | tf_op jit(solution)/shard_map/pallas_call | solution.py:462
Async XLA Ops:
  0.6 8.4 %copy-start.2 = (f32[8,20,1024]{2,0,1:T(8,128)S(1)}, f32[8,20,1024]{2,0,1:T(8,128)}, u32[]{:S(2)}) copy-start(f32[8,20,1024]{2,0,1:T(8,128)} %param.16) | copy-start | bytes 1966084
  0.6 8.4 %copy-start = (bf16[8,8,2048]{2,1,0:T(8,128)(2,1)S(1)}, bf16[8,8,2048]{2,1,0:T(8,128)(2,1)}, u32[]{:S(2)}) copy-start(bf16[8,8,2048]{2,1,0:T(8,128)(2,1)} %query_ref.3) | copy-start | bytes 786436
  0.7 8.4 %copy-start.1 = (bf16[8,8,2048]{2,1,0:T(8,128)(2,1)S(1)}, bf16[8,8,2048]{2,1,0:T(8,128)(2,1)}, u32[]{:S(2)}) copy-start(bf16[8,8,2048]{2,1,0:T(8,128)(2,1)} %prior_ref.3) | copy-start | bytes 786436
  0.7 13.4 %collective-permute-start.1 = (bf16[1024,2048]{1,0:T(8,128)(2,1)}, bf16[1024,2048]{1,0:T(8,128)(2,1)S(1)}, u32[]{:S(2)}, u32[]{:S(2)}) collective-permute-start(bf16[1024,2048]{1,0:T(8,128)(2,1)} %tokens_ref.1), channel_id=1, source_target_pairs={{0,1},{1,0},{2,3},{3,2},{4,5},{5,4},{6,7},{7,6},{8,9},{9,8},{10,11... | collective-permute-start | bytes 12582920 | tf_op jit(solution)/shard_map/ppermute | solution.py:23
  4.5 13.9 %collective-permute-start = (bf16[160,1024]{1,0:T(8,128)(2,1)}, bf16[160,1024]{1,0:T(8,128)(2,1)S(1)}, u32[]{:S(2)}, u32[]{:S(2)}) collective-permute-start(bf16[160,1024]{1,0:T(8,128)(2,1)} %shard_map.104), channel_id=1, source_target_pairs={{0,2},{1,3},{2,4},{3,5},{4,6},{5,7},{6,8},{7,9},{8,10},{9,11},{10,... | collective-permute-start | bytes 983048 | tf_op jit(solution)/shard_map/ppermute | solution.py:29
  14.1 4.4 %copy-start.3 = (s32[64,20]{0,1:T(8,128)S(1)}, s32[64,20]{0,1:T(8,128)}, u32[]{:S(2)}) copy-start(s32[64,20]{0,1:T(8,128)} %param.10) | copy-start | bytes 15364
  14.1 4.4 %copy-start.4 = (s32[64]{0:T(128)S(1)}, s32[64]{0:T(128)}, u32[]{:S(2)}) copy-start(s32[64]{0:T(128)} %param.11) | copy-start | bytes 772
  19.3 1.3 %collective-permute-start.2 = (f32[72,128]{1,0:T(8,128)S(1)}, f32[72,128]{1,0:T(8,128)S(1)}, u32[]{:S(2)}, u32[]{:S(2)}) collective-permute-start(f32[72,128]{1,0:T(8,128)S(1)} %shard_map.107.mine_ref), channel_id=1, source_target_pairs={{0,1},{1,0},{2,3},{3,2},{4,5},{5,4},{6,7},{7,6},{8,9},{9,8},{10,11... | collective-permute-start | bytes 110600 | tf_op jit(solution)/shard_map/ppermute | solution.py:23

commit v4 on v3

--- a/solution.py
+++ b/solution.py
@@ -130,14 +130,16 @@
 F32 = jnp.float32
 BF16 = jnp.bfloat16
 PAD = 24
-CHUNKS = 4
 GRAD_CHUNKS = 4
 DH_BITS = 7
 OBS_BITS = 4
 MIB = 2**20
-PRIOR_MIB = 54
-OWN_MIB = 48
-PEER_MIB = 40
+PRIOR_MIB = 12
+OWN_MIB = 16
+PEER_MIB = 16
+PRIOR_COST = 40
+SPREAD_COST = 100000
+SPREAD_MIB = 53
 
 
 def dot_nt(left, right):
@@ -172,27 +174,17 @@
     return jnp.concatenate(pieces, axis=0)
 
 
-def chunk_copies(source_ref, target_ref, sems, first):
-    chunk = source_ref.shape[0] // CHUNKS
-    copies = []
-    for i in range(CHUNKS):
-        rows = pl.ds(i * chunk, chunk)
-        copies.append(
-            pltpu.make_async_copy(source_ref.at[rows], target_ref.at[rows], sems.at[first + i])
-        )
-    return copies
-
-
-def spread_into(spread_ref, head_buf, level):
-    head = head_buf[:, pl.ds(level, 1), :].reshape(A, H * DH)
+def spread_into(spread_ref, head_ref):
+    level = lax.axis_index("dp") // PAIR
+    head = head_ref[:, pl.ds(level, 1), :].reshape(A, H * DH)
     high, low = split_high(spread_heads(head))
     spread_ref[:SPREAD, :] = high
     spread_ref[SPREAD:, :] = low
     return head
 
 
-def fold_into(out_ref, proj_buf, spread_ref, parts):
-    product = dot_nt(spread_ref[...], proj_buf[...])
+def fold_into(out_ref, proj_ref, spread_ref, parts):
+    product = dot_nt(spread_ref[...], proj_ref[...])
     product = product[:SPREAD] + product[SPREAD:]
     if parts == 1:
         out_ref[...] = product.astype(BF16)
@@ -202,44 +194,53 @@
         out_ref[SPREAD:] = low
 
 
-def prior_kernel(head_ref, proj_ref, out_ref, head_buf, proj_buf, spread_ref, sems):
-    head_copy = pltpu.make_async_copy(head_ref, head_buf, sems.at[CHUNKS])
-    head_copy.start()
-    copies = chunk_copies(proj_ref, proj_buf, sems, 0)
-    for copy in copies:
-        copy.start()
-    head_copy.wait()
-    spread_into(spread_ref, head_buf, lax.axis_index("dp") // PAIR)
-    for copy in copies:
-        copy.wait()
-    fold_into(out_ref, proj_buf, spread_ref, 1)
+def spread_kernel(head_ref, spread_ref, head_buf, sem):
+    copy = pltpu.make_async_copy(head_ref, head_buf, sem)
+    copy.start()
+    copy.wait()
+    spread_into(spread_ref, head_buf)
+
+
+def prior_kernel(spread_ref, proj_ref, out_ref):
+    fold_into(out_ref, proj_ref, spread_ref, 1)
 
 
 IN_HBM = pl.BlockSpec(memory_space=pltpu.HBM)
 IN_VMEM = pl.BlockSpec(memory_space=pltpu.VMEM)
 
 
-def prior_fold(head_t, proj):
+def head_spread(head_t):
+    width = head_t.shape[2]
+    return pl.pallas_call(
+        spread_kernel,
+        in_specs=[IN_HBM],
+        out_specs=IN_VMEM,
+        out_shape=jax.ShapeDtypeStruct((2 * SPREAD, width), BF16),
+        scratch_shapes=[pltpu.VMEM(head_t.shape, F32), pltpu.SemaphoreType.DMA],
+        compiler_params=pltpu.CompilerParams(vmem_limit_bytes=SPREAD_MIB * MIB),
+        cost_estimate=pl.CostEstimate(
+            flops=SPREAD_COST * SPREAD * width, bytes_accessed=4 * head_t.size, transcendentals=0
+        ),
+    )(head_t)
+
+
+def prior_fold(spread, proj):
     depth, width = proj.shape
     return pl.pallas_call(
         prior_kernel,
-        in_specs=[IN_HBM, IN_HBM],
+        in_specs=[IN_VMEM, IN_VMEM],
         out_specs=IN_VMEM,
         out_shape=jax.ShapeDtypeStruct((SPREAD, depth), BF16),
-        scratch_shapes=[
-            pltpu.VMEM(head_t.shape, F32),
-            pltpu.VMEM(proj.shape, BF16),
-            pltpu.VMEM((2 * SPREAD, width), BF16),
-            pltpu.SemaphoreType.DMA((CHUNKS + 1,)),
-        ],
         compiler_params=pltpu.CompilerParams(vmem_limit_bytes=PRIOR_MIB * MIB),
         cost_estimate=pl.CostEstimate(
-            flops=4 * SPREAD * depth * width, bytes_accessed=2 * depth * width, transcendentals=0
-        ),
-    )(head_t, proj)
-
-
-def pool_into(out_ref, tokens_ref, copies, query_ref, prior_ref):
+            flops=PRIOR_COST * SPREAD * depth * width,
+            bytes_accessed=2 * depth * width,
+            transcendentals=0,
+        ),
+    )(spread, proj)
+
+
+def pool_into(out_ref, tokens_ref, query_ref, prior_ref):
     count = tokens_ref.shape[0]
     half = out_ref.shape[3]
     block = BLOCK_ROWS * OBS
@@ -258,12 +259,8 @@
         == lax.broadcasted_iota(jnp.int32, (BLOCK_ROWS, block), 1) >> OBS_BITS
     )
     start = pl.multiple_of(device_place % PAIR * half, half)
-    scores = []
-    for step in range(blocks // 2):
-        for copy in copies[2 * step : 2 * step + 2]:
-            copy.wait()
-        two = dot_nt(queries, tokens_ref[2 * step * block : 2 * (step + 1) * block])
-        scores += [two[:, :block], two[:, block:]]
+    scores = dot_nt(queries, tokens_ref[...])
+    scores = [scores[:, i * block : (i + 1) * block] for i in range(blocks)]
     exp_scores = jnp.exp(5.0 * jnp.tanh(jnp.concatenate(scores, axis=0) / 5.0))
     first, rest = split_high(exp_scores)
     second, third = split_high(exp_scores - first.astype(F32))
@@ -283,24 +280,15 @@
 
 
 def own_kernel(
-    tokens_ref, query_ref, prior_ref, head_ref, proj_ref,
-    pool_ref, map_ref, wide_ref, tokens_buf, head_buf, proj_buf, spread_ref, sems,
+    tokens_ref, query_ref, prior_ref, head_ref, proj_ref, pool_ref, map_ref, wide_ref, spread_ref
 ):
-    token_copies = chunk_copies(tokens_ref, tokens_buf, sems, 0)
-    proj_copies = chunk_copies(proj_ref, proj_buf, sems, CHUNKS)
-    head_copy = pltpu.make_async_copy(head_ref, head_buf, sems.at[2 * CHUNKS])
-    for copy in [head_copy] + proj_copies + token_copies:
-        copy.start()
-    head_copy.wait()
-    head = spread_into(spread_ref, head_buf, lax.axis_index("dp") // PAIR)
-    for copy in proj_copies:
-        copy.wait()
-    fold_into(map_ref, proj_buf, spread_ref, 2)
+    head = spread_into(spread_ref, head_ref)
+    fold_into(map_ref, proj_ref, spread_ref, 2)
     head = jnp.concatenate([head, jnp.zeros((PAD - A, H * DH), F32)], axis=0)
     lane_head = lax.broadcasted_iota(jnp.int32, (PAD, H * DH), 1) >> DH_BITS
     wide = [jnp.where(lane_head == h, head, 0.0) for h in range(H)]
     wide_ref[...] = jnp.concatenate(wide, axis=0).astype(BF16)
-    pool_into(pool_ref, tokens_buf, token_copies, query_ref, prior_ref)
+    pool_into(pool_ref, tokens_ref, query_ref, prior_ref)
 
 
 def own_side(tokens, query_weight, query_prior, head_t, proj):
@@ -308,20 +296,14 @@
     half = proj.shape[0]
     return pl.pallas_call(
         own_kernel,
-        in_specs=[IN_HBM, IN_VMEM, IN_VMEM, IN_HBM, IN_HBM],
+        in_specs=[IN_VMEM] * 5,
         out_specs=[IN_VMEM] * 3,
         out_shape=[
             jax.ShapeDtypeStruct((2, H, count // OBS, half), BF16),
             jax.ShapeDtypeStruct((2 * SPREAD, half), BF16),
             jax.ShapeDtypeStruct((H * PAD, H * DH), BF16),
         ],
-        scratch_shapes=[
-            pltpu.VMEM(tokens.shape, BF16),
-            pltpu.VMEM(head_t.shape, F32),
-            pltpu.VMEM(proj.shape, BF16),
-            pltpu.VMEM((2 * SPREAD, H * DH), BF16),
-            pltpu.SemaphoreType.DMA((2 * CHUNKS + 1,)),
-        ],
+        scratch_shapes=[pltpu.VMEM((2 * SPREAD, H * DH), BF16)],
         compiler_params=pltpu.CompilerParams(vmem_limit_bytes=OWN_MIB * MIB),
         cost_estimate=pl.CostEstimate(
             flops=2 * count * width * 2 * H + 4 * count * H * BLOCK_ROWS * half,
@@ -331,16 +313,10 @@
     )(tokens, query_weight, query_prior, head_t, proj)
 
 
-def peer_kernel(
-    tokens_ref, query_ref, prior_ref, map_ref, own_ref, pool_ref, raw_ref, tokens_buf, sems
-):
-    copies = chunk_copies(tokens_ref, tokens_buf, sems, 0)
-    for copy in copies:
-        copy.start()
+def peer_kernel(tokens_ref, query_ref, prior_ref, map_ref, own_ref, pool_ref, raw_ref):
+    pool_into(pool_ref, tokens_ref, query_ref, prior_ref)
     tables = [map_ref[:SPREAD], map_ref[SPREAD:]]
-    own_raw = raw_sums(tables, [own_ref], 0)
-    pool_into(pool_ref, tokens_buf, copies, query_ref, prior_ref)
-    raw_ref[...] = jnp.concatenate([own_raw, raw_sums(tables, [pool_ref], 0)], axis=1)
+    raw_ref[...] = raw_sums(tables, [own_ref, pool_ref], 0)
 
 
 def peer_side(tokens, query_weight, query_prior, own_map, own_pool):
@@ -348,13 +324,12 @@
     half = own_map.shape[1]
     return pl.pallas_call(
         peer_kernel,
-        in_specs=[IN_HBM, IN_VMEM, IN_VMEM, IN_VMEM, IN_VMEM],
+        in_specs=[IN_VMEM] * 5,
         out_specs=[IN_VMEM] * 2,
         out_shape=[
             jax.ShapeDtypeStruct((2, H, count // OBS, half), BF16),
             jax.ShapeDtypeStruct((PAD, 2 * count // OBS), F32),
         ],
-        scratch_shapes=[pltpu.VMEM(tokens.shape, BF16), pltpu.SemaphoreType.DMA((CHUNKS,))],
         compiler_params=pltpu.CompilerParams(vmem_limit_bytes=PEER_MIB * MIB),
         cost_estimate=pl.CostEstimate(
             flops=2 * count * width * 2 * H + 4 * count * H * BLOCK_ROWS * half,
@@ -485,7 +460,8 @@
     query_weight, query_prior, policy_head, head_prior,
 ):
     peer_tokens = partner_2(tokens, "dp", 0)
-    prior_map = prior_fold(jnp.transpose(head_prior, (1, 0, 2)), value_prior)
+    spread = head_spread(jnp.transpose(head_prior, (1, 0, 2)))
+    prior_map = prior_fold(spread, value_prior)
     lower_map = shifted(prior_map, "dp", PAIR)
     own_pool, own_map, wide = own_side(
         tokens, query_weight, query_prior, jnp.transpose(policy_head, (1, 0, 2)), value_weight

time: 24 us -> 22.5 us (0.938)
  the two profiles are of different devices: /device:TPU:0 before, /device:TPU:25 now
where the time goes in v4:
time: 22.5 us; the launch traced here: 22.3 us
  Pallas kernels  12.8 us (57%)
  starting transfers between devices  5.02 us (22%)
  waiting for transfers between devices  3.31 us (15%)
  between operations  0.76 us (3%)
  local copies, waits for them, and re-layouts  0.4 us (2%)
    pallas_call x1, Pallas kernels, peer_side(): pl.pallas_call(peer_kernel, in_specs=[IN_VMEM] * 5, out_specs=[IN_VMEM] *...  3.62 us
    ppermute x1, starting transfers between devices, shifted(): return lax.ppermute(block, axis, route)  3.41 us
    pallas_call x1, Pallas kernels, gradient(): pl.pallas_call(grad_kernel, in_specs=[IN_VMEM] * 5, out_specs=[IN_HBM, IN...  3.3 us
    pallas_call x1, Pallas kernels, own_side(): pl.pallas_call(own_kernel, in_specs=[IN_VMEM] * 5, out_specs=[IN_VMEM] *...  2.8 us
    ppermute x1, waiting for transfers between devices, shifted(): return lax.ppermute(block, axis, route)  2.44 us
    ppermute x2, starting transfers between devices, partner_2(): return lax.ppermute(block, axis, route)  1.61 us
    pallas_call x1, Pallas kernels, head_spread(): pl.pallas_call(spread_kernel, in_specs=[IN_HBM], out_specs=IN_VMEM, out_s...  1.41 us
    pallas_call x1, Pallas kernels, prior_fold(): pl.pallas_call(prior_kernel, in_specs=[IN_VMEM, IN_VMEM], out_specs=IN_VM...  0.87 us
  transfers between devices with their start and end apart: 3, of which 2 were waited for; matrix products, arithmetic and copies ran while one was open for 0% of the time, Pallas kernels for 39%

profile of v4, /device:TPU:25, one launch (start us, length us, event | category | flops | bytes accessed | tf_op | source)
XLA Modules:
  0.0 22.3 jit_solution(7011761615047488240)
XLA Ops:
  0.6 0.7 %collective-permute-start.1 = (bf16[1024,2048]{1,0:T(8,128)(2,1)}, bf16[1024,2048]{1,0:T(8,128)(2,1)S(1)}, u32[]{:S(2)}, u32[]{:S(2)}) collective-permute-start(bf16[1024,2048]{1,0:T(8,128)(2,1)} %tokens_ref.1), channel_id=1, source_target_pairs={{0,1},{1,0},{2,3},{3,2},{4,5},{5,4},{6,7},{7,6},{8,9},{9,8},{10,11... | collective-permute-start | bytes 12582920 | tf_op jit(solution)/shard_map/ppermute | solution.py:23
  1.4 0.0 copy-start.7
  1.4 1.4 %shard_map.104.spread_ref = bf16[320,1024]{1,0:T(8,128)(2,1)S(1)} custom-call(f32[20,8,1024]{2,1,0:T(8,128)} %bitcast.8), custom_call_target="tpu_custom_call" | custom-call | flops 16384000000 | bytes 655360 | tf_op jit(solution)/shard_map/pallas_call | solution.py:214
  2.8 0.4 %copy-done.7 = bf16[1024,1024]{1,0:T(8,128)(2,1)S(1)} copy-done((bf16[1024,1024]{1,0:T(8,128)(2,1)S(1)}, bf16[1024,1024]{1,0:T(8,128)(2,1)}, u32[]{:S(2)}) %copy-start.7) | copy-done | bytes 2097176
  3.2 0.0 copy-start.4
  3.2 0.9 %shard_map.105 = bf16[160,1024]{1,0:T(8,128)(2,1)S(1)} custom-call(bf16[320,1024]{1,0:T(8,128)(2,1)S(1)} %shard_map.104.spread_ref, bf16[1024,1024]{1,0:T(8,128)(2,1)S(1)} %copy-done.7), custom_call_target="tpu_custom_call" | custom-call | flops 6710886400 | bytes 2097152 | tf_op jit(solution)/shard_map/pallas_call | solution.py:229
  4.1 3.4 %collective-permute-start = (bf16[160,1024]{1,0:T(8,128)(2,1)S(1)}, bf16[160,1024]{1,0:T(8,128)(2,1)S(1)}, u32[]{:S(2)}, u32[]{:S(2)}) collective-permute-start(bf16[160,1024]{1,0:T(8,128)(2,1)S(1)} %shard_map.105), channel_id=1, source_target_pairs={{0,2},{1,3},{2,4},{3,5},{4,6},{5,7},{6,8},{7,9},{8,10},{9,11},{10,... | collective-permute-start | bytes 983048 | tf_op jit(solution)/shard_map/ppermute | solution.py:29
  7.5 0.0 copy-done
  7.5 0.0 copy-done.1
  7.5 0.0 copy-done.2
  7.5 0.0 copy-done.3
  7.5 0.0 copy-done.4
  7.5 2.8 %shard_map.106 = (bf16[2,8,64,1024]{3,2,1,0:T(8,128)(2,1)S(1)}, bf16[320,1024]{1,0:T(8,128)(2,1)S(1)}, bf16[192,1024]{1,0:T(8,128)(2,1)S(1)}) custom-call(bf16[1024,2048]{1,0:T(8,128)(2,1)S(1)} %copy-done, bf16[8,8,2048]{2,1,0:T(8,128)(2,1)S(1)} %copy-done.2, bf16[8,8,2048]{2,1,0:T(8,128)(2,1)S(1)} %copy-done.3, f32[20,8,1024]{2,1,0:T(8,128)S(1)} %bitcast.5, ...), custom_call_target="tpu_custom_call" | custom-call | flops 603979776 | bytes 8388608 | tf_op jit(solution)/shard_map/pallas_call | solution.py:297
  10.3 0.0 collective-permute-done.1.tokens_ref
  10.3 0.0 copy-start.5
  10.4 0.0 copy-start.6
  10.4 3.6 %shard_map.107 = (bf16[2,8,64,1024]{3,2,1,0:T(8,128)(2,1)S(1)}, f32[24,128]{1,0:T(8,128)S(1)}) custom-call(bf16[1024,2048]{1,0:T(8,128)(2,1)S(1)} %collective-permute-done.1.tokens_ref, bf16[8,8,2048]{2,1,0:T(8,128)(2,1)S(1)} %copy-done.2, bf16[8,8,2048]{2,1,0:T(8,128)(2,1)S(1)} %copy-done.3, bf16[320,1024]{1,0:T(8,128)(2,1)S(1)} %get-tuple-element.10.map_ref, ...), custom_call_target="tpu_custom_call" | custom-call | flops 603979776 | bytes 6291456 | tf_op jit(solution)/shard_map/pallas_call | solution.py:325
  14.0 2.4 %collective-permute-done.map_ref = bf16[160,1024]{1,0:T(8,128)(2,1)S(1)} collective-permute-done((bf16[160,1024]{1,0:T(8,128)(2,1)S(1)}, bf16[160,1024]{1,0:T(8,128)(2,1)S(1)}, u32[]{:S(2)}, u32[]{:S(2)}) %collective-permute-start) | collective-permute-done | bytes 327712 | tf_op jit(solution)/shard_map/ppermute | solution.py:29
  16.4 0.0 copy-done.5
  16.4 0.0 copy-done.6
  16.4 0.8 %shard_map.108.mine_ref = f32[72,128]{1,0:T(8,128)S(1)} custom-call(bf16[160,1024]{1,0:T(8,128)(2,1)S(1)} %collective-permute-done.map_ref, bf16[2,8,64,1024]{3,2,1,0:T(8,128)(2,1)S(1)} %get-tuple-element.9.own_ref, bf16[2,8,64,1024]{3,2,1,0:T(8,128)(2,1)S(1)} %get-tuple-element.11.peer_ref, f32[24,128]{1,0:T(8,128)S(1)} %get-tuple-element.12.raw_ref, ...), custom_call_target="tpu_custom_call" | custom-call | flops 67108864 | bytes 2097152 | tf_op jit(solution)/shard_map/pallas_call | solution.py:376
  17.3 0.9 %collective-permute-start.2 = (f32[72,128]{1,0:T(8,128)S(1)}, f32[72,128]{1,0:T(8,128)S(1)}, u32[]{:S(2)}, u32[]{:S(2)}) collective-permute-start(f32[72,128]{1,0:T(8,128)S(1)} %shard_map.108.mine_ref), channel_id=1, source_target_pairs={{0,1},{1,0},{2,3},{3,2},{4,5},{5,4},{6,7},{7,6},{8,9},{9,8},{10,11... | collective-permute-start | bytes 110600 | tf_op jit(solution)/shard_map/ppermute | solution.py:23
  18.1 0.9 %collective-permute-done.2.theirs_ref = f32[72,128]{1,0:T(8,128)S(1)} collective-permute-done((f32[72,128]{1,0:T(8,128)S(1)}, f32[72,128]{1,0:T(8,128)S(1)}, u32[]{:S(2)}, u32[]{:S(2)}) %collective-permute-start.2) | collective-permute-done | bytes 36896 | tf_op jit(solution)/shard_map/ppermute | solution.py:23
  19.0 3.3 %shard_map.109 = (f32[1024,1024]{1,0:T(8,128)}, f32[1,64]{1,0:T(1,128)}) custom-call(f32[72,128]{1,0:T(8,128)S(1)} %shard_map.108.mine_ref, f32[72,128]{1,0:T(8,128)S(1)} %collective-permute-done.2.theirs_ref, bf16[192,1024]{1,0:T(8,128)(2,1)S(1)} %get-tuple-element.13.wide_ref, bf16[2,8,64,1024]{3,2,1,0:T(8,128)(2,1)S(1)} %get-tuple-element.9.own_ref, ...), custom_call_target="tpu_custom_call" | custom-call | flops 402653184 | bytes 6291456 | tf_op jit(solution)/shard_map/pallas_call | solution.py:437
  (4 shorter events, 0.0 us)
Async XLA Ops:
  0.6 9.7 %collective-permute-start.1 = (bf16[1024,2048]{1,0:T(8,128)(2,1)}, bf16[1024,2048]{1,0:T(8,128)(2,1)S(1)}, u32[]{:S(2)}, u32[]{:S(2)}) collective-permute-start(bf16[1024,2048]{1,0:T(8,128)(2,1)} %tokens_ref.1), channel_id=1, source_target_pairs={{0,1},{1,0},{2,3},{3,2},{4,5},{5,4},{6,7},{7,6},{8,9},{9,8},{10,11... | collective-permute-start | bytes 12582920 | tf_op jit(solution)/shard_map/ppermute | solution.py:23
  1.4 1.8 %copy-start.7 = (bf16[1024,1024]{1,0:T(8,128)(2,1)S(1)}, bf16[1024,1024]{1,0:T(8,128)(2,1)}, u32[]{:S(2)}) copy-start(bf16[1024,1024]{1,0:T(8,128)(2,1)} %proj_ref.2) | copy-start | bytes 6291460
  3.2 4.3 %copy-start = (bf16[1024,2048]{1,0:T(8,128)(2,1)S(1)}, bf16[1024,2048]{1,0:T(8,128)(2,1)}, u32[]{:S(2)}) copy-start(bf16[1024,2048]{1,0:T(8,128)(2,1)} %tokens_ref.1) | copy-start | bytes 12582916
  3.2 4.3 %copy-start.1 = (bf16[1024,1024]{1,0:T(8,128)(2,1)S(1)}, bf16[1024,1024]{1,0:T(8,128)(2,1)}, u32[]{:S(2)}) copy-start(bf16[1024,1024]{1,0:T(8,128)(2,1)} %proj_ref.3) | copy-start | bytes 6291460
  3.2 4.3 %copy-start.2 = (bf16[8,8,2048]{2,1,0:T(8,128)(2,1)S(1)}, bf16[8,8,2048]{2,1,0:T(8,128)(2,1)}, u32[]{:S(2)}) copy-start(bf16[8,8,2048]{2,1,0:T(8,128)(2,1)} %query_ref.3) | copy-start | bytes 786436
  3.2 4.3 %copy-start.3 = (bf16[8,8,2048]{2,1,0:T(8,128)(2,1)S(1)}, bf16[8,8,2048]{2,1,0:T(8,128)(2,1)}, u32[]{:S(2)}) copy-start(bf16[8,8,2048]{2,1,0:T(8,128)(2,1)} %prior_ref.3) | copy-start | bytes 786436
  3.2 4.4 %copy-start.4 = (f32[8,20,1024]{2,0,1:T(8,128)S(1)}, f32[8,20,1024]{2,0,1:T(8,128)}, u32[]{:S(2)}) copy-start(f32[8,20,1024]{2,0,1:T(8,128)} %param.16) | copy-start | bytes 1966084
  4.1 12.4 %collective-permute-start = (bf16[160,1024]{1,0:T(8,128)(2,1)S(1)}, bf16[160,1024]{1,0:T(8,128)(2,1)S(1)}, u32[]{:S(2)}, u32[]{:S(2)}) collective-permute-start(bf16[160,1024]{1,0:T(8,128)(2,1)S(1)} %shard_map.105), channel_id=1, source_target_pairs={{0,2},{1,3},{2,4},{3,5},{4,6},{5,7},{6,8},{7,9},{8,10},{9,11},{10,... | collective-permute-start | bytes 983048 | tf_op jit(solution)/shard_map/ppermute | solution.py:29
  10.3 6.1 %copy-start.5 = (s32[64,20]{0,1:T(8,128)S(1)}, s32[64,20]{0,1:T(8,128)}, u32[]{:S(2)}) copy-start(s32[64,20]{0,1:T(8,128)} %param.10) | copy-start | bytes 15364
  10.4 6.1 %copy-start.6 = (s32[64]{0:T(128)S(1)}, s32[64]{0:T(128)}, u32[]{:S(2)}) copy-start(s32[64]{0:T(128)} %param.11) | copy-start | bytes 772
  17.3 1.7 %collective-permute-start.2 = (f32[72,128]{1,0:T(8,128)S(1)}, f32[72,128]{1,0:T(8,128)S(1)}, u32[]{:S(2)}, u32[]{:S(2)}) collective-permute-start(f32[72,128]{1,0:T(8,128)S(1)} %shard_map.108.mine_ref), channel_id=1, source_target_pairs={{0,1},{1,0},{2,3},{3,2},{4,5},{5,4},{6,7},{7,6},{8,9},{9,8},{10,11... | collective-permute-start | bytes 110600 | tf_op jit(solution)/shard_map/ppermute | solution.py:23

commit v5 on v4

--- a/solution.py
+++ b/solution.py
@@ -313,22 +313,28 @@
     )(tokens, query_weight, query_prior, head_t, proj)
 
 
-def peer_kernel(tokens_ref, query_ref, prior_ref, map_ref, own_ref, pool_ref, raw_ref):
+def peer_kernel(
+    tokens_ref, query_ref, prior_ref, map_ref, own_ref, legal_ref, label_ref, pool_ref, told_ref
+):
     pool_into(pool_ref, tokens_ref, query_ref, prior_ref)
     tables = [map_ref[:SPREAD], map_ref[SPREAD:]]
-    raw_ref[...] = raw_sums(tables, [own_ref, pool_ref], 0)
-
-
-def peer_side(tokens, query_weight, query_prior, own_map, own_pool):
+    rows = own_ref.shape[2]
+    told_ref[:PAD] = raw_sums(tables, [own_ref, pool_ref], 0)
+    told_ref[PAD:] = jnp.zeros((PAD, 2 * rows), F32)
+    told_ref[PAD : PAD + A, :rows] = legal_ref[...].astype(F32)
+    told_ref[PAD + A : PAD + A + 1, :rows] = label_ref[...].astype(F32)
+
+
+def peer_side(tokens, query_weight, query_prior, own_map, own_pool, legal_t, label):
     count, width = tokens.shape
     half = own_map.shape[1]
     return pl.pallas_call(
         peer_kernel,
-        in_specs=[IN_VMEM] * 5,
+        in_specs=[IN_VMEM] * 7,
         out_specs=[IN_VMEM] * 2,
         out_shape=[
             jax.ShapeDtypeStruct((2, H, count // OBS, half), BF16),
-            jax.ShapeDtypeStruct((PAD, 2 * count // OBS), F32),
+            jax.ShapeDtypeStruct((2 * PAD, 2 * count // OBS), F32),
         ],
         compiler_params=pltpu.CompilerParams(vmem_limit_bytes=PEER_MIB * MIB),
         cost_estimate=pl.CostEstimate(
@@ -336,7 +342,7 @@
             bytes_accessed=2 * count * width + 2 * count * half,
             transcendentals=4 * count * H,
         ),
-    )(tokens, query_weight, query_prior, own_map, own_pool)
+    )(tokens, query_weight, query_prior, own_map, own_pool, legal_t, label)
 
 
 def finish_raw(top, rest):
@@ -362,27 +368,22 @@
     return finish_raw(top, rest)
 
 
-def lower_raw_kernel(map_ref, own_ref, peer_ref, raw_ref, legal_ref, label_ref, out_ref):
-    rows = own_ref.shape[2]
-    out_ref[:PAD] = raw_ref[...]
-    out_ref[PAD : 2 * PAD] = raw_sums([map_ref[...]], [own_ref, peer_ref], 1)
-    out_ref[2 * PAD :] = jnp.zeros((PAD, 2 * rows), F32)
-    out_ref[2 * PAD : 2 * PAD + A, :rows] = legal_ref[...].astype(F32)
-    out_ref[2 * PAD + A : 2 * PAD + A + 1, :rows] = label_ref[...].astype(F32)
-
-
-def raw_call(kernel, rows_out, *operands):
-    _, _, rows, half = operands[1].shape
+def lower_kernel(map_ref, own_ref, peer_ref, earlier_ref, out_ref):
+    out_ref[...] = raw_sums([map_ref[...]], [own_ref, peer_ref], 1)
+
+
+def lower_raw(lower_map, own_pool, peer_pool, earlier):
+    _, _, rows, half = own_pool.shape
     return pl.pallas_call(
-        kernel,
-        in_specs=[IN_VMEM] * len(operands),
+        lower_kernel,
+        in_specs=[IN_VMEM] * 4,
         out_specs=IN_VMEM,
-        out_shape=jax.ShapeDtypeStruct((rows_out, 2 * rows), F32),
-        compiler_params=pltpu.CompilerParams(vmem_limit_bytes=12 * 2**20),
+        out_shape=jax.ShapeDtypeStruct((PAD, 2 * rows), F32),
+        compiler_params=pltpu.CompilerParams(vmem_limit_bytes=12 * MIB),
         cost_estimate=pl.CostEstimate(
             flops=8 * TOP * rows * H * half, bytes_accessed=4 * rows * H * half, transcendentals=0
         ),
-    )(*operands)
+    )(lower_map, own_pool, peer_pool, earlier)
 
 
 def policy_rows(raw, legal):
@@ -392,21 +393,22 @@
     return logits, exp_logits / partition, logits - jnp.log(partition)
 
 
-def grad_kernel(
-    mine_ref, theirs_ref, wide_ref, own_ref, peer_ref, out_ref, loss_ref, out_buf, sems,
-):
+def swapped(theirs):
+    rows = theirs.shape[1] // 2
+    return jnp.concatenate([theirs[:, rows:], theirs[:, :rows]], axis=1)
+
+
+def grad_into(out_ref, loss_ref, out_buf, sems, mine_ref, theirs_ref, wide_ref, own_ref, peer_ref, lower):
     rows = own_ref.shape[2]
-    theirs = theirs_ref[: 2 * PAD]
-    theirs = jnp.concatenate([theirs[:, rows:], theirs[:, :rows]], axis=1)
-    raw = mine_ref[: 2 * PAD] + theirs
-    told = jnp.concatenate([mine_ref[2 * PAD :, :rows], theirs_ref[2 * PAD :, :rows]], axis=1)
+    told = jnp.concatenate([mine_ref[PAD:, :rows], theirs_ref[PAD:, :rows]], axis=1)
     move = lax.broadcasted_iota(jnp.int32, told.shape, 0)
     legal = jnp.where(move < A, told, 0.0)
     onehot = (move.astype(F32) == told[A : A + 1]).astype(F32)
-    logits, policy, log_policy = policy_rows(raw[:PAD], legal)
-    _, lower_policy, _ = policy_rows(raw[PAD:], legal)
-    uniform = legal / jnp.sum(legal, axis=0, keepdims=True)
-    partner = jnp.where(lax.axis_index("dp") // PAIR == 0, uniform, lower_policy)
+    logits, policy, log_policy = policy_rows(mine_ref[:PAD] + swapped(theirs_ref[:PAD]), legal)
+    if lower is None:
+        partner = legal / jnp.sum(legal, axis=0, keepdims=True)
+    else:
+        partner = policy_rows(lower, legal)[1]
     target = 0.5 * onehot + 0.5 * partner
     loss = -jnp.sum(target * log_policy, axis=0, keepdims=True)
     loss_ref[...] = loss[:, :rows]
@@ -431,17 +433,50 @@
         copy.wait()
 
 
-def gradient(mine, theirs, wide, own_pool, peer_pool):
-    _, _, rows, half = own_pool.shape
+def lowest_grad_kernel(
+    mine_ref, theirs_ref, wide_ref, own_ref, peer_ref, out_ref, loss_ref, out_buf, sems
+):
+    @pl.when(lax.axis_index("dp") // PAIR == 0)
+    def _():
+        grad_into(
+            out_ref, loss_ref, out_buf, sems,
+            mine_ref, theirs_ref, wide_ref, own_ref, peer_ref, None,
+        )
+
+
+def upper_grad_kernel(
+    mine_ref, theirs_ref, wide_ref, own_ref, peer_ref,
+    lower_ref, lower_theirs_ref, lowest_ref, lowest_loss_ref,
+    out_ref, loss_ref, out_buf, sems,
+):
+    level = lax.axis_index("dp") // PAIR
+
+    @pl.when(level == 0)
+    def _():
+        loss_ref[...] = lowest_loss_ref[...]
+
+    @pl.when(level > 0)
+    def _():
+        grad_into(
+            out_ref, loss_ref, out_buf, sems,
+            mine_ref, theirs_ref, wide_ref, own_ref, peer_ref,
+            lower_ref[...] + swapped(lower_theirs_ref[...]),
+        )
+
+
+def gradient(kernel, operands, into):
+    _, _, rows, half = operands[3].shape
     width = H * DH
+    count = len(operands)
     return pl.pallas_call(
-        grad_kernel,
-        in_specs=[IN_VMEM] * 5,
+        kernel,
+        in_specs=[IN_VMEM] * count + ([IN_HBM, IN_VMEM] if into else []),
         out_specs=[IN_HBM, IN_VMEM],
         out_shape=[
             jax.ShapeDtypeStruct((half, width), F32),
             jax.ShapeDtypeStruct((1, rows), F32),
         ],
+        input_output_aliases={count: 0} if into else {},
         scratch_shapes=[
             pltpu.VMEM((half, width), F32),
             pltpu.SemaphoreType.DMA((GRAD_CHUNKS,)),
@@ -452,7 +487,12 @@
             bytes_accessed=4 * half * width + 4 * rows * H * half,
             transcendentals=0,
         ),
-    )(mine, theirs, wide, own_pool, peer_pool)
+    )(*operands, *into)
+
+
+def rotated(block, axis, distance):
+    count = lax.axis_size(axis)
+    return lax.ppermute(block, axis, [(i, (i + distance) % count) for i in range(count)])
 
 
 def paired_device(
@@ -462,17 +502,20 @@
     peer_tokens = partner_2(tokens, "dp", 0)
     spread = head_spread(jnp.transpose(head_prior, (1, 0, 2)))
     prior_map = prior_fold(spread, value_prior)
-    lower_map = shifted(prior_map, "dp", PAIR)
+    lower_map = rotated(prior_map, "dp", PAIR)
     own_pool, own_map, wide = own_side(
         tokens, query_weight, query_prior, jnp.transpose(policy_head, (1, 0, 2)), value_weight
     )
-    peer_pool, raw = peer_side(peer_tokens, query_weight, query_prior, own_map, own_pool)
-    mine = raw_call(
-        lower_raw_kernel, 3 * PAD,
-        lower_map, own_pool, peer_pool, raw, legal_moves.T, action_label.reshape(1, -1),
+    peer_pool, mine = peer_side(
+        peer_tokens, query_weight, query_prior, own_map, own_pool,
+        legal_moves.T, action_label.reshape(1, -1),
     )
     theirs = partner_2(mine, "dp", 0)
-    weight_grad, row_loss = gradient(mine, theirs, wide, own_pool, peer_pool)
+    operands = [mine, theirs, wide, own_pool, peer_pool]
+    lowest = gradient(lowest_grad_kernel, operands, [])
+    lower = lower_raw(lower_map, own_pool, peer_pool, lowest[1])
+    lower_theirs = partner_2(lower, "dp", 0)
+    weight_grad, row_loss = gradient(upper_grad_kernel, operands + [lower, lower_theirs], lowest)
     return weight_grad, row_loss.reshape(-1)
 
 

time: 22.5 us -> 20.6 us (0.916)
  the two profiles are of different devices: /device:TPU:25 before, /device:TPU:0 now
where the time goes in v5:
time: 20.6 us; the launch traced here: 20.5 us
  Pallas kernels  12.9 us (63%)
  starting transfers between devices  3.45 us (17%)
  waiting for transfers between devices  3 us (15%)
  between operations  0.75 us (4%)
  local copies, waits for them, and re-layouts  0.4 us (2%)
    pallas_call x1, Pallas kernels, peer_side(): pl.pallas_call(peer_kernel, in_specs=[IN_VMEM] * 7, out_specs=[IN_VMEM] *...  3.63 us
    pallas_call x2, Pallas kernels, gradient(): pl.pallas_call(kernel, in_specs=[IN_VMEM] * count + ([IN_HBM, IN_VMEM] if...  3.34 us
    pallas_call x1, Pallas kernels, own_side(): pl.pallas_call(own_kernel, in_specs=[IN_VMEM] * 5, out_specs=[IN_VMEM] *...  2.8 us
    ppermute x1, starting transfers between devices, rotated(): lax.ppermute(block, axis, [(i, (i + distance) % count) for i in range(cou...  2.58 us
    ppermute x3, waiting for transfers between devices, partner_2(): return lax.ppermute(block, axis, route)  2.15 us
    pallas_call x1, Pallas kernels, head_spread(): pl.pallas_call(spread_kernel, in_specs=[IN_HBM], out_specs=IN_VMEM, out_s...  1.41 us
    pallas_call x1, Pallas kernels, prior_fold(): pl.pallas_call(prior_kernel, in_specs=[IN_VMEM, IN_VMEM], out_specs=IN_VM...  0.88 us
    ppermute x3, starting transfers between devices, partner_2(): return lax.ppermute(block, axis, route)  0.87 us
  transfers between devices with their start and end apart: 4, of which 3 were waited for; matrix products, arithmetic and copies ran while one was open for 0% of the time, Pallas kernels for 56%

profile of v5, /device:TPU:0, one launch (start us, length us, event | category | flops | bytes accessed | tf_op | source)
XLA Modules:
  0.0 20.5 jit_solution(12493720937260545258)
XLA Ops:
  0.6 0.5 %collective-permute-start = (bf16[1024,2048]{1,0:T(8,128)(2,1)}, bf16[1024,2048]{1,0:T(8,128)(2,1)S(1)}, u32[]{:S(2)}, u32[]{:S(2)}) collective-permute-start(bf16[1024,2048]{1,0:T(8,128)(2,1)} %tokens_ref.1), channel_id=1, source_target_pairs={{0,1},{1,0},{2,3},{3,2},{4,5},{5,4},{6,7},{7,6},{8,9},{9,8},{10,11... | collective-permute-start | bytes 12582920 | tf_op jit(solution)/shard_map/ppermute | solution.py:23
  1.1 1.4 %shard_map.106.spread_ref = bf16[320,1024]{1,0:T(8,128)(2,1)S(1)} custom-call(f32[20,8,1024]{2,1,0:T(8,128)} %bitcast.8), custom_call_target="tpu_custom_call" | custom-call | flops 16384000000 | bytes 655360 | tf_op jit(solution)/shard_map/pallas_call | solution.py:214
  2.6 0.4 %copy-done.7 = bf16[1024,1024]{1,0:T(8,128)(2,1)S(1)} copy-done((bf16[1024,1024]{1,0:T(8,128)(2,1)S(1)}, bf16[1024,1024]{1,0:T(8,128)(2,1)}, u32[]{:S(2)}) %copy-start.7) | copy-done | bytes 2097176
  2.9 0.0 copy-start.4
  3.0 0.9 %shard_map.107 = bf16[160,1024]{1,0:T(8,128)(2,1)S(1)} custom-call(bf16[320,1024]{1,0:T(8,128)(2,1)S(1)} %shard_map.106.spread_ref, bf16[1024,1024]{1,0:T(8,128)(2,1)S(1)} %copy-done.7), custom_call_target="tpu_custom_call" | custom-call | flops 6710886400 | bytes 2097152 | tf_op jit(solution)/shard_map/pallas_call | solution.py:229
  3.8 0.0 copy-start.5
  3.9 0.0 copy-start.6
  3.9 2.6 %collective-permute-start.2 = (bf16[160,1024]{1,0:T(8,128)(2,1)S(1)}, bf16[160,1024]{1,0:T(8,128)(2,1)S(1)}, u32[]{:S(2)}, u32[]{:S(2)}) collective-permute-start(bf16[160,1024]{1,0:T(8,128)(2,1)S(1)} %shard_map.107), channel_id=1, source_target_pairs={{0,2},{1,3},{2,4},{3,5},{4,6},{5,7},{6,8},{7,9},{8,10},{9,11},{10,... | collective-permute-start | bytes 983048 | tf_op jit(solution)/shard_map/ppermute | solution.py:495
  6.5 0.0 copy-done
  6.5 0.0 copy-done.1
  6.5 0.0 copy-done.2
  6.5 0.0 copy-done.3
  6.5 0.0 copy-done.4
  6.5 2.8 %shard_map.104 = (bf16[2,8,64,1024]{3,2,1,0:T(8,128)(2,1)S(1)}, bf16[320,1024]{1,0:T(8,128)(2,1)S(1)}, bf16[192,1024]{1,0:T(8,128)(2,1)S(1)}) custom-call(bf16[1024,2048]{1,0:T(8,128)(2,1)S(1)} %copy-done, bf16[8,8,2048]{2,1,0:T(8,128)(2,1)S(1)} %copy-done.2, bf16[8,8,2048]{2,1,0:T(8,128)(2,1)S(1)} %copy-done.3, f32[20,8,1024]{2,1,0:T(8,128)S(1)} %bitcast.5, ...), custom_call_target="tpu_custom_call" | custom-call | flops 603979776 | bytes 8388608 | tf_op jit(solution)/shard_map/pallas_call | solution.py:297
  9.3 0.0 collective-permute-done.tokens_ref
  9.3 3.6 %shard_map.105 = (bf16[2,8,64,1024]{3,2,1,0:T(8,128)(2,1)S(1)}, f32[48,128]{1,0:T(8,128)S(1)}) custom-call(bf16[1024,2048]{1,0:T(8,128)(2,1)S(1)} %collective-permute-done.tokens_ref, bf16[8,8,2048]{2,1,0:T(8,128)(2,1)S(1)} %copy-done.2, bf16[8,8,2048]{2,1,0:T(8,128)(2,1)S(1)} %copy-done.3, bf16[320,1024]{1,0:T(8,128)(2,1)S(1)} %get-tuple-element.11.map_ref, ...), custom_call_target="tpu_custom_call" | custom-call | flops 603979776 | bytes 6291456 | tf_op jit(solution)/shard_map/pallas_call | solution.py:331
  12.9 0.3 %collective-permute-start.1 = (f32[48,128]{1,0:T(8,128)S(1)}, f32[48,128]{1,0:T(8,128)S(1)}, u32[]{:S(2)}, u32[]{:S(2)}) collective-permute-start(f32[48,128]{1,0:T(8,128)S(1)} %get-tuple-element.13.mine_ref), channel_id=1, source_target_pairs={{0,1},{1,0},{2,3},{3,2},{4,5},{5,4},{6,7},{7,6},{8,9},{9,8},{10,11... | collective-permute-start | bytes 73736 | tf_op jit(solution)/shard_map/ppermute | solution.py:23
  13.2 1.0 %collective-permute-done.1.theirs_ref = f32[48,128]{1,0:T(8,128)S(1)} collective-permute-done((f32[48,128]{1,0:T(8,128)S(1)}, f32[48,128]{1,0:T(8,128)S(1)}, u32[]{:S(2)}, u32[]{:S(2)}) %collective-permute-start.1) | collective-permute-done | bytes 24608 | tf_op jit(solution)/shard_map/ppermute | solution.py:23
  14.2 2.8 %shard_map.108 = (f32[1024,1024]{1,0:T(8,128)}, f32[1,64]{1,0:T(1,128)S(1)}) custom-call(f32[48,128]{1,0:T(8,128)S(1)} %get-tuple-element.13.mine_ref, f32[48,128]{1,0:T(8,128)S(1)} %collective-permute-done.1.theirs_ref, bf16[192,1024]{1,0:T(8,128)(2,1)S(1)} %get-tuple-element.14.wide_ref, bf16[2,8,64,1024]{3,2,1,0:T(8,128)(2,1)S(1)} %get-tuple-element.12.own_ref, ...), custom_call_target="tpu_custom_call" | custom-call | flops 402653184 | bytes 6291456 | tf_op jit(solution)/shard_map/pallas_call | solution.py:471
  17.0 0.8 %collective-permute-done.2.map_ref = bf16[160,1024]{1,0:T(8,128)(2,1)S(1)} collective-permute-done((bf16[160,1024]{1,0:T(8,128)(2,1)S(1)}, bf16[160,1024]{1,0:T(8,128)(2,1)S(1)}, u32[]{:S(2)}, u32[]{:S(2)}) %collective-permute-start.2) | collective-permute-done | bytes 327712 | tf_op jit(solution)/shard_map/ppermute | solution.py:495
  17.9 0.8 %shard_map.109.lower_ref = f32[24,128]{1,0:T(8,128)S(1)} custom-call(bf16[160,1024]{1,0:T(8,128)(2,1)S(1)} %collective-permute-done.2.map_ref, bf16[2,8,64,1024]{3,2,1,0:T(8,128)(2,1)S(1)} %get-tuple-element.12.own_ref, bf16[2,8,64,1024]{3,2,1,0:T(8,128)(2,1)S(1)} %get-tuple-element.15.peer_ref, f32[1,64]{1,0:T(1,128)S(1)} %get-tuple-element.16.earlier_ref.lowest_loss_ref), custom_call_target="tpu_custom_call" | custom-call | flops 67108864 | bytes 2097152 | tf_op jit(solution)/shard_map/pallas_call | solution.py:377
  18.7 0.1 collective-permute-start.3
  18.7 1.2 %collective-permute-done.3.lower_theirs_ref = f32[24,128]{1,0:T(8,128)S(1)} collective-permute-done((f32[24,128]{1,0:T(8,128)S(1)}, f32[24,128]{1,0:T(8,128)S(1)}, u32[]{:S(2)}, u32[]{:S(2)}) %collective-permute-start.3) | collective-permute-done | bytes 12320 | tf_op jit(solution)/shard_map/ppermute | solution.py:23
  19.9 0.5 %shard_map.110 = (f32[1024,1024]{1,0:T(8,128)}, f32[1,64]{1,0:T(1,128)}) custom-call(f32[48,128]{1,0:T(8,128)S(1)} %get-tuple-element.13.mine_ref, f32[48,128]{1,0:T(8,128)S(1)} %collective-permute-done.1.theirs_ref, bf16[192,1024]{1,0:T(8,128)(2,1)S(1)} %get-tuple-element.14.wide_ref, ...), custom_call_target="tpu_custom_call", output_to_operand_aliasing={{0}: (7, {})} | custom-call | flops 402653184 | bytes 6291456 | tf_op jit(solution)/shard_map/pallas_call | solution.py:471
  (7 shorter events, 0.0 us)
Async XLA Ops:
  0.6 8.7 %collective-permute-start = (bf16[1024,2048]{1,0:T(8,128)(2,1)}, bf16[1024,2048]{1,0:T(8,128)(2,1)S(1)}, u32[]{:S(2)}, u32[]{:S(2)}) collective-permute-start(bf16[1024,2048]{1,0:T(8,128)(2,1)} %tokens_ref.1), channel_id=1, source_target_pairs={{0,1},{1,0},{2,3},{3,2},{4,5},{5,4},{6,7},{7,6},{8,9},{9,8},{10,11... | collective-permute-start | bytes 12582920 | tf_op jit(solution)/shard_map/ppermute | solution.py:23
  1.1 1.8 %copy-start.7 = (bf16[1024,1024]{1,0:T(8,128)(2,1)S(1)}, bf16[1024,1024]{1,0:T(8,128)(2,1)}, u32[]{:S(2)}) copy-start(bf16[1024,1024]{1,0:T(8,128)(2,1)} %proj_ref.3) | copy-start | bytes 6291460
  2.9 3.5 %copy-start = (bf16[1024,2048]{1,0:T(8,128)(2,1)S(1)}, bf16[1024,2048]{1,0:T(8,128)(2,1)}, u32[]{:S(2)}) copy-start(bf16[1024,2048]{1,0:T(8,128)(2,1)} %tokens_ref.1) | copy-start | bytes 12582916
  2.9 3.5 %copy-start.1 = (bf16[1024,1024]{1,0:T(8,128)(2,1)S(1)}, bf16[1024,1024]{1,0:T(8,128)(2,1)}, u32[]{:S(2)}) copy-start(bf16[1024,1024]{1,0:T(8,128)(2,1)} %proj_ref.2) | copy-start | bytes 6291460
  2.9 3.5 %copy-start.2 = (bf16[8,8,2048]{2,1,0:T(8,128)(2,1)S(1)}, bf16[8,8,2048]{2,1,0:T(8,128)(2,1)}, u32[]{:S(2)}) copy-start(bf16[8,8,2048]{2,1,0:T(8,128)(2,1)} %query_ref.3) | copy-start | bytes 786436
  2.9 3.5 %copy-start.3 = (bf16[8,8,2048]{2,1,0:T(8,128)(2,1)S(1)}, bf16[8,8,2048]{2,1,0:T(8,128)(2,1)}, u32[]{:S(2)}) copy-start(bf16[8,8,2048]{2,1,0:T(8,128)(2,1)} %prior_ref.3) | copy-start | bytes 786436
  2.9 3.5 %copy-start.4 = (f32[8,20,1024]{2,0,1:T(8,128)S(1)}, f32[8,20,1024]{2,0,1:T(8,128)}, u32[]{:S(2)}) copy-start(f32[8,20,1024]{2,0,1:T(8,128)} %param.16) | copy-start | bytes 1966084
  3.8 5.4 %copy-start.5 = (s32[64,20]{0,1:T(8,128)S(1)}, s32[64,20]{0,1:T(8,128)}, u32[]{:S(2)}) copy-start(s32[64,20]{0,1:T(8,128)} %param.10) | copy-start | bytes 15364
  3.9 5.4 %copy-start.6 = (s32[64]{0:T(128)S(1)}, s32[64]{0:T(128)}, u32[]{:S(2)}) copy-start(s32[64]{0:T(128)} %param.11) | copy-start | bytes 772
  3.9 14.0 %collective-permute-start.2 = (bf16[160,1024]{1,0:T(8,128)(2,1)S(1)}, bf16[160,1024]{1,0:T(8,128)(2,1)S(1)}, u32[]{:S(2)}, u32[]{:S(2)}) collective-permute-start(bf16[160,1024]{1,0:T(8,128)(2,1)S(1)} %shard_map.107), channel_id=1, source_target_pairs={{0,2},{1,3},{2,4},{3,5},{4,6},{5,7},{6,8},{7,9},{8,10},{9,11},{10,... | collective-permute-start | bytes 983048 | tf_op jit(solution)/shard_map/ppermute | solution.py:495
  12.9 1.3 %collective-permute-start.1 = (f32[48,128]{1,0:T(8,128)S(1)}, f32[48,128]{1,0:T(8,128)S(1)}, u32[]{:S(2)}, u32[]{:S(2)}) collective-permute-start(f32[48,128]{1,0:T(8,128)S(1)} %get-tuple-element.13.mine_ref), channel_id=1, source_target_pairs={{0,1},{1,0},{2,3},{3,2},{4,5},{5,4},{6,7},{7,6},{8,9},{9,8},{10,11... | collective-permute-start | bytes 73736 | tf_op jit(solution)/shard_map/ppermute | solution.py:23
  18.7 1.2 %collective-permute-start.3 = (f32[24,128]{1,0:T(8,128)S(1)}, f32[24,128]{1,0:T(8,128)S(1)}, u32[]{:S(2)}, u32[]{:S(2)}) collective-permute-start(f32[24,128]{1,0:T(8,128)S(1)} %shard_map.109.lower_ref), channel_id=1, source_target_pairs={{0,1},{1,0},{2,3},{3,2},{4,5},{5,4},{6,7},{7,6},{8,9},{9,8},{10,11... | collective-permute-start | bytes 36872 | tf_op jit(solution)/shard_map/ppermute | solution.py:23

commit v6 on v5

--- a/solution.py
+++ b/solution.py
@@ -174,13 +174,15 @@
     return jnp.concatenate(pieces, axis=0)
 
 
-def spread_into(spread_ref, head_ref):
+def level_head(head_ref):
     level = lax.axis_index("dp") // PAIR
-    head = head_ref[:, pl.ds(level, 1), :].reshape(A, H * DH)
+    return head_ref[:, pl.ds(level, 1), :].reshape(A, H * DH)
+
+
+def spread_into(spread_ref, head):
     high, low = split_high(spread_heads(head))
     spread_ref[:SPREAD, :] = high
     spread_ref[SPREAD:, :] = low
-    return head
 
 
 def fold_into(out_ref, proj_ref, spread_ref, parts):
@@ -195,10 +197,11 @@
 
 
 def spread_kernel(head_ref, spread_ref, head_buf, sem):
-    copy = pltpu.make_async_copy(head_ref, head_buf, sem)
+    level = lax.axis_index("dp") // PAIR
+    copy = pltpu.make_async_copy(head_ref.at[:, pl.ds(level, 1)], head_buf, sem)
     copy.start()
     copy.wait()
-    spread_into(spread_ref, head_buf)
+    spread_into(spread_ref, head_buf[...].reshape(A, H * DH))
 
 
 def prior_kernel(spread_ref, proj_ref, out_ref):
@@ -216,7 +219,7 @@
         in_specs=[IN_HBM],
         out_specs=IN_VMEM,
         out_shape=jax.ShapeDtypeStruct((2 * SPREAD, width), BF16),
-        scratch_shapes=[pltpu.VMEM(head_t.shape, F32), pltpu.SemaphoreType.DMA],
+        scratch_shapes=[pltpu.VMEM((A, 1, width), F32), pltpu.SemaphoreType.DMA],
         compiler_params=pltpu.CompilerParams(vmem_limit_bytes=SPREAD_MIB * MIB),
         cost_estimate=pl.CostEstimate(
             flops=SPREAD_COST * SPREAD * width, bytes_accessed=4 * head_t.size, transcendentals=0
@@ -282,7 +285,8 @@
 def own_kernel(
     tokens_ref, query_ref, prior_ref, head_ref, proj_ref, pool_ref, map_ref, wide_ref, spread_ref
 ):
-    head = spread_into(spread_ref, head_ref)
+    head = level_head(head_ref)
+    spread_into(spread_ref, head)
     fold_into(map_ref, proj_ref, spread_ref, 2)
     head = jnp.concatenate([head, jnp.zeros((PAD - A, H * DH), F32)], axis=0)
     lane_head = lax.broadcasted_iota(jnp.int32, (PAD, H * DH), 1) >> DH_BITS
@@ -369,7 +373,15 @@
 
 
 def lower_kernel(map_ref, own_ref, peer_ref, earlier_ref, out_ref):
-    out_ref[...] = raw_sums([map_ref[...]], [own_ref, peer_ref], 1)
+    level = lax.axis_index("dp") // PAIR
+
+    @pl.when(level == 0)
+    def _():
+        out_ref[...] = jnp.zeros_like(out_ref)
+
+    @pl.when(level > 0)
+    def _():
+        out_ref[...] = raw_sums([map_ref[...]], [own_ref, peer_ref], 1)
 
 
 def lower_raw(lower_map, own_pool, peer_pool, earlier):
@@ -386,11 +398,17 @@
     )(lower_map, own_pool, peer_pool, earlier)
 
 
-def policy_rows(raw, legal):
-    logits = 30.0 * jnp.tanh(raw / 30.0)
-    exp_logits = jnp.exp(logits) * legal
-    partition = jnp.sum(exp_logits, axis=0, keepdims=True)
-    return logits, exp_logits / partition, logits - jnp.log(partition)
+def policy_rows(raws, legal):
+    squashed = jnp.tanh(jnp.concatenate(raws, axis=0) * (1.0 / 30.0))
+    logits = 30.0 * squashed
+    exp_logits = jnp.exp(logits)
+    found = []
+    for i in range(len(raws)):
+        rows = slice(i * PAD, (i + 1) * PAD)
+        weights = exp_logits[rows] * legal
+        partition = jnp.sum(weights, axis=0, keepdims=True)
+        found.append((squashed[rows], logits[rows], weights * (1.0 / partition), partition))
+    return found
 
 
 def swapped(theirs):
@@ -398,21 +416,26 @@
     return jnp.concatenate([theirs[:, rows:], theirs[:, :rows]], axis=1)
 
 
-def grad_into(out_ref, loss_ref, out_buf, sems, mine_ref, theirs_ref, wide_ref, own_ref, peer_ref, lower):
+def grad_into(out_ref, loss_ref, out_buf, loss_buf, sems, mine_ref, theirs_ref, wide_ref, own_ref, peer_ref, lower):
     rows = own_ref.shape[2]
     told = jnp.concatenate([mine_ref[PAD:, :rows], theirs_ref[PAD:, :rows]], axis=1)
     move = lax.broadcasted_iota(jnp.int32, told.shape, 0)
     legal = jnp.where(move < A, told, 0.0)
     onehot = (move.astype(F32) == told[A : A + 1]).astype(F32)
-    logits, policy, log_policy = policy_rows(mine_ref[:PAD] + swapped(theirs_ref[:PAD]), legal)
-    if lower is None:
-        partner = legal / jnp.sum(legal, axis=0, keepdims=True)
+    raws = [mine_ref[:PAD] + swapped(theirs_ref[:PAD])] + lower
+    found = policy_rows(raws, legal)
+    squashed, logits, policy, partition = found[0]
+    if lower:
+        partner = found[1][2]
     else:
-        partner = policy_rows(lower, legal)[1]
+        partner = legal * (1.0 / jnp.sum(legal, axis=0, keepdims=True))
     target = 0.5 * onehot + 0.5 * partner
+    log_policy = logits - jnp.log(partition)
     loss = -jnp.sum(target * log_policy, axis=0, keepdims=True)
-    loss_ref[...] = loss[:, :rows]
-    logit_grad = (policy - target) * (1.0 - (logits / 30.0) ** 2)
+    loss_buf[...] = loss[:, :rows]
+    loss_copy = pltpu.make_async_copy(loss_buf, loss_ref, sems.at[GRAD_CHUNKS])
+    loss_copy.start()
+    logit_grad = (policy - target) * (1.0 - squashed * squashed)
     high, low = split_high(logit_grad)
     left = jnp.concatenate([high.astype(F32), low.astype(F32)], axis=0).astype(BF16)
     chunk = out_buf.shape[0] // GRAD_CHUNKS
@@ -429,38 +452,35 @@
         part = pl.ds(i * chunk, chunk)
         copies.append(pltpu.make_async_copy(out_buf.at[part], out_ref.at[part], sems.at[i]))
         copies[i].start()
-    for copy in copies:
+    for copy in copies + [loss_copy]:
         copy.wait()
 
 
 def lowest_grad_kernel(
-    mine_ref, theirs_ref, wide_ref, own_ref, peer_ref, out_ref, loss_ref, out_buf, sems
+    mine_ref, theirs_ref, wide_ref, own_ref, peer_ref,
+    out_ref, loss_ref, token_ref, out_buf, loss_buf, sems,
 ):
+    token_ref[...] = jnp.zeros_like(token_ref)
+
     @pl.when(lax.axis_index("dp") // PAIR == 0)
     def _():
         grad_into(
-            out_ref, loss_ref, out_buf, sems,
-            mine_ref, theirs_ref, wide_ref, own_ref, peer_ref, None,
+            out_ref, loss_ref, out_buf, loss_buf, sems,
+            mine_ref, theirs_ref, wide_ref, own_ref, peer_ref, [],
         )
 
 
 def upper_grad_kernel(
     mine_ref, theirs_ref, wide_ref, own_ref, peer_ref,
     lower_ref, lower_theirs_ref, lowest_ref, lowest_loss_ref,
-    out_ref, loss_ref, out_buf, sems,
+    out_ref, loss_ref, out_buf, loss_buf, sems,
 ):
-    level = lax.axis_index("dp") // PAIR
-
-    @pl.when(level == 0)
-    def _():
-        loss_ref[...] = lowest_loss_ref[...]
-
-    @pl.when(level > 0)
+    @pl.when(lax.axis_index("dp") // PAIR > 0)
     def _():
         grad_into(
-            out_ref, loss_ref, out_buf, sems,
+            out_ref, loss_ref, out_buf, loss_buf, sems,
             mine_ref, theirs_ref, wide_ref, own_ref, peer_ref,
-            lower_ref[...] + swapped(lower_theirs_ref[...]),
+            [lower_ref[...] + swapped(lower_theirs_ref[...])],
         )
 
 
@@ -470,16 +490,18 @@
     count = len(operands)
     return pl.pallas_call(
         kernel,
-        in_specs=[IN_VMEM] * count + ([IN_HBM, IN_VMEM] if into else []),
-        out_specs=[IN_HBM, IN_VMEM],
+        in_specs=[IN_VMEM] * count + [IN_HBM] * len(into),
+        out_specs=[IN_HBM, IN_HBM] + ([] if into else [IN_VMEM]),
         out_shape=[
             jax.ShapeDtypeStruct((half, width), F32),
             jax.ShapeDtypeStruct((1, rows), F32),
-        ],
-        input_output_aliases={count: 0} if into else {},
+        ]
+        + ([] if into else [jax.ShapeDtypeStruct((8, DH), F32)]),
+        input_output_aliases={count + i: i for i in range(len(into))},
         scratch_shapes=[
             pltpu.VMEM((half, width), F32),
-            pltpu.SemaphoreType.DMA((GRAD_CHUNKS,)),
+            pltpu.VMEM((1, rows), F32),
+            pltpu.SemaphoreType.DMA((GRAD_CHUNKS + 1,)),
         ],
         compiler_params=pltpu.CompilerParams(vmem_limit_bytes=16 * MIB),
         cost_estimate=pl.CostEstimate(
@@ -512,8 +534,8 @@
     )
     theirs = partner_2(mine, "dp", 0)
     operands = [mine, theirs, wide, own_pool, peer_pool]
-    lowest = gradient(lowest_grad_kernel, operands, [])
-    lower = lower_raw(lower_map, own_pool, peer_pool, lowest[1])
+    *lowest, token = gradient(lowest_grad_kernel, operands, [])
+    lower = lower_raw(lower_map, own_pool, peer_pool, token)
     lower_theirs = partner_2(lower, "dp", 0)
     weight_grad, row_loss = gradient(upper_grad_kernel, operands + [lower, lower_theirs], lowest)
     return weight_grad, row_loss.reshape(-1)

time: 20.6 us -> 19.7 us (0.956)
  the two profiles are of different devices: /device:TPU:0 before, /device:TPU:25 now
where the time goes in v6:
time: 19.7 us; the launch traced here: 19.5 us
  Pallas kernels  12.1 us (61%)
  starting transfers between devices  2.98 us (15%)
  waiting for transfers between devices  2.33 us (12%)
  local copies, waits for them, and re-layouts  1.33 us (7%)
  between operations  0.73 us (4%)
    pallas_call x1, Pallas kernels, peer_side(): pl.pallas_call(peer_kernel, in_specs=[IN_VMEM] * 7, out_specs=[IN_VMEM] *...  3.63 us
    pallas_call x2, Pallas kernels, gradient(): pl.pallas_call(kernel, in_specs=[IN_VMEM] * count + [IN_HBM] * len(into),...  2.84 us
    pallas_call x1, Pallas kernels, own_side(): pl.pallas_call(own_kernel, in_specs=[IN_VMEM] * 5, out_specs=[IN_VMEM] *...  2.8 us
    ppermute x3, waiting for transfers between devices, partner_2(): return lax.ppermute(block, axis, route)  2.01 us
    ppermute x3, starting transfers between devices, partner_2(): return lax.ppermute(block, axis, route)  1.69 us
    unnamed x16, local copies, waits for them, and re-layouts  1.33 us
    ppermute x1, starting transfers between devices, rotated(): lax.ppermute(block, axis, [(i, (i + distance) % count) for i in range(cou...  1.29 us
    pallas_call x1, Pallas kernels, head_spread(): pl.pallas_call(spread_kernel, in_specs=[IN_HBM], out_specs=IN_VMEM, out_s...  1.19 us
  transfers between devices with their start and end apart: 4, of which 3 were waited for; matrix products, arithmetic and copies ran while one was open for 0% of the time, Pallas kernels for 44%

profile of v6, /device:TPU:25, one launch (start us, length us, event | category | flops | bytes accessed | tf_op | source)
XLA Modules:
  0.0 19.5 jit_solution(1351217913797107583)
XLA Ops:
  0.6 0.7 %collective-permute-start = (bf16[1024,2048]{1,0:T(8,128)(2,1)}, bf16[1024,2048]{1,0:T(8,128)(2,1)S(1)}, u32[]{:S(2)}, u32[]{:S(2)}) collective-permute-start(bf16[1024,2048]{1,0:T(8,128)(2,1)} %tokens_ref.1), channel_id=1, source_target_pairs={{0,1},{1,0},{2,3},{3,2},{4,5},{5,4},{6,7},{7,6},{8,9},{9,8},{10,11... | collective-permute-start | bytes 12582920 | tf_op jit(solution)/shard_map/ppermute | solution.py:23
  1.4 1.2 %shard_map.106.spread_ref = bf16[320,1024]{1,0:T(8,128)(2,1)S(1)} custom-call(f32[20,8,1024]{2,1,0:T(8,128)} %bitcast.9), custom_call_target="tpu_custom_call" | custom-call | flops 16384000000 | bytes 655360 | tf_op jit(solution)/shard_map/pallas_call | solution.py:217
  2.6 0.4 %copy-done.7 = bf16[1024,1024]{1,0:T(8,128)(2,1)S(1)} copy-done((bf16[1024,1024]{1,0:T(8,128)(2,1)S(1)}, bf16[1024,1024]{1,0:T(8,128)(2,1)}, u32[]{:S(2)}) %copy-start.7) | copy-done | bytes 2097176
  3.0 0.0 copy-start.4
  3.0 0.9 %shard_map.107 = bf16[160,1024]{1,0:T(8,128)(2,1)S(1)} custom-call(bf16[320,1024]{1,0:T(8,128)(2,1)S(1)} %shard_map.106.spread_ref, bf16[1024,1024]{1,0:T(8,128)(2,1)S(1)} %copy-done.7), custom_call_target="tpu_custom_call" | custom-call | flops 6710886400 | bytes 2097152 | tf_op jit(solution)/shard_map/pallas_call | solution.py:232
  3.9 0.0 copy-start.5
  3.9 0.0 copy-start.6
  3.9 1.3 %collective-permute-start.2 = (bf16[160,1024]{1,0:T(8,128)(2,1)S(1)}, bf16[160,1024]{1,0:T(8,128)(2,1)S(1)}, u32[]{:S(2)}, u32[]{:S(2)}) collective-permute-start(bf16[160,1024]{1,0:T(8,128)(2,1)S(1)} %shard_map.107), channel_id=1, source_target_pairs={{0,2},{1,3},{2,4},{3,5},{4,6},{5,7},{6,8},{7,9},{8,10},{9,11},{10,... | collective-permute-start | bytes 983048 | tf_op jit(solution)/shard_map/ppermute | solution.py:517
  5.2 0.0 copy-done
  5.2 0.6 %copy-done.1 = bf16[1024,1024]{1,0:T(8,128)(2,1)S(1)} copy-done((bf16[1024,1024]{1,0:T(8,128)(2,1)S(1)}, bf16[1024,1024]{1,0:T(8,128)(2,1)}, u32[]{:S(2)}) %copy-start.1) | copy-done | bytes 2097176
  5.9 0.0 copy-done.3
  5.9 0.2 %copy-done.4 = f32[8,20,1024]{2,0,1:T(8,128)S(1)} copy-done((f32[8,20,1024]{2,0,1:T(8,128)S(1)}, f32[8,20,1024]{2,0,1:T(8,128)}, u32[]{:S(2)}) %copy-start.4) | copy-done | bytes 655384
  6.1 2.8 %shard_map.104 = (bf16[2,8,64,1024]{3,2,1,0:T(8,128)(2,1)S(1)}, bf16[320,1024]{1,0:T(8,128)(2,1)S(1)}, bf16[192,1024]{1,0:T(8,128)(2,1)S(1)}) custom-call(bf16[1024,2048]{1,0:T(8,128)(2,1)S(1)} %copy-done, bf16[8,8,2048]{2,1,0:T(8,128)(2,1)S(1)} %copy-done.2, bf16[8,8,2048]{2,1,0:T(8,128)(2,1)S(1)} %copy-done.3, f32[20,8,1024]{2,1,0:T(8,128)S(1)} %bitcast.5, ...), custom_call_target="tpu_custom_call" | custom-call | flops 603979776 | bytes 8388608 | tf_op jit(solution)/shard_map/pallas_call | solution.py:301
  8.9 0.0 collective-permute-done.tokens_ref
  8.9 0.0 copy-done.5
  8.9 0.0 copy-done.6
  8.9 3.6 %shard_map.105 = (bf16[2,8,64,1024]{3,2,1,0:T(8,128)(2,1)S(1)}, f32[48,128]{1,0:T(8,128)S(1)}) custom-call(bf16[1024,2048]{1,0:T(8,128)(2,1)S(1)} %collective-permute-done.tokens_ref, bf16[8,8,2048]{2,1,0:T(8,128)(2,1)S(1)} %copy-done.2, bf16[8,8,2048]{2,1,0:T(8,128)(2,1)S(1)} %copy-done.3, bf16[320,1024]{1,0:T(8,128)(2,1)S(1)} %get-tuple-element.12.map_ref, ...), custom_call_target="tpu_custom_call" | custom-call | flops 603979776 | bytes 6291456 | tf_op jit(solution)/shard_map/pallas_call | solution.py:335
  12.6 0.1 collective-permute-start.1
  12.7 1.2 %collective-permute-done.1.theirs_ref = f32[48,128]{1,0:T(8,128)S(1)} collective-permute-done((f32[48,128]{1,0:T(8,128)S(1)}, f32[48,128]{1,0:T(8,128)S(1)}, u32[]{:S(2)}, u32[]{:S(2)}) %collective-permute-start.1) | collective-permute-done | bytes 24608 | tf_op jit(solution)/shard_map/ppermute | solution.py:23
  13.9 0.3 %collective-permute-done.2.map_ref = bf16[160,1024]{1,0:T(8,128)(2,1)S(1)} collective-permute-done((bf16[160,1024]{1,0:T(8,128)(2,1)S(1)}, bf16[160,1024]{1,0:T(8,128)(2,1)S(1)}, u32[]{:S(2)}, u32[]{:S(2)}) %collective-permute-start.2) | collective-permute-done | bytes 327712 | tf_op jit(solution)/shard_map/ppermute | solution.py:517
  14.2 0.8 %shard_map.109.lower_ref = f32[24,128]{1,0:T(8,128)S(1)} custom-call(bf16[160,1024]{1,0:T(8,128)(2,1)S(1)} %collective-permute-done.2.map_ref, bf16[2,8,64,1024]{3,2,1,0:T(8,128)(2,1)S(1)} %get-tuple-element.13.own_ref, bf16[2,8,64,1024]{3,2,1,0:T(8,128)(2,1)S(1)} %get-tuple-element.16.peer_ref, f32[8,128]{1,0:T(8,128)S(1)} %get-tuple-element.17.earlier_ref), custom_call_target="tpu_custom_call" | custom-call | flops 67108864 | bytes 2097152 | tf_op jit(solution)/shard_map/pallas_call | solution.py:389
  15.0 0.9 %collective-permute-start.3 = (f32[24,128]{1,0:T(8,128)S(1)}, f32[24,128]{1,0:T(8,128)S(1)}, u32[]{:S(2)}, u32[]{:S(2)}) collective-permute-start(f32[24,128]{1,0:T(8,128)S(1)} %shard_map.109.lower_ref), channel_id=1, source_target_pairs={{0,1},{1,0},{2,3},{3,2},{4,5},{5,4},{6,7},{7,6},{8,9},{9,8},{10,11... | collective-permute-start | bytes 36872 | tf_op jit(solution)/shard_map/ppermute | solution.py:23
  15.9 0.8 %collective-permute-done.3.lower_theirs_ref = f32[24,128]{1,0:T(8,128)S(1)} collective-permute-done((f32[24,128]{1,0:T(8,128)S(1)}, f32[24,128]{1,0:T(8,128)S(1)}, u32[]{:S(2)}, u32[]{:S(2)}) %collective-permute-start.3) | collective-permute-done | bytes 12320 | tf_op jit(solution)/shard_map/ppermute | solution.py:23
  16.7 2.8 %shard_map.110 = (f32[1024,1024]{1,0:T(8,128)}, f32[1,64]{1,0:T(1,128)}) custom-call(f32[48,128]{1,0:T(8,128)S(1)} %get-tuple-element.14.mine_ref, f32[48,128]{1,0:T(8,128)S(1)} %collective-permute-done.1.theirs_ref, bf16[192,1024]{1,0:T(8,128)(2,1)S(1)} %get-tuple-element.15.wide_ref, ...), custom_call_target="tpu_custom_call", output_to_operand_aliasing={{0}: (7, {}), {1}: (8, {})} | custom-call | flops 402653184 | bytes 6291456 | tf_op jit(solution)/shard_map/pallas_call | solution.py:491
  (7 shorter events, 0.1 us)
Async XLA Ops:
  0.6 8.3 %collective-permute-start = (bf16[1024,2048]{1,0:T(8,128)(2,1)}, bf16[1024,2048]{1,0:T(8,128)(2,1)S(1)}, u32[]{:S(2)}, u32[]{:S(2)}) collective-permute-start(bf16[1024,2048]{1,0:T(8,128)(2,1)} %tokens_ref.1), channel_id=1, source_target_pairs={{0,1},{1,0},{2,3},{3,2},{4,5},{5,4},{6,7},{7,6},{8,9},{9,8},{10,11... | collective-permute-start | bytes 12582920 | tf_op jit(solution)/shard_map/ppermute | solution.py:23
  1.4 1.6 %copy-start.7 = (bf16[1024,1024]{1,0:T(8,128)(2,1)S(1)}, bf16[1024,1024]{1,0:T(8,128)(2,1)}, u32[]{:S(2)}) copy-start(bf16[1024,1024]{1,0:T(8,128)(2,1)} %proj_ref.3) | copy-start | bytes 6291460
  3.0 2.2 %copy-start = (bf16[1024,2048]{1,0:T(8,128)(2,1)S(1)}, bf16[1024,2048]{1,0:T(8,128)(2,1)}, u32[]{:S(2)}) copy-start(bf16[1024,2048]{1,0:T(8,128)(2,1)} %tokens_ref.1) | copy-start | bytes 12582916
  3.0 2.9 %copy-start.1 = (bf16[1024,1024]{1,0:T(8,128)(2,1)S(1)}, bf16[1024,1024]{1,0:T(8,128)(2,1)}, u32[]{:S(2)}) copy-start(bf16[1024,1024]{1,0:T(8,128)(2,1)} %proj_ref.2) | copy-start | bytes 6291460
  3.0 2.9 %copy-start.2 = (bf16[8,8,2048]{2,1,0:T(8,128)(2,1)S(1)}, bf16[8,8,2048]{2,1,0:T(8,128)(2,1)}, u32[]{:S(2)}) copy-start(bf16[8,8,2048]{2,1,0:T(8,128)(2,1)} %query_ref.3) | copy-start | bytes 786436
  3.0 2.9 %copy-start.3 = (bf16[8,8,2048]{2,1,0:T(8,128)(2,1)S(1)}, bf16[8,8,2048]{2,1,0:T(8,128)(2,1)}, u32[]{:S(2)}) copy-start(bf16[8,8,2048]{2,1,0:T(8,128)(2,1)} %prior_ref.3) | copy-start | bytes 786436
  3.0 3.1 %copy-start.4 = (f32[8,20,1024]{2,0,1:T(8,128)S(1)}, f32[8,20,1024]{2,0,1:T(8,128)}, u32[]{:S(2)}) copy-start(f32[8,20,1024]{2,0,1:T(8,128)} %param.16) | copy-start | bytes 1966084
  3.9 5.0 %copy-start.5 = (s32[64,20]{0,1:T(8,128)S(1)}, s32[64,20]{0,1:T(8,128)}, u32[]{:S(2)}) copy-start(s32[64,20]{0,1:T(8,128)} %param.10) | copy-start | bytes 15364
  3.9 5.0 %copy-start.6 = (s32[64]{0:T(128)S(1)}, s32[64]{0:T(128)}, u32[]{:S(2)}) copy-start(s32[64]{0:T(128)} %param.11) | copy-start | bytes 772
  3.9 10.3 %collective-permute-start.2 = (bf16[160,1024]{1,0:T(8,128)(2,1)S(1)}, bf16[160,1024]{1,0:T(8,128)(2,1)S(1)}, u32[]{:S(2)}, u32[]{:S(2)}) collective-permute-start(bf16[160,1024]{1,0:T(8,128)(2,1)S(1)} %shard_map.107), channel_id=1, source_target_pairs={{0,2},{1,3},{2,4},{3,5},{4,6},{5,7},{6,8},{7,9},{8,10},{9,11},{10,... | collective-permute-start | bytes 983048 | tf_op jit(solution)/shard_map/ppermute | solution.py:517
  12.6 1.3 %collective-permute-start.1 = (f32[48,128]{1,0:T(8,128)S(1)}, f32[48,128]{1,0:T(8,128)S(1)}, u32[]{:S(2)}, u32[]{:S(2)}) collective-permute-start(f32[48,128]{1,0:T(8,128)S(1)} %get-tuple-element.14.mine_ref), channel_id=1, source_target_pairs={{0,1},{1,0},{2,3},{3,2},{4,5},{5,4},{6,7},{7,6},{8,9},{9,8},{10,11... | collective-permute-start | bytes 73736 | tf_op jit(solution)/shard_map/ppermute | solution.py:23
  15.0 1.7 %collective-permute-start.3 = (f32[24,128]{1,0:T(8,128)S(1)}, f32[24,128]{1,0:T(8,128)S(1)}, u32[]{:S(2)}, u32[]{:S(2)}) collective-permute-start(f32[24,128]{1,0:T(8,128)S(1)} %shard_map.109.lower_ref), channel_id=1, source_target_pairs={{0,1},{1,0},{2,3},{3,2},{4,5},{5,4},{6,7},{7,6},{8,9},{9,8},{10,11... | collective-permute-start | bytes 36872 | tf_op jit(solution)/shard_map/ppermute | solution.py:23

commit v7 on v6

--- a/solution.py
+++ b/solution.py
@@ -357,19 +357,19 @@
 
 def raw_sums(tables, pools, which):
     rows = len(pools) * pools[0].shape[2]
-    top = jnp.zeros((TOP, rows), F32)
-    rest = jnp.zeros((TOP, rows), F32)
-    place = lax.broadcasted_iota(jnp.int32, (TOP, rows), 0) >> 2
+    total = jnp.zeros((rows, 2 * TOP * len(tables)), F32)
+    lane = lax.broadcasted_iota(jnp.int32, total.shape, 1) & (2 * TOP - 1)
     for h in range(H):
-        left = []
+        right = []
         for table in tables:
-            left += [table[h * TOP : (h + 1) * TOP], table[H * TOP + h // 4 * TOP :][:TOP]]
+            right += [table[h * TOP : (h + 1) * TOP], table[H * TOP + h // 4 * TOP :][:TOP]]
         pooled = jnp.concatenate([pool[which, h] for pool in pools], axis=0)
-        result = dot_nt(jnp.concatenate(left, axis=0), pooled)
-        for i in range(len(tables)):
-            top = top + result[2 * i * TOP :][:TOP]
-            rest = rest + jnp.where(place == h % 4, result[(2 * i + 1) * TOP :][:TOP], 0.0)
-    return finish_raw(top, rest)
+        result = dot_nt(pooled, jnp.concatenate(right, axis=0))
+        kept = (lane < TOP) | ((lane - TOP) >> 2 == h % 4)
+        total = total + jnp.where(kept, result, 0.0)
+    total = total.T
+    total = sum(total[2 * TOP * i :][: 2 * TOP] for i in range(len(tables)))
+    return finish_raw(total[:TOP], total[TOP:])
 
 
 def lower_kernel(map_ref, own_ref, peer_ref, earlier_ref, out_ref):

time: 19.7 us -> 19.6 us (level)
  Pallas kernels: 12.1 us -> 11.1 us
  waiting for transfers between devices: 2.33 us -> 3.31 us
    ppermute x1, waiting for transfers between devices: 0.32 us -> 1.29 us  [rotated(): lax.ppermute(block, axis, [(i, (i + distance) % count) for i in range(cou...]
    pallas_call x1, Pallas kernels: 3.63 us -> 2.66 us  [peer_side(): pl.pallas_call(peer_kernel, in_specs=[IN_VMEM] * 7, out_specs=[IN_VMEM] *...]
  transfers between devices with their start and end apart: 4 -> 4, of which waited for: 3 -> 3; matrix products, arithmetic and copies ran while one was open for 0% -> 0% of each run, Pallas kernels for 44% -> 39%
where the time goes in v7:
time: 19.6 us; the launch traced here: 19.4 us
  Pallas kernels  11.1 us (57%)
  waiting for transfers between devices  3.31 us (17%)
  starting transfers between devices  2.95 us (15%)
  local copies, waits for them, and re-layouts  1.33 us (7%)
  between operations  0.72 us (4%)
    pallas_call x2, Pallas kernels, gradient(): pl.pallas_call(kernel, in_specs=[IN_VMEM] * count + [IN_HBM] * len(into),...  2.84 us
    pallas_call x1, Pallas kernels, own_side(): pl.pallas_call(own_kernel, in_specs=[IN_VMEM] * 5, out_specs=[IN_VMEM] *...  2.8 us
    pallas_call x1, Pallas kernels, peer_side(): pl.pallas_call(peer_kernel, in_specs=[IN_VMEM] * 7, out_specs=[IN_VMEM] *...  2.66 us
    ppermute x3, waiting for transfers between devices, partner_2(): return lax.ppermute(block, axis, route)  2.01 us
    ppermute x3, starting transfers between devices, partner_2(): return lax.ppermute(block, axis, route)  1.66 us
    unnamed x16, local copies, waits for them, and re-layouts  1.33 us
    ppermute x1, waiting for transfers between devices, rotated(): lax.ppermute(block, axis, [(i, (i + distance) % count) for i in range(cou...  1.29 us
    ppermute x1, starting transfers between devices, rotated(): lax.ppermute(block, axis, [(i, (i + distance) % count) for i in range(cou...  1.29 us
  transfers between devices with their start and end apart: 4, of which 3 were waited for; matrix products, arithmetic and copies ran while one was open for 0% of the time, Pallas kernels for 39%

profile of v7, /device:TPU:25, one launch (start us, length us, event | category | flops | bytes accessed | tf_op | source)
XLA Modules:
  0.0 19.4 jit_solution(8376105677363576934)
XLA Ops:
  0.6 0.7 %collective-permute-start = (bf16[1024,2048]{1,0:T(8,128)(2,1)}, bf16[1024,2048]{1,0:T(8,128)(2,1)S(1)}, u32[]{:S(2)}, u32[]{:S(2)}) collective-permute-start(bf16[1024,2048]{1,0:T(8,128)(2,1)} %tokens_ref.1), channel_id=1, source_target_pairs={{0,1},{1,0},{2,3},{3,2},{4,5},{5,4},{6,7},{7,6},{8,9},{9,8},{10,11... | collective-permute-start | bytes 12582920 | tf_op jit(solution)/shard_map/ppermute | solution.py:23
  1.4 1.2 %shard_map.106.spread_ref = bf16[320,1024]{1,0:T(8,128)(2,1)S(1)} custom-call(f32[20,8,1024]{2,1,0:T(8,128)} %bitcast.9), custom_call_target="tpu_custom_call" | custom-call | flops 16384000000 | bytes 655360 | tf_op jit(solution)/shard_map/pallas_call | solution.py:217
  2.6 0.4 %copy-done.7 = bf16[1024,1024]{1,0:T(8,128)(2,1)S(1)} copy-done((bf16[1024,1024]{1,0:T(8,128)(2,1)S(1)}, bf16[1024,1024]{1,0:T(8,128)(2,1)}, u32[]{:S(2)}) %copy-start.7) | copy-done | bytes 2097176
  3.0 0.0 copy-start.4
  3.0 0.9 %shard_map.107 = bf16[160,1024]{1,0:T(8,128)(2,1)S(1)} custom-call(bf16[320,1024]{1,0:T(8,128)(2,1)S(1)} %shard_map.106.spread_ref, bf16[1024,1024]{1,0:T(8,128)(2,1)S(1)} %copy-done.7), custom_call_target="tpu_custom_call" | custom-call | flops 6710886400 | bytes 2097152 | tf_op jit(solution)/shard_map/pallas_call | solution.py:232
  3.9 0.0 copy-start.5
  3.9 0.0 copy-start.6
  3.9 1.3 %collective-permute-start.2 = (bf16[160,1024]{1,0:T(8,128)(2,1)S(1)}, bf16[160,1024]{1,0:T(8,128)(2,1)S(1)}, u32[]{:S(2)}, u32[]{:S(2)}) collective-permute-start(bf16[160,1024]{1,0:T(8,128)(2,1)S(1)} %shard_map.107), channel_id=1, source_target_pairs={{0,2},{1,3},{2,4},{3,5},{4,6},{5,7},{6,8},{7,9},{8,10},{9,11},{10,... | collective-permute-start | bytes 983048 | tf_op jit(solution)/shard_map/ppermute | solution.py:517
  5.2 0.0 copy-done
  5.2 0.6 %copy-done.1 = bf16[1024,1024]{1,0:T(8,128)(2,1)S(1)} copy-done((bf16[1024,1024]{1,0:T(8,128)(2,1)S(1)}, bf16[1024,1024]{1,0:T(8,128)(2,1)}, u32[]{:S(2)}) %copy-start.1) | copy-done | bytes 2097176
  5.9 0.0 copy-done.2
  5.9 0.0 copy-done.3
  5.9 0.2 %copy-done.4 = f32[8,20,1024]{2,0,1:T(8,128)S(1)} copy-done((f32[8,20,1024]{2,0,1:T(8,128)S(1)}, f32[8,20,1024]{2,0,1:T(8,128)}, u32[]{:S(2)}) %copy-start.4) | copy-done | bytes 655384
  6.1 2.8 %shard_map.104 = (bf16[2,8,64,1024]{3,2,1,0:T(8,128)(2,1)S(1)}, bf16[320,1024]{1,0:T(8,128)(2,1)S(1)}, bf16[192,1024]{1,0:T(8,128)(2,1)S(1)}) custom-call(bf16[1024,2048]{1,0:T(8,128)(2,1)S(1)} %copy-done, bf16[8,8,2048]{2,1,0:T(8,128)(2,1)S(1)} %copy-done.2, bf16[8,8,2048]{2,1,0:T(8,128)(2,1)S(1)} %copy-done.3, f32[20,8,1024]{2,1,0:T(8,128)S(1)} %bitcast.5, ...), custom_call_target="tpu_custom_call" | custom-call | flops 603979776 | bytes 8388608 | tf_op jit(solution)/shard_map/pallas_call | solution.py:301
  8.9 0.0 collective-permute-done.tokens_ref
  8.9 0.0 copy-done.5
  8.9 2.7 %shard_map.105 = (bf16[2,8,64,1024]{3,2,1,0:T(8,128)(2,1)S(1)}, f32[48,128]{1,0:T(8,128)S(1)}) custom-call(bf16[1024,2048]{1,0:T(8,128)(2,1)S(1)} %collective-permute-done.tokens_ref, bf16[8,8,2048]{2,1,0:T(8,128)(2,1)S(1)} %copy-done.2, bf16[8,8,2048]{2,1,0:T(8,128)(2,1)S(1)} %copy-done.3, bf16[320,1024]{1,0:T(8,128)(2,1)S(1)} %get-tuple-element.12.map_ref, ...), custom_call_target="tpu_custom_call" | custom-call | flops 603979776 | bytes 6291456 | tf_op jit(solution)/shard_map/pallas_call | solution.py:335
  11.6 0.1 collective-permute-start.1
  11.7 1.2 %collective-permute-done.1.theirs_ref = f32[48,128]{1,0:T(8,128)S(1)} collective-permute-done((f32[48,128]{1,0:T(8,128)S(1)}, f32[48,128]{1,0:T(8,128)S(1)}, u32[]{:S(2)}, u32[]{:S(2)}) %collective-permute-start.1) | collective-permute-done | bytes 24608 | tf_op jit(solution)/shard_map/ppermute | solution.py:23
  12.9 1.3 %collective-permute-done.2.map_ref = bf16[160,1024]{1,0:T(8,128)(2,1)S(1)} collective-permute-done((bf16[160,1024]{1,0:T(8,128)(2,1)S(1)}, bf16[160,1024]{1,0:T(8,128)(2,1)S(1)}, u32[]{:S(2)}, u32[]{:S(2)}) %collective-permute-start.2) | collective-permute-done | bytes 327712 | tf_op jit(solution)/shard_map/ppermute | solution.py:517
  14.2 0.7 %shard_map.109.lower_ref = f32[24,128]{1,0:T(8,128)S(1)} custom-call(bf16[160,1024]{1,0:T(8,128)(2,1)S(1)} %collective-permute-done.2.map_ref, bf16[2,8,64,1024]{3,2,1,0:T(8,128)(2,1)S(1)} %get-tuple-element.13.own_ref, bf16[2,8,64,1024]{3,2,1,0:T(8,128)(2,1)S(1)} %get-tuple-element.16.peer_ref, f32[8,128]{1,0:T(8,128)S(1)} %get-tuple-element.17.earlier_ref), custom_call_target="tpu_custom_call" | custom-call | flops 67108864 | bytes 2097152 | tf_op jit(solution)/shard_map/pallas_call | solution.py:389
  14.9 0.8 %collective-permute-start.3 = (f32[24,128]{1,0:T(8,128)S(1)}, f32[24,128]{1,0:T(8,128)S(1)}, u32[]{:S(2)}, u32[]{:S(2)}) collective-permute-start(f32[24,128]{1,0:T(8,128)S(1)} %shard_map.109.lower_ref), channel_id=1, source_target_pairs={{0,1},{1,0},{2,3},{3,2},{4,5},{5,4},{6,7},{7,6},{8,9},{9,8},{10,11... | collective-permute-start | bytes 36872 | tf_op jit(solution)/shard_map/ppermute | solution.py:23
  15.8 0.8 %collective-permute-done.3.lower_theirs_ref = f32[24,128]{1,0:T(8,128)S(1)} collective-permute-done((f32[24,128]{1,0:T(8,128)S(1)}, f32[24,128]{1,0:T(8,128)S(1)}, u32[]{:S(2)}, u32[]{:S(2)}) %collective-permute-start.3) | collective-permute-done | bytes 12320 | tf_op jit(solution)/shard_map/ppermute | solution.py:23
  16.6 2.8 %shard_map.110 = (f32[1024,1024]{1,0:T(8,128)}, f32[1,64]{1,0:T(1,128)}) custom-call(f32[48,128]{1,0:T(8,128)S(1)} %get-tuple-element.14.mine_ref, f32[48,128]{1,0:T(8,128)S(1)} %collective-permute-done.1.theirs_ref, bf16[192,1024]{1,0:T(8,128)(2,1)S(1)} %get-tuple-element.15.wide_ref, ...), custom_call_target="tpu_custom_call", output_to_operand_aliasing={{0}: (7, {}), {1}: (8, {})} | custom-call | flops 402653184 | bytes 6291456 | tf_op jit(solution)/shard_map/pallas_call | solution.py:491
  (7 shorter events, 0.1 us)
Async XLA Ops:
  0.6 8.3 %collective-permute-start = (bf16[1024,2048]{1,0:T(8,128)(2,1)}, bf16[1024,2048]{1,0:T(8,128)(2,1)S(1)}, u32[]{:S(2)}, u32[]{:S(2)}) collective-permute-start(bf16[1024,2048]{1,0:T(8,128)(2,1)} %tokens_ref.1), channel_id=1, source_target_pairs={{0,1},{1,0},{2,3},{3,2},{4,5},{5,4},{6,7},{7,6},{8,9},{9,8},{10,11... | collective-permute-start | bytes 12582920 | tf_op jit(solution)/shard_map/ppermute | solution.py:23
  1.4 1.6 %copy-start.7 = (bf16[1024,1024]{1,0:T(8,128)(2,1)S(1)}, bf16[1024,1024]{1,0:T(8,128)(2,1)}, u32[]{:S(2)}) copy-start(bf16[1024,1024]{1,0:T(8,128)(2,1)} %proj_ref.3) | copy-start | bytes 6291460
  3.0 2.2 %copy-start = (bf16[1024,2048]{1,0:T(8,128)(2,1)S(1)}, bf16[1024,2048]{1,0:T(8,128)(2,1)}, u32[]{:S(2)}) copy-start(bf16[1024,2048]{1,0:T(8,128)(2,1)} %tokens_ref.1) | copy-start | bytes 12582916
  3.0 2.9 %copy-start.1 = (bf16[1024,1024]{1,0:T(8,128)(2,1)S(1)}, bf16[1024,1024]{1,0:T(8,128)(2,1)}, u32[]{:S(2)}) copy-start(bf16[1024,1024]{1,0:T(8,128)(2,1)} %proj_ref.2) | copy-start | bytes 6291460
  3.0 2.9 %copy-start.2 = (bf16[8,8,2048]{2,1,0:T(8,128)(2,1)S(1)}, bf16[8,8,2048]{2,1,0:T(8,128)(2,1)}, u32[]{:S(2)}) copy-start(bf16[8,8,2048]{2,1,0:T(8,128)(2,1)} %query_ref.3) | copy-start | bytes 786436
  3.0 2.9 %copy-start.3 = (bf16[8,8,2048]{2,1,0:T(8,128)(2,1)S(1)}, bf16[8,8,2048]{2,1,0:T(8,128)(2,1)}, u32[]{:S(2)}) copy-start(bf16[8,8,2048]{2,1,0:T(8,128)(2,1)} %prior_ref.3) | copy-start | bytes 786436
  3.0 3.1 %copy-start.4 = (f32[8,20,1024]{2,0,1:T(8,128)S(1)}, f32[8,20,1024]{2,0,1:T(8,128)}, u32[]{:S(2)}) copy-start(f32[8,20,1024]{2,0,1:T(8,128)} %param.16) | copy-start | bytes 1966084
  3.9 5.0 %copy-start.5 = (s32[64,20]{0,1:T(8,128)S(1)}, s32[64,20]{0,1:T(8,128)}, u32[]{:S(2)}) copy-start(s32[64,20]{0,1:T(8,128)} %param.10) | copy-start | bytes 15364
  3.9 5.0 %copy-start.6 = (s32[64]{0:T(128)S(1)}, s32[64]{0:T(128)}, u32[]{:S(2)}) copy-start(s32[64]{0:T(128)} %param.11) | copy-start | bytes 772
  3.9 10.3 %collective-permute-start.2 = (bf16[160,1024]{1,0:T(8,128)(2,1)S(1)}, bf16[160,1024]{1,0:T(8,128)(2,1)S(1)}, u32[]{:S(2)}, u32[]{:S(2)}) collective-permute-start(bf16[160,1024]{1,0:T(8,128)(2,1)S(1)} %shard_map.107), channel_id=1, source_target_pairs={{0,2},{1,3},{2,4},{3,5},{4,6},{5,7},{6,8},{7,9},{8,10},{9,11},{10,... | collective-permute-start | bytes 983048 | tf_op jit(solution)/shard_map/ppermute | solution.py:517
  11.6 1.3 %collective-permute-start.1 = (f32[48,128]{1,0:T(8,128)S(1)}, f32[48,128]{1,0:T(8,128)S(1)}, u32[]{:S(2)}, u32[]{:S(2)}) collective-permute-start(f32[48,128]{1,0:T(8,128)S(1)} %get-tuple-element.14.mine_ref), channel_id=1, source_target_pairs={{0,1},{1,0},{2,3},{3,2},{4,5},{5,4},{6,7},{7,6},{8,9},{9,8},{10,11... | collective-permute-start | bytes 73736 | tf_op jit(solution)/shard_map/ppermute | solution.py:23
  14.9 1.7 %collective-permute-start.3 = (f32[24,128]{1,0:T(8,128)S(1)}, f32[24,128]{1,0:T(8,128)S(1)}, u32[]{:S(2)}, u32[]{:S(2)}) collective-permute-start(f32[24,128]{1,0:T(8,128)S(1)} %shard_map.109.lower_ref), channel_id=1, source_target_pairs={{0,1},{1,0},{2,3},{3,2},{4,5},{5,4},{6,7},{7,6},{8,9},{9,8},{10,11... | collective-permute-start | bytes 36872 | tf_op jit(solution)/shard_map/ppermute | solution.py:23

commit v8 on v7

--- a/solution.py
+++ b/solution.py
@@ -130,6 +130,7 @@
 F32 = jnp.float32
 BF16 = jnp.bfloat16
 PAD = 24
+PAIR_ROWS = 48
 GRAD_CHUNKS = 4
 DH_BITS = 7
 OBS_BITS = 4
@@ -139,7 +140,7 @@
 PEER_MIB = 16
 PRIOR_COST = 40
 SPREAD_COST = 100000
-SPREAD_MIB = 53
+SPREAD_MIB = 53.5
 
 
 def dot_nt(left, right):
@@ -162,15 +163,19 @@
 
 
 def spread_heads(rows):
-    width = rows.shape[1]
-    top = rows[:TOP]
+    width = 2 * DH
     lane_head = lax.broadcasted_iota(jnp.int32, (TOP, width), 1) >> DH_BITS
-    pieces = [jnp.where(lane_head == h, top, 0.0) for h in range(H)]
-    rest = rows[TOP:A]
-    rest = jnp.concatenate([rest, rest], axis=0)
-    lane_head = lax.broadcasted_iota(jnp.int32, (8, width), 1) >> DH_BITS
     upper = lax.broadcasted_iota(jnp.int32, (8, width), 0) >> 2
-    pieces += [jnp.where(lane_head == 2 * i + upper, rest, 0.0) for i in range(H // 2)]
+    pieces = []
+    for pair in range(H // 2):
+        part = rows[:, pair * width : (pair + 1) * width]
+        rest = jnp.concatenate([part[TOP:A], part[TOP:A]], axis=0)
+        pieces += [
+            jnp.where(lane_head == 0, part[:TOP], 0.0),
+            jnp.where(lane_head == 1, part[:TOP], 0.0),
+            jnp.where(lane_head[:8] == upper, rest, 0.0),
+            jnp.zeros((8, width), F32),
+        ]
     return jnp.concatenate(pieces, axis=0)
 
 
@@ -181,13 +186,23 @@
 
 def spread_into(spread_ref, head):
     high, low = split_high(spread_heads(head))
-    spread_ref[:SPREAD, :] = high
-    spread_ref[SPREAD:, :] = low
+    for pair in range(H // 2):
+        at = 2 * pair * PAIR_ROWS
+        rows = slice(pair * PAIR_ROWS, (pair + 1) * PAIR_ROWS)
+        spread_ref[at : at + PAIR_ROWS, :] = high[rows]
+        spread_ref[at + PAIR_ROWS : at + 2 * PAIR_ROWS, :] = low[rows]
 
 
 def fold_into(out_ref, proj_ref, spread_ref, parts):
-    product = dot_nt(spread_ref[...], proj_ref[...])
-    product = product[:SPREAD] + product[SPREAD:]
+    tops, rests = [], []
+    for pair in range(H // 2):
+        proj = proj_ref[:, pair * 2 * DH : (pair + 1) * 2 * DH]
+        spread = spread_ref[2 * pair * PAIR_ROWS : 2 * (pair + 1) * PAIR_ROWS]
+        product = dot_nt(proj, spread).T
+        product = product[:PAIR_ROWS] + product[PAIR_ROWS:]
+        tops.append(product[: 2 * TOP])
+        rests.append(product[2 * TOP : 2 * TOP + 8])
+    product = jnp.concatenate(tops + rests, axis=0)
     if parts == 1:
         out_ref[...] = product.astype(BF16)
     else:
@@ -218,9 +233,9 @@
         spread_kernel,
         in_specs=[IN_HBM],
         out_specs=IN_VMEM,
-        out_shape=jax.ShapeDtypeStruct((2 * SPREAD, width), BF16),
+        out_shape=jax.ShapeDtypeStruct((H * PAIR_ROWS, 2 * DH), BF16),
         scratch_shapes=[pltpu.VMEM((A, 1, width), F32), pltpu.SemaphoreType.DMA],
-        compiler_params=pltpu.CompilerParams(vmem_limit_bytes=SPREAD_MIB * MIB),
+        compiler_params=pltpu.CompilerParams(vmem_limit_bytes=int(SPREAD_MIB * MIB)),
         cost_estimate=pl.CostEstimate(
             flops=SPREAD_COST * SPREAD * width, bytes_accessed=4 * head_t.size, transcendentals=0
         ),
@@ -288,10 +303,8 @@
     head = level_head(head_ref)
     spread_into(spread_ref, head)
     fold_into(map_ref, proj_ref, spread_ref, 2)
-    head = jnp.concatenate([head, jnp.zeros((PAD - A, H * DH), F32)], axis=0)
-    lane_head = lax.broadcasted_iota(jnp.int32, (PAD, H * DH), 1) >> DH_BITS
-    wide = [jnp.where(lane_head == h, head, 0.0) for h in range(H)]
-    wide_ref[...] = jnp.concatenate(wide, axis=0).astype(BF16)
+    empty = jnp.zeros((PAD - A, H * DH), F32)
+    wide_ref[...] = jnp.concatenate([head, empty, head, empty], axis=0).astype(BF16)
     pool_into(pool_ref, tokens_ref, query_ref, prior_ref)
 
 
@@ -305,9 +318,9 @@
         out_shape=[
             jax.ShapeDtypeStruct((2, H, count // OBS, half), BF16),
             jax.ShapeDtypeStruct((2 * SPREAD, half), BF16),
-            jax.ShapeDtypeStruct((H * PAD, H * DH), BF16),
+            jax.ShapeDtypeStruct((2 * PAD, H * DH), BF16),
         ],
-        scratch_shapes=[pltpu.VMEM((2 * SPREAD, H * DH), BF16)],
+        scratch_shapes=[pltpu.VMEM((H * PAIR_ROWS, 2 * DH), BF16)],
         compiler_params=pltpu.CompilerParams(vmem_limit_bytes=OWN_MIB * MIB),
         cost_estimate=pl.CostEstimate(
             flops=2 * count * width * 2 * H + 4 * count * H * BLOCK_ROWS * half,
@@ -318,7 +331,8 @@
 
 
 def peer_kernel(
-    tokens_ref, query_ref, prior_ref, map_ref, own_ref, legal_ref, label_ref, pool_ref, told_ref
+    tokens_ref, query_ref, prior_ref, map_ref, own_ref, legal_ref, label_ref,
+    pool_ref, told_ref, turned_ref,
 ):
     pool_into(pool_ref, tokens_ref, query_ref, prior_ref)
     tables = [map_ref[:SPREAD], map_ref[SPREAD:]]
@@ -327,6 +341,9 @@
     told_ref[PAD:] = jnp.zeros((PAD, 2 * rows), F32)
     told_ref[PAD : PAD + A, :rows] = legal_ref[...].astype(F32)
     told_ref[PAD + A : PAD + A + 1, :rows] = label_ref[...].astype(F32)
+    for h in range(H):
+        pooled = jnp.concatenate([own_ref[0, h], pool_ref[0, h]], axis=0)
+        turned_ref[:, h * 2 * rows : (h + 1) * 2 * rows] = pooled.T
 
 
 def peer_side(tokens, query_weight, query_prior, own_map, own_pool, legal_t, label):
@@ -335,10 +352,11 @@
     return pl.pallas_call(
         peer_kernel,
         in_specs=[IN_VMEM] * 7,
-        out_specs=[IN_VMEM] * 2,
+        out_specs=[IN_VMEM] * 3,
         out_shape=[
             jax.ShapeDtypeStruct((2, H, count // OBS, half), BF16),
             jax.ShapeDtypeStruct((2 * PAD, 2 * count // OBS), F32),
+            jax.ShapeDtypeStruct((half, 2 * H * count // OBS), BF16),
         ],
         compiler_params=pltpu.CompilerParams(vmem_limit_bytes=PEER_MIB * MIB),
         cost_estimate=pl.CostEstimate(
@@ -416,8 +434,9 @@
     return jnp.concatenate([theirs[:, rows:], theirs[:, :rows]], axis=1)
 
 
-def grad_into(out_ref, loss_ref, out_buf, loss_buf, sems, mine_ref, theirs_ref, wide_ref, own_ref, peer_ref, lower):
-    rows = own_ref.shape[2]
+def grad_into(out_ref, loss_ref, out_buf, loss_buf, sems, mine_ref, theirs_ref, wide_ref, turned_ref, lower):
+
+    rows = mine_ref.shape[1] // 2
     told = jnp.concatenate([mine_ref[PAD:, :rows], theirs_ref[PAD:, :rows]], axis=1)
     move = lax.broadcasted_iota(jnp.int32, told.shape, 0)
     legal = jnp.where(move < A, told, 0.0)
@@ -438,17 +457,25 @@
     logit_grad = (policy - target) * (1.0 - squashed * squashed)
     high, low = split_high(logit_grad)
     left = jnp.concatenate([high.astype(F32), low.astype(F32)], axis=0).astype(BF16)
+    pooled_grad = dot_tn(left, wide_ref[...]).astype(BF16)
+    empty = jnp.zeros((2 * rows, DH), BF16)
+    diagonal = []
+    for pair in range(H // 2):
+        first = pooled_grad[:, 2 * pair * DH : (2 * pair + 1) * DH]
+        second = pooled_grad[:, (2 * pair + 1) * DH : 2 * (pair + 1) * DH]
+        first = jnp.concatenate([first, empty], axis=1)
+        second = jnp.concatenate([empty, second], axis=1)
+        diagonal.append(jnp.concatenate([first, second], axis=0))
     chunk = out_buf.shape[0] // GRAD_CHUNKS
     copies = []
     for i in range(GRAD_CHUNKS):
-        columns = slice(i * chunk, (i + 1) * chunk)
-        narrow = []
-        for h in range(H):
-            pooled = jnp.concatenate([own_ref[0, h, :, columns], peer_ref[0, h, :, columns]], axis=0)
-            product = dot_nn(left, pooled)
-            narrow.append(product[:PAD] + product[PAD:])
-        narrow = jnp.concatenate(narrow, axis=0).astype(BF16)
-        out_buf[columns, :] = dot_tn(narrow, wide_ref[...])
+        for pair in range(H // 2):
+            turned = turned_ref[
+                i * chunk : (i + 1) * chunk, 4 * pair * rows : 4 * (pair + 1) * rows
+            ]
+            out_buf[i * chunk : (i + 1) * chunk, 2 * pair * DH : 2 * (pair + 1) * DH] = dot_nn(
+                turned, diagonal[pair]
+            )
         part = pl.ds(i * chunk, chunk)
         copies.append(pltpu.make_async_copy(out_buf.at[part], out_ref.at[part], sems.at[i]))
         copies[i].start()
@@ -457,7 +484,7 @@
 
 
 def lowest_grad_kernel(
-    mine_ref, theirs_ref, wide_ref, own_ref, peer_ref,
+    mine_ref, theirs_ref, wide_ref, turned_ref,
     out_ref, loss_ref, token_ref, out_buf, loss_buf, sems,
 ):
     token_ref[...] = jnp.zeros_like(token_ref)
@@ -466,12 +493,12 @@
     def _():
         grad_into(
             out_ref, loss_ref, out_buf, loss_buf, sems,
-            mine_ref, theirs_ref, wide_ref, own_ref, peer_ref, [],
+            mine_ref, theirs_ref, wide_ref, turned_ref, [],
         )
 
 
 def upper_grad_kernel(
-    mine_ref, theirs_ref, wide_ref, own_ref, peer_ref,
+    mine_ref, theirs_ref, wide_ref, turned_ref,
     lower_ref, lower_theirs_ref, lowest_ref, lowest_loss_ref,
     out_ref, loss_ref, out_buf, loss_buf, sems,
 ):
@@ -479,13 +506,14 @@
     def _():
         grad_into(
             out_ref, loss_ref, out_buf, loss_buf, sems,
-            mine_ref, theirs_ref, wide_ref, own_ref, peer_ref,
+            mine_ref, theirs_ref, wide_ref, turned_ref,
             [lower_ref[...] + swapped(lower_theirs_ref[...])],
         )
 
 
 def gradient(kernel, operands, into):
-    _, _, rows, half = operands[3].shape
+    half = operands[3].shape[0]
+    rows = operands[0].shape[1] // 2
     width = H * DH
     count = len(operands)
     return pl.pallas_call(
@@ -528,12 +556,12 @@
     own_pool, own_map, wide = own_side(
         tokens, query_weight, query_prior, jnp.transpose(policy_head, (1, 0, 2)), value_weight
     )
-    peer_pool, mine = peer_side(
+    peer_pool, mine, turned = peer_side(
         peer_tokens, query_weight, query_prior, own_map, own_pool,
         legal_moves.T, action_label.reshape(1, -1),
     )
     theirs = partner_2(mine, "dp", 0)
-    operands = [mine, theirs, wide, own_pool, peer_pool]
+    operands = [mine, theirs, wide, turned]
     *lowest, token = gradient(lowest_grad_kernel, operands, [])
     lower = lower_raw(lower_map, own_pool, peer_pool, token)
     lower_theirs = partner_2(lower, "dp", 0)

time: 19.6 us -> 19.3 us (0.985)
  Pallas kernels: 11.1 us -> 10.8 us
  local copies, waits for them, and re-layouts: 1.33 us -> 1.54 us
    unnamed x16, local copies, waits for them, and re-layouts: 1.33 us -> 1.54 us
    pallas_call x1, Pallas kernels: 2.66 us -> 2.86 us  [peer_side(): pl.pallas_call(peer_kernel, in_specs=[IN_VMEM] * 7, out_specs=[IN_VMEM] *...]
where the time goes in v8:
time: 19.3 us; the launch traced here: 19.2 us
  Pallas kernels  10.8 us (56%)
  waiting for transfers between devices  3.17 us (16%)
  starting transfers between devices  2.95 us (15%)
  local copies, waits for them, and re-layouts  1.54 us (8%)
  between operations  0.71 us (4%)
    pallas_call x1, Pallas kernels, peer_side(): pl.pallas_call(peer_kernel, in_specs=[IN_VMEM] * 7, out_specs=[IN_VMEM] *...  2.86 us
    pallas_call x2, Pallas kernels, gradient(): pl.pallas_call(kernel, in_specs=[IN_VMEM] * count + [IN_HBM] * len(into),...  2.71 us
    pallas_call x1, Pallas kernels, own_side(): pl.pallas_call(own_kernel, in_specs=[IN_VMEM] * 5, out_specs=[IN_VMEM] *...  2.62 us
    ppermute x3, waiting for transfers between devices, partner_2(): return lax.ppermute(block, axis, route)  2.02 us
    ppermute x3, starting transfers between devices, partner_2(): return lax.ppermute(block, axis, route)  1.66 us
    unnamed x16, local copies, waits for them, and re-layouts  1.54 us
    ppermute x1, starting transfers between devices, rotated(): lax.ppermute(block, axis, [(i, (i + distance) % count) for i in range(cou...  1.29 us
    ppermute x1, waiting for transfers between devices, rotated(): lax.ppermute(block, axis, [(i, (i + distance) % count) for i in range(cou...  1.16 us
  transfers between devices with their start and end apart: 4, of which 3 were waited for; matrix products, arithmetic and copies ran while one was open for 0% of the time, Pallas kernels for 39%

profile of v8, /device:TPU:25, one launch (start us, length us, event | category | flops | bytes accessed | tf_op | source)
XLA Modules:
  0.0 19.2 jit_solution(10366757491387434057)
XLA Ops:
  0.6 0.7 %collective-permute-start = (bf16[1024,2048]{1,0:T(8,128)(2,1)}, bf16[1024,2048]{1,0:T(8,128)(2,1)S(1)}, u32[]{:S(2)}, u32[]{:S(2)}) collective-permute-start(bf16[1024,2048]{1,0:T(8,128)(2,1)} %tokens_ref.1), channel_id=1, source_target_pairs={{0,1},{1,0},{2,3},{3,2},{4,5},{5,4},{6,7},{7,6},{8,9},{9,8},{10,11... | collective-permute-start | bytes 12582920 | tf_op jit(solution)/shard_map/ppermute | solution.py:23
  1.4 0.0 copy-start.7
  1.4 1.1 %shard_map.106.spread_ref = bf16[384,256]{1,0:T(8,128)(2,1)S(1)} custom-call(f32[20,8,1024]{2,1,0:T(8,128)} %bitcast.9), custom_call_target="tpu_custom_call" | custom-call | flops 16384000000 | bytes 655360 | tf_op jit(solution)/shard_map/pallas_call | solution.py:232
  2.5 0.5 %copy-done.7 = bf16[1024,1024]{1,0:T(8,128)(2,1)S(1)} copy-done((bf16[1024,1024]{1,0:T(8,128)(2,1)S(1)}, bf16[1024,1024]{1,0:T(8,128)(2,1)}, u32[]{:S(2)}) %copy-start.7) | copy-done | bytes 2097176
  3.0 0.0 copy-start.4
  3.0 0.8 %shard_map.107 = bf16[160,1024]{1,0:T(8,128)(2,1)S(1)} custom-call(bf16[384,256]{1,0:T(8,128)(2,1)S(1)} %shard_map.106.spread_ref, bf16[1024,1024]{1,0:T(8,128)(2,1)S(1)} %copy-done.7), custom_call_target="tpu_custom_call" | custom-call | flops 6710886400 | bytes 2097152 | tf_op jit(solution)/shard_map/pallas_call | solution.py:247
  3.8 1.3 %collective-permute-start.2 = (bf16[160,1024]{1,0:T(8,128)(2,1)S(1)}, bf16[160,1024]{1,0:T(8,128)(2,1)S(1)}, u32[]{:S(2)}, u32[]{:S(2)}) collective-permute-start(bf16[160,1024]{1,0:T(8,128)(2,1)S(1)} %shard_map.107), channel_id=1, source_target_pairs={{0,2},{1,3},{2,4},{3,5},{4,6},{5,7},{6,8},{7,9},{8,10},{9,11},{10,... | collective-permute-start | bytes 983048 | tf_op jit(solution)/shard_map/ppermute | solution.py:545
  5.1 0.1 copy-done
  5.2 0.7 %copy-done.1 = bf16[1024,1024]{1,0:T(8,128)(2,1)S(1)} copy-done((bf16[1024,1024]{1,0:T(8,128)(2,1)S(1)}, bf16[1024,1024]{1,0:T(8,128)(2,1)}, u32[]{:S(2)}) %copy-start.1) | copy-done | bytes 2097176
  5.9 0.0 copy-done.2
  5.9 0.0 copy-done.3
  5.9 0.2 %copy-done.4 = f32[8,20,1024]{2,0,1:T(8,128)S(1)} copy-done((f32[8,20,1024]{2,0,1:T(8,128)S(1)}, f32[8,20,1024]{2,0,1:T(8,128)}, u32[]{:S(2)}) %copy-start.4) | copy-done | bytes 655384
  6.1 2.6 %shard_map.104 = (bf16[2,8,64,1024]{3,2,1,0:T(8,128)(2,1)S(1)}, bf16[320,1024]{1,0:T(8,128)(2,1)S(1)}, bf16[48,1024]{1,0:T(8,128)(2,1)S(1)}) custom-call(bf16[1024,2048]{1,0:T(8,128)(2,1)S(1)} %copy-done, bf16[8,8,2048]{2,1,0:T(8,128)(2,1)S(1)} %copy-done.2, bf16[8,8,2048]{2,1,0:T(8,128)(2,1)S(1)} %copy-done.3, f32[20,8,1024]{2,1,0:T(8,128)S(1)} %bitcast.5, ...), custom_call_target="tpu_custom_call" | custom-call | flops 603979776 | bytes 8388608 | tf_op jit(solution)/shard_map/pallas_call | solution.py:314
  8.7 0.0 collective-permute-done.tokens_ref
  8.7 0.0 copy-done.5
  8.8 0.0 copy-done.6
  8.8 2.9 %shard_map.105 = (bf16[2,8,64,1024]{3,2,1,0:T(8,128)(2,1)S(1)}, f32[48,128]{1,0:T(8,128)S(1)}, bf16[1024,1024]{1,0:T(8,128)(2,1)S(1)}) custom-call(bf16[1024,2048]{1,0:T(8,128)(2,1)S(1)} %collective-permute-done.tokens_ref, bf16[8,8,2048]{2,1,0:T(8,128)(2,1)S(1)} %copy-done.2, bf16[8,8,2048]{2,1,0:T(8,128)(2,1)S(1)} %copy-done.3, ...), custom_call_target="tpu_custom_call" | custom-call | flops 603979776 | bytes 6291456 | tf_op jit(solution)/shard_map/pallas_call | solution.py:352
  11.6 0.1 collective-permute-start.1
  11.7 1.2 %collective-permute-done.1.theirs_ref = f32[48,128]{1,0:T(8,128)S(1)} collective-permute-done((f32[48,128]{1,0:T(8,128)S(1)}, f32[48,128]{1,0:T(8,128)S(1)}, u32[]{:S(2)}, u32[]{:S(2)}) %collective-permute-start.1) | collective-permute-done | bytes 24608 | tf_op jit(solution)/shard_map/ppermute | solution.py:23
  12.9 1.2 %collective-permute-done.2.map_ref = bf16[160,1024]{1,0:T(8,128)(2,1)S(1)} collective-permute-done((bf16[160,1024]{1,0:T(8,128)(2,1)S(1)}, bf16[160,1024]{1,0:T(8,128)(2,1)S(1)}, u32[]{:S(2)}, u32[]{:S(2)}) %collective-permute-start.2) | collective-permute-done | bytes 327712 | tf_op jit(solution)/shard_map/ppermute | solution.py:545
  14.1 0.7 %shard_map.109.lower_ref = f32[24,128]{1,0:T(8,128)S(1)} custom-call(bf16[160,1024]{1,0:T(8,128)(2,1)S(1)} %collective-permute-done.2.map_ref, bf16[2,8,64,1024]{3,2,1,0:T(8,128)(2,1)S(1)} %get-tuple-element.14.own_ref, bf16[2,8,64,1024]{3,2,1,0:T(8,128)(2,1)S(1)} %get-tuple-element.18.peer_ref, f32[8,128]{1,0:T(8,128)S(1)} %get-tuple-element.19.earlier_ref), custom_call_target="tpu_custom_call" | custom-call | flops 67108864 | bytes 2097152 | tf_op jit(solution)/shard_map/pallas_call | solution.py:407
  14.8 0.8 %collective-permute-start.3 = (f32[24,128]{1,0:T(8,128)S(1)}, f32[24,128]{1,0:T(8,128)S(1)}, u32[]{:S(2)}, u32[]{:S(2)}) collective-permute-start(f32[24,128]{1,0:T(8,128)S(1)} %shard_map.109.lower_ref), channel_id=1, source_target_pairs={{0,1},{1,0},{2,3},{3,2},{4,5},{5,4},{6,7},{7,6},{8,9},{9,8},{10,11... | collective-permute-start | bytes 36872 | tf_op jit(solution)/shard_map/ppermute | solution.py:23
  15.7 0.8 %collective-permute-done.3.lower_theirs_ref = f32[24,128]{1,0:T(8,128)S(1)} collective-permute-done((f32[24,128]{1,0:T(8,128)S(1)}, f32[24,128]{1,0:T(8,128)S(1)}, u32[]{:S(2)}, u32[]{:S(2)}) %collective-permute-start.3) | collective-permute-done | bytes 12320 | tf_op jit(solution)/shard_map/ppermute | solution.py:23
  16.5 2.7 %shard_map.110 = (f32[1024,1024]{1,0:T(8,128)}, f32[1,64]{1,0:T(1,128)}) custom-call(f32[48,128]{1,0:T(8,128)S(1)} %get-tuple-element.15.mine_ref, f32[48,128]{1,0:T(8,128)S(1)} %collective-permute-done.1.theirs_ref, bf16[48,1024]{1,0:T(8,128)(2,1)S(1)} %get-tuple-element.16.wide_ref, ...), custom_call_target="tpu_custom_call", output_to_operand_aliasing={{0}: (6, {}), {1}: (7, {})} | custom-call | flops 402653184 | bytes 6291456 | tf_op jit(solution)/shard_map/pallas_call | solution.py:519
  (7 shorter events, 0.1 us)
Async XLA Ops:
  0.6 8.1 %collective-permute-start = (bf16[1024,2048]{1,0:T(8,128)(2,1)}, bf16[1024,2048]{1,0:T(8,128)(2,1)S(1)}, u32[]{:S(2)}, u32[]{:S(2)}) collective-permute-start(bf16[1024,2048]{1,0:T(8,128)(2,1)} %tokens_ref.1), channel_id=1, source_target_pairs={{0,1},{1,0},{2,3},{3,2},{4,5},{5,4},{6,7},{7,6},{8,9},{9,8},{10,11... | collective-permute-start | bytes 12582920 | tf_op jit(solution)/shard_map/ppermute | solution.py:23
  1.4 1.6 %copy-start.7 = (bf16[1024,1024]{1,0:T(8,128)(2,1)S(1)}, bf16[1024,1024]{1,0:T(8,128)(2,1)}, u32[]{:S(2)}) copy-start(bf16[1024,1024]{1,0:T(8,128)(2,1)} %proj_ref.3) | copy-start | bytes 6291460
  3.0 2.2 %copy-start = (bf16[1024,2048]{1,0:T(8,128)(2,1)S(1)}, bf16[1024,2048]{1,0:T(8,128)(2,1)}, u32[]{:S(2)}) copy-start(bf16[1024,2048]{1,0:T(8,128)(2,1)} %tokens_ref.1) | copy-start | bytes 12582916
  3.0 2.9 %copy-start.1 = (bf16[1024,1024]{1,0:T(8,128)(2,1)S(1)}, bf16[1024,1024]{1,0:T(8,128)(2,1)}, u32[]{:S(2)}) copy-start(bf16[1024,1024]{1,0:T(8,128)(2,1)} %proj_ref.2) | copy-start | bytes 6291460
  3.0 2.9 %copy-start.2 = (bf16[8,8,2048]{2,1,0:T(8,128)(2,1)S(1)}, bf16[8,8,2048]{2,1,0:T(8,128)(2,1)}, u32[]{:S(2)}) copy-start(bf16[8,8,2048]{2,1,0:T(8,128)(2,1)} %query_ref.3) | copy-start | bytes 786436
  3.0 2.9 %copy-start.3 = (bf16[8,8,2048]{2,1,0:T(8,128)(2,1)S(1)}, bf16[8,8,2048]{2,1,0:T(8,128)(2,1)}, u32[]{:S(2)}) copy-start(bf16[8,8,2048]{2,1,0:T(8,128)(2,1)} %prior_ref.3) | copy-start | bytes 786436
  3.0 3.1 %copy-start.4 = (f32[8,20,1024]{2,0,1:T(8,128)S(1)}, f32[8,20,1024]{2,0,1:T(8,128)}, u32[]{:S(2)}) copy-start(f32[8,20,1024]{2,0,1:T(8,128)} %param.16) | copy-start | bytes 1966084
  3.8 10.3 %collective-permute-start.2 = (bf16[160,1024]{1,0:T(8,128)(2,1)S(1)}, bf16[160,1024]{1,0:T(8,128)(2,1)S(1)}, u32[]{:S(2)}, u32[]{:S(2)}) collective-permute-start(bf16[160,1024]{1,0:T(8,128)(2,1)S(1)} %shard_map.107), channel_id=1, source_target_pairs={{0,2},{1,3},{2,4},{3,5},{4,6},{5,7},{6,8},{7,9},{8,10},{9,11},{10,... | collective-permute-start | bytes 983048 | tf_op jit(solution)/shard_map/ppermute | solution.py:545
  6.1 2.6 %copy-start.5 = (s32[64,20]{0,1:T(8,128)S(1)}, s32[64,20]{0,1:T(8,128)}, u32[]{:S(2)}) copy-start(s32[64,20]{0,1:T(8,128)} %param.10) | copy-start | bytes 15364
  6.1 2.7 %copy-start.6 = (s32[64]{0:T(128)S(1)}, s32[64]{0:T(128)}, u32[]{:S(2)}) copy-start(s32[64]{0:T(128)} %param.11) | copy-start | bytes 772
  11.6 1.3 %collective-permute-start.1 = (f32[48,128]{1,0:T(8,128)S(1)}, f32[48,128]{1,0:T(8,128)S(1)}, u32[]{:S(2)}, u32[]{:S(2)}) collective-permute-start(f32[48,128]{1,0:T(8,128)S(1)} %get-tuple-element.15.mine_ref), channel_id=1, source_target_pairs={{0,1},{1,0},{2,3},{3,2},{4,5},{5,4},{6,7},{7,6},{8,9},{9,8},{10,11... | collective-permute-start | bytes 73736 | tf_op jit(solution)/shard_map/ppermute | solution.py:23
  14.8 1.7 %collective-permute-start.3 = (f32[24,128]{1,0:T(8,128)S(1)}, f32[24,128]{1,0:T(8,128)S(1)}, u32[]{:S(2)}, u32[]{:S(2)}) collective-permute-start(f32[24,128]{1,0:T(8,128)S(1)} %shard_map.109.lower_ref), channel_id=1, source_target_pairs={{0,1},{1,0},{2,3},{3,2},{4,5},{5,4},{6,7},{7,6},{8,9},{9,8},{10,11... | collective-permute-start | bytes 36872 | tf_op jit(solution)/shard_map/ppermute | solution.py:23

commit v9 on v8

--- a/solution.py
+++ b/solution.py
@@ -131,7 +131,9 @@
 BF16 = jnp.bfloat16
 PAD = 24
 PAIR_ROWS = 48
-GRAD_CHUNKS = 4
+GRAD_CUTS = (0, 1, 2, 4, 6, 8)
+GRAD_UNITS = GRAD_CUTS[-1]
+GRAD_CHUNKS = len(GRAD_CUTS) - 1
 DH_BITS = 7
 OBS_BITS = 4
 MIB = 2**20
@@ -466,17 +468,13 @@
         first = jnp.concatenate([first, empty], axis=1)
         second = jnp.concatenate([empty, second], axis=1)
         diagonal.append(jnp.concatenate([first, second], axis=0))
-    chunk = out_buf.shape[0] // GRAD_CHUNKS
+    unit = out_buf.shape[0] // GRAD_UNITS
     copies = []
     for i in range(GRAD_CHUNKS):
+        part = slice(GRAD_CUTS[i] * unit, GRAD_CUTS[i + 1] * unit)
         for pair in range(H // 2):
-            turned = turned_ref[
-                i * chunk : (i + 1) * chunk, 4 * pair * rows : 4 * (pair + 1) * rows
-            ]
-            out_buf[i * chunk : (i + 1) * chunk, 2 * pair * DH : 2 * (pair + 1) * DH] = dot_nn(
-                turned, diagonal[pair]
-            )
-        part = pl.ds(i * chunk, chunk)
+            turned = turned_ref[part, 4 * pair * rows : 4 * (pair + 1) * rows]
+            out_buf[part, 2 * pair * DH : 2 * (pair + 1) * DH] = dot_nn(turned, diagonal[pair])
         copies.append(pltpu.make_async_copy(out_buf.at[part], out_ref.at[part], sems.at[i]))
         copies[i].start()
     for copy in copies + [loss_copy]:

time: 19.3 us -> 19.3 us (level)
  no operation moved by 1% of the time
where the time goes in v9:
time: 19.3 us; the launch traced here: 19.1 us
  Pallas kernels  10.8 us (56%)
  waiting for transfers between devices  3.16 us (16%)
  starting transfers between devices  2.95 us (15%)
  local copies, waits for them, and re-layouts  1.54 us (8%)
  between operations  0.71 us (4%)
    pallas_call x1, Pallas kernels, peer_side(): pl.pallas_call(peer_kernel, in_specs=[IN_VMEM] * 7, out_specs=[IN_VMEM] *...  2.86 us
    pallas_call x2, Pallas kernels, gradient(): pl.pallas_call(kernel, in_specs=[IN_VMEM] * count + [IN_HBM] * len(into),...  2.66 us
    pallas_call x1, Pallas kernels, own_side(): pl.pallas_call(own_kernel, in_specs=[IN_VMEM] * 5, out_specs=[IN_VMEM] *...  2.62 us
    ppermute x3, waiting for transfers between devices, partner_2(): return lax.ppermute(block, axis, route)  2.02 us
    ppermute x3, starting transfers between devices, partner_2(): return lax.ppermute(block, axis, route)  1.66 us
    unnamed x16, local copies, waits for them, and re-layouts  1.54 us
    ppermute x1, starting transfers between devices, rotated(): lax.ppermute(block, axis, [(i, (i + distance) % count) for i in range(cou...  1.29 us
    ppermute x1, waiting for transfers between devices, rotated(): lax.ppermute(block, axis, [(i, (i + distance) % count) for i in range(cou...  1.15 us
  transfers between devices with their start and end apart: 4, of which 3 were waited for; matrix products, arithmetic and copies ran while one was open for 0% of the time, Pallas kernels for 39%

profile of v9, /device:TPU:25, one launch (start us, length us, event | category | flops | bytes accessed | tf_op | source)
XLA Modules:
  0.0 19.1 jit_solution(15533888490321526119)
XLA Ops:
  0.6 0.7 %collective-permute-start = (bf16[1024,2048]{1,0:T(8,128)(2,1)}, bf16[1024,2048]{1,0:T(8,128)(2,1)S(1)}, u32[]{:S(2)}, u32[]{:S(2)}) collective-permute-start(bf16[1024,2048]{1,0:T(8,128)(2,1)} %tokens_ref.1), channel_id=1, source_target_pairs={{0,1},{1,0},{2,3},{3,2},{4,5},{5,4},{6,7},{7,6},{8,9},{9,8},{10,11... | collective-permute-start | bytes 12582920 | tf_op jit(solution)/shard_map/ppermute | solution.py:23
  1.4 1.1 %shard_map.106.spread_ref = bf16[384,256]{1,0:T(8,128)(2,1)S(1)} custom-call(f32[20,8,1024]{2,1,0:T(8,128)} %bitcast.9), custom_call_target="tpu_custom_call" | custom-call | flops 16384000000 | bytes 655360 | tf_op jit(solution)/shard_map/pallas_call | solution.py:234
  2.5 0.5 %copy-done.7 = bf16[1024,1024]{1,0:T(8,128)(2,1)S(1)} copy-done((bf16[1024,1024]{1,0:T(8,128)(2,1)S(1)}, bf16[1024,1024]{1,0:T(8,128)(2,1)}, u32[]{:S(2)}) %copy-start.7) | copy-done | bytes 2097176
  3.0 0.0 copy-start.4
  3.0 0.8 %shard_map.107 = bf16[160,1024]{1,0:T(8,128)(2,1)S(1)} custom-call(bf16[384,256]{1,0:T(8,128)(2,1)S(1)} %shard_map.106.spread_ref, bf16[1024,1024]{1,0:T(8,128)(2,1)S(1)} %copy-done.7), custom_call_target="tpu_custom_call" | custom-call | flops 6710886400 | bytes 2097152 | tf_op jit(solution)/shard_map/pallas_call | solution.py:249
  3.8 1.3 %collective-permute-start.2 = (bf16[160,1024]{1,0:T(8,128)(2,1)S(1)}, bf16[160,1024]{1,0:T(8,128)(2,1)S(1)}, u32[]{:S(2)}, u32[]{:S(2)}) collective-permute-start(bf16[160,1024]{1,0:T(8,128)(2,1)S(1)} %shard_map.107), channel_id=1, source_target_pairs={{0,2},{1,3},{2,4},{3,5},{4,6},{5,7},{6,8},{7,9},{8,10},{9,11},{10,... | collective-permute-start | bytes 983048 | tf_op jit(solution)/shard_map/ppermute | solution.py:543
  5.1 0.1 copy-done
  5.2 0.7 %copy-done.1 = bf16[1024,1024]{1,0:T(8,128)(2,1)S(1)} copy-done((bf16[1024,1024]{1,0:T(8,128)(2,1)S(1)}, bf16[1024,1024]{1,0:T(8,128)(2,1)}, u32[]{:S(2)}) %copy-start.1) | copy-done | bytes 2097176
  5.9 0.0 copy-done.2
  5.9 0.0 copy-done.3
  5.9 0.2 %copy-done.4 = f32[8,20,1024]{2,0,1:T(8,128)S(1)} copy-done((f32[8,20,1024]{2,0,1:T(8,128)S(1)}, f32[8,20,1024]{2,0,1:T(8,128)}, u32[]{:S(2)}) %copy-start.4) | copy-done | bytes 655384
  6.1 2.6 %shard_map.104 = (bf16[2,8,64,1024]{3,2,1,0:T(8,128)(2,1)S(1)}, bf16[320,1024]{1,0:T(8,128)(2,1)S(1)}, bf16[48,1024]{1,0:T(8,128)(2,1)S(1)}) custom-call(bf16[1024,2048]{1,0:T(8,128)(2,1)S(1)} %copy-done, bf16[8,8,2048]{2,1,0:T(8,128)(2,1)S(1)} %copy-done.2, bf16[8,8,2048]{2,1,0:T(8,128)(2,1)S(1)} %copy-done.3, f32[20,8,1024]{2,1,0:T(8,128)S(1)} %bitcast.5, ...), custom_call_target="tpu_custom_call" | custom-call | flops 603979776 | bytes 8388608 | tf_op jit(solution)/shard_map/pallas_call | solution.py:316
  8.7 0.0 collective-permute-done.tokens_ref
  8.7 0.0 copy-done.5
  8.8 0.0 copy-done.6
  8.8 2.9 %shard_map.105 = (bf16[2,8,64,1024]{3,2,1,0:T(8,128)(2,1)S(1)}, f32[48,128]{1,0:T(8,128)S(1)}, bf16[1024,1024]{1,0:T(8,128)(2,1)S(1)}) custom-call(bf16[1024,2048]{1,0:T(8,128)(2,1)S(1)} %collective-permute-done.tokens_ref, bf16[8,8,2048]{2,1,0:T(8,128)(2,1)S(1)} %copy-done.2, bf16[8,8,2048]{2,1,0:T(8,128)(2,1)S(1)} %copy-done.3, ...), custom_call_target="tpu_custom_call" | custom-call | flops 603979776 | bytes 6291456 | tf_op jit(solution)/shard_map/pallas_call | solution.py:354
  11.6 0.1 collective-permute-start.1
  11.7 1.2 %collective-permute-done.1.theirs_ref = f32[48,128]{1,0:T(8,128)S(1)} collective-permute-done((f32[48,128]{1,0:T(8,128)S(1)}, f32[48,128]{1,0:T(8,128)S(1)}, u32[]{:S(2)}, u32[]{:S(2)}) %collective-permute-start.1) | collective-permute-done | bytes 24608 | tf_op jit(solution)/shard_map/ppermute | solution.py:23
  12.9 0.1 shard_map.108
  13.0 1.1 %collective-permute-done.2.map_ref = bf16[160,1024]{1,0:T(8,128)(2,1)S(1)} collective-permute-done((bf16[160,1024]{1,0:T(8,128)(2,1)S(1)}, bf16[160,1024]{1,0:T(8,128)(2,1)S(1)}, u32[]{:S(2)}, u32[]{:S(2)}) %collective-permute-start.2) | collective-permute-done | bytes 327712 | tf_op jit(solution)/shard_map/ppermute | solution.py:543
  14.1 0.7 %shard_map.109.lower_ref = f32[24,128]{1,0:T(8,128)S(1)} custom-call(bf16[160,1024]{1,0:T(8,128)(2,1)S(1)} %collective-permute-done.2.map_ref, bf16[2,8,64,1024]{3,2,1,0:T(8,128)(2,1)S(1)} %get-tuple-element.14.own_ref, bf16[2,8,64,1024]{3,2,1,0:T(8,128)(2,1)S(1)} %get-tuple-element.18.peer_ref, f32[8,128]{1,0:T(8,128)S(1)} %get-tuple-element.19.earlier_ref), custom_call_target="tpu_custom_call" | custom-call | flops 67108864 | bytes 2097152 | tf_op jit(solution)/shard_map/pallas_call | solution.py:409
  14.8 0.8 %collective-permute-start.3 = (f32[24,128]{1,0:T(8,128)S(1)}, f32[24,128]{1,0:T(8,128)S(1)}, u32[]{:S(2)}, u32[]{:S(2)}) collective-permute-start(f32[24,128]{1,0:T(8,128)S(1)} %shard_map.109.lower_ref), channel_id=1, source_target_pairs={{0,1},{1,0},{2,3},{3,2},{4,5},{5,4},{6,7},{7,6},{8,9},{9,8},{10,11... | collective-permute-start | bytes 36872 | tf_op jit(solution)/shard_map/ppermute | solution.py:23
  15.7 0.8 %collective-permute-done.3.lower_theirs_ref = f32[24,128]{1,0:T(8,128)S(1)} collective-permute-done((f32[24,128]{1,0:T(8,128)S(1)}, f32[24,128]{1,0:T(8,128)S(1)}, u32[]{:S(2)}, u32[]{:S(2)}) %collective-permute-start.3) | collective-permute-done | bytes 12320 | tf_op jit(solution)/shard_map/ppermute | solution.py:23
  16.5 2.6 %shard_map.110 = (f32[1024,1024]{1,0:T(8,128)}, f32[1,64]{1,0:T(1,128)}) custom-call(f32[48,128]{1,0:T(8,128)S(1)} %get-tuple-element.15.mine_ref, f32[48,128]{1,0:T(8,128)S(1)} %collective-permute-done.1.theirs_ref, bf16[48,1024]{1,0:T(8,128)(2,1)S(1)} %get-tuple-element.16.wide_ref, ...), custom_call_target="tpu_custom_call", output_to_operand_aliasing={{0}: (6, {}), {1}: (7, {})} | custom-call | flops 402653184 | bytes 6291456 | tf_op jit(solution)/shard_map/pallas_call | solution.py:517
  (7 shorter events, 0.0 us)
Async XLA Ops:
  0.6 8.1 %collective-permute-start = (bf16[1024,2048]{1,0:T(8,128)(2,1)}, bf16[1024,2048]{1,0:T(8,128)(2,1)S(1)}, u32[]{:S(2)}, u32[]{:S(2)}) collective-permute-start(bf16[1024,2048]{1,0:T(8,128)(2,1)} %tokens_ref.1), channel_id=1, source_target_pairs={{0,1},{1,0},{2,3},{3,2},{4,5},{5,4},{6,7},{7,6},{8,9},{9,8},{10,11... | collective-permute-start | bytes 12582920 | tf_op jit(solution)/shard_map/ppermute | solution.py:23
  1.4 1.6 %copy-start.7 = (bf16[1024,1024]{1,0:T(8,128)(2,1)S(1)}, bf16[1024,1024]{1,0:T(8,128)(2,1)}, u32[]{:S(2)}) copy-start(bf16[1024,1024]{1,0:T(8,128)(2,1)} %proj_ref.3) | copy-start | bytes 6291460
  3.0 2.2 %copy-start = (bf16[1024,2048]{1,0:T(8,128)(2,1)S(1)}, bf16[1024,2048]{1,0:T(8,128)(2,1)}, u32[]{:S(2)}) copy-start(bf16[1024,2048]{1,0:T(8,128)(2,1)} %tokens_ref.1) | copy-start | bytes 12582916
  3.0 2.9 %copy-start.1 = (bf16[1024,1024]{1,0:T(8,128)(2,1)S(1)}, bf16[1024,1024]{1,0:T(8,128)(2,1)}, u32[]{:S(2)}) copy-start(bf16[1024,1024]{1,0:T(8,128)(2,1)} %proj_ref.2) | copy-start | bytes 6291460
  3.0 2.9 %copy-start.2 = (bf16[8,8,2048]{2,1,0:T(8,128)(2,1)S(1)}, bf16[8,8,2048]{2,1,0:T(8,128)(2,1)}, u32[]{:S(2)}) copy-start(bf16[8,8,2048]{2,1,0:T(8,128)(2,1)} %query_ref.3) | copy-start | bytes 786436
  3.0 2.9 %copy-start.3 = (bf16[8,8,2048]{2,1,0:T(8,128)(2,1)S(1)}, bf16[8,8,2048]{2,1,0:T(8,128)(2,1)}, u32[]{:S(2)}) copy-start(bf16[8,8,2048]{2,1,0:T(8,128)(2,1)} %prior_ref.3) | copy-start | bytes 786436
  3.0 3.1 %copy-start.4 = (f32[8,20,1024]{2,0,1:T(8,128)S(1)}, f32[8,20,1024]{2,0,1:T(8,128)}, u32[]{:S(2)}) copy-start(f32[8,20,1024]{2,0,1:T(8,128)} %param.16) | copy-start | bytes 1966084
  3.8 10.3 %collective-permute-start.2 = (bf16[160,1024]{1,0:T(8,128)(2,1)S(1)}, bf16[160,1024]{1,0:T(8,128)(2,1)S(1)}, u32[]{:S(2)}, u32[]{:S(2)}) collective-permute-start(bf16[160,1024]{1,0:T(8,128)(2,1)S(1)} %shard_map.107), channel_id=1, source_target_pairs={{0,2},{1,3},{2,4},{3,5},{4,6},{5,7},{6,8},{7,9},{8,10},{9,11},{10,... | collective-permute-start | bytes 983048 | tf_op jit(solution)/shard_map/ppermute | solution.py:543
  6.1 2.6 %copy-start.5 = (s32[64,20]{0,1:T(8,128)S(1)}, s32[64,20]{0,1:T(8,128)}, u32[]{:S(2)}) copy-start(s32[64,20]{0,1:T(8,128)} %param.10) | copy-start | bytes 15364
  6.1 2.7 %copy-start.6 = (s32[64]{0:T(128)S(1)}, s32[64]{0:T(128)}, u32[]{:S(2)}) copy-start(s32[64]{0:T(128)} %param.11) | copy-start | bytes 772
  11.6 1.3 %collective-permute-start.1 = (f32[48,128]{1,0:T(8,128)S(1)}, f32[48,128]{1,0:T(8,128)S(1)}, u32[]{:S(2)}, u32[]{:S(2)}) collective-permute-start(f32[48,128]{1,0:T(8,128)S(1)} %get-tuple-element.15.mine_ref), channel_id=1, source_target_pairs={{0,1},{1,0},{2,3},{3,2},{4,5},{5,4},{6,7},{7,6},{8,9},{9,8},{10,11... | collective-permute-start | bytes 73736 | tf_op jit(solution)/shard_map/ppermute | solution.py:23
  14.8 1.7 %collective-permute-start.3 = (f32[24,128]{1,0:T(8,128)S(1)}, f32[24,128]{1,0:T(8,128)S(1)}, u32[]{:S(2)}, u32[]{:S(2)}) collective-permute-start(f32[24,128]{1,0:T(8,128)S(1)} %shard_map.109.lower_ref), channel_id=1, source_target_pairs={{0,1},{1,0},{2,3},{3,2},{4,5},{5,4},{6,7},{7,6},{8,9},{9,8},{10,11... | collective-permute-start | bytes 36872 | tf_op jit(solution)/shard_map/ppermute | solution.py:23
